TPU v7x, 768 devices: a whole 4x8x12 slice. The times are simulated.
768 devices in a mesh: outer: 48 (over z_lo, y), dev: 16 (over x, z_hi, core).
Axes of the slice: x: 4, y: 8, z: 12 (z_hi: 2, z_lo: 6; z = z_hi * 6 + z_lo), core: 2. Of those that a mesh axis runs over, the one named last changes fastest.
Arguments:
- queries: bfloat16 [192, 6144], P('outer'), may hold values from -480 to 480
- key_cache: bfloat16 [192, 1024, 1024], P('outer', 'dev'), may hold values from -6 to 6
- value_cache: bfloat16 [192, 1024, 1024], P('outer', 'dev'), may hold values from -6 to 6
- new_key: bfloat16 [192, 1024], P('outer'), may hold values from -6 to 6
- new_value: bfloat16 [192, 1024], P('outer'), may hold values from -6 to 6
- lengths: int32 [192], P('outer'), may hold values from 256 to 1024, as said below
- experts: int32 [192, 2], P('outer'), may hold values from 0 to 7, all different within a row; in each aligned block of 4 rows (0 to 3, 4 to 7, ...) at most 2 rows name the same one
- combine: float32 [192, 2], P('outer'), may hold values from 0.2 to 1
- residual: bfloat16 [192, 6144], P('outer'), may hold values from -3 to 3
- norm_gain: float32 [6144], replicated, may hold values from 0.1 to 1.9
- w_gate: bfloat16 [6144, 73728], P(None, ('outer', 'dev')), may hold values from -0.078125 to 0.078125
- w_up: bfloat16 [6144, 73728], P(None, ('outer', 'dev')), may hold values from -0.078125 to 0.078125
- w_down: bfloat16 [73728, 6144], P(('outer', 'dev')), may hold values from -0.0625 to 0.0625
Outputs:
- mixed: bfloat16 [192, 6144], P('outer', 'dev')
Inputs may be any that keep to these rules, and one draw needn't show every extreme that they name: `lengths`: some token has exactly 1024 cached positions and some exactly 256. Each row names 2 different experts; in each aligned block of 4 rows no expert is named by more than 2 rows, a bound that some block reaches.
All inputs are finite; a program needn't handle non-finite values.
Results may differ from a plain program's by a relative error of at most 0.008.
Values may be sent and summed in bfloat16 or wider, within the bound.
No kernel may reach another device: no remote copies, remote signals or barrier semaphores. Data moves between devices by JAX's collectives and lax.ppermute only.
A program may use at most 32 MiB of HBM per device.

v0:
```python
import math

import jax
import jax.numpy as jnp
from jax import lax
from jax.sharding import PartitionSpec as P

HEADS = 48
KVH = 8
HD = 128
EXPERTS = 8
TOPK = 2
CAP = 2


def body(
    queries,
    key_cache,
    value_cache,
    new_key,
    new_value,
    lengths,
    experts,
    combine,
    residual,
    norm_gain,
    w_gate,
    w_up,
    w_down,
):
    row_count = queries.shape[0]
    model_width = residual.shape[1]
    group_size = HEADS // KVH
    dev_count = lax.axis_size("dev")
    dev_index = lax.axis_index("dev")
    share_width = model_width // dev_count
    local_span = key_cache.shape[1]
    score_scale = 1.0 / math.sqrt(HD)
    query_heads = queries.reshape(row_count, KVH, group_size, HD)
    cached_keys = key_cache.reshape(row_count, local_span, KVH, HD)
    cached_values = value_cache.reshape(row_count, local_span, KVH, HD)
    scores = (
        jnp.einsum("rgjd,rpgd->rgjp", query_heads, cached_keys, preferred_element_type=jnp.float32)
        * score_scale
    )
    own_score = (
        jnp.einsum(
            "rgjd,rgd->rgj",
            query_heads,
            new_key.reshape(row_count, KVH, HD),
            preferred_element_type=jnp.float32,
        )
        * score_scale
    )
    positions = dev_index * local_span + jnp.arange(local_span, dtype=jnp.int32)
    is_live = (positions[None, :] < lengths[:, None])[:, None, None, :]
    local_top = jnp.maximum(jnp.max(jnp.where(is_live, scores, -jnp.inf), axis=-1), own_score)
    row_top = lax.pmax(local_top, "dev")
    weights = jnp.where(is_live, jnp.exp(scores - row_top[..., None]), 0.0).astype(jnp.bfloat16)
    own_weight = lax.optimization_barrier(jnp.exp(own_score - row_top).astype(jnp.bfloat16)).astype(
        jnp.float32
    )
    accumulated = jnp.einsum(
        "rgjp,rpgd->rgjd", weights, cached_values, preferred_element_type=jnp.float32
    )
    totals = jnp.sum(weights.astype(jnp.float32), axis=-1)
    own_value = new_value.reshape(row_count, KVH, 1, HD).astype(jnp.float32)
    own_term = own_weight[..., None] * own_value
    accumulated, totals = lax.psum((accumulated, totals), "dev")
    attended = ((accumulated + own_term) / (totals + own_weight)[..., None]).reshape(
        row_count, model_width
    )
    full_state = residual.astype(jnp.float32) + attended
    mean_square = jnp.mean(full_state * full_state, axis=1, keepdims=True)
    hidden_state = lax.dynamic_slice_in_dim(full_state, dev_index * share_width, share_width, 1)
    gain_share = lax.dynamic_slice_in_dim(norm_gain, dev_index * share_width, share_width, 0)
    normed = (hidden_state * lax.rsqrt(mean_square + 1e-05) * gain_share).astype(jnp.bfloat16)
    outer_count = lax.axis_size("outer")
    copies = outer_count // EXPERTS
    chosen_ids = experts.reshape(row_count * TOPK)
    expert_hits = (chosen_ids[:, None] == jnp.arange(EXPERTS, dtype=jnp.int32)[None, :]).astype(
        jnp.int32
    )
    slot_rank = jnp.sum((jnp.cumsum(expert_hits, axis=0) - expert_hits) * expert_hits, axis=1)
    slot_hits = (slot_rank[:, None] == jnp.arange(CAP, dtype=jnp.int32)[None, :]).astype(jnp.int32)
    placement = (expert_hits[:, :, None] * slot_hits[:, None, :]).reshape(
        row_count, TOPK, EXPERTS, CAP
    )
    row_slots = jnp.sum(placement, axis=1)
    packed = jnp.einsum(
        "rec,rd->ecd", row_slots.astype(jnp.bfloat16), normed, preferred_element_type=jnp.float32
    ).astype(jnp.bfloat16)
    outgoing = jnp.repeat(packed, copies, axis=0)
    incoming = lax.all_to_all(outgoing, "outer", split_axis=0, concat_axis=0, tiled=True)
    token_slab = incoming.reshape(outer_count * CAP, share_width)
    expert_rows = lax.all_gather(token_slab, "dev", axis=1, tiled=True)
    gate_sum = jnp.dot(expert_rows, w_gate, preferred_element_type=jnp.float32)
    up_sum = jnp.dot(expert_rows, w_up, preferred_element_type=jnp.float32)
    activation = (jax.nn.silu(gate_sum) * up_sum).astype(jnp.bfloat16)
    partial_sum = jnp.dot(activation, w_down, preferred_element_type=jnp.float32)
    share_sum = lax.psum_scatter(partial_sum, "dev", scatter_dimension=1, tiled=True)
    returned = lax.all_to_all(
        share_sum.reshape(outer_count, CAP, share_width),
        "outer",
        split_axis=0,
        concat_axis=0,
        tiled=True,
    )
    expert_output = jnp.sum(returned.reshape(EXPERTS, copies, CAP, share_width), axis=1)
    mix_weights = jnp.sum(placement.astype(jnp.float32) * combine[:, :, None, None], axis=1)
    moe_output = jnp.einsum(
        "rec,ecd->rd", mix_weights, expert_output, precision=lax.Precision.HIGHEST
    )
    return (hidden_state + moe_output).astype(jnp.bfloat16)


def solution(mesh):
    return jax.shard_map(
        body,
        mesh=mesh,
        in_specs=(
            P("outer", None),
            P("outer", "dev", None),
            P("outer", "dev", None),
            P("outer", None),
            P("outer", None),
            P("outer"),
            P("outer", None),
            P("outer", None),
            P("outer", None),
            P(),
            P(None, ("outer", "dev")),
            P(None, ("outer", "dev")),
            P(("outer", "dev"), None),
        ),
        out_specs=P("outer", "dev"),
        check_vma=False,
    )
```

profile of v0, /device:TPU:2, one launch (start us, length us, event | category | flops | bytes accessed | tf_op | source)
XLA Modules:
  0.0 589.0 jit_solution(13365926908379225282)
XLA Ops:
  6.6 0.8 reshape.138
  7.4 0.9 reshape.123
  8.3 0.7 broadcast_compare_fusion
  9.2 1.5 select_reduce_fusion
  10.7 106.3 %pmax.7 = f32[4,8,6]{2,1,0:T(8,128)S(1)} all-reduce(f32[4,8,6]{2,1,0:T(8,128)S(1)} %multiply_maximum_fusion), channel_id=1, replica_groups=mesh['outer'=48,'dev'=16] {'dev'}, use_global_device_ids=true, to_apply=%region_1.2 | all-reduce | flops 192 | bytes 1536 | tf_op jit(solution)/shard_map/pmax | solution.py:58
  117.0 1.0 fusion.4
  118.2 0.2 convert_reduce_fusion
  118.6 0.2 select_reduce_fusion.1
  119.1 102.2 %psum.15 = f32[4,8,6]{2,1,0:T(8,128)S(1)} all-reduce(f32[4,8,6]{2,1,0:T(8,128)S(1)} %convert_reduce_fusion), channel_id=1, replica_groups=mesh['outer'=48,'dev'=16] {'dev'}, use_global_device_ids=true, to_apply=%region_4.5 | all-reduce | flops 192 | bytes 1536 | tf_op jit(solution)/shard_map/psum | solution.py:69
  221.2 0.8 dynamic_slice.7
  222.1 115.7 %all-reduce.2.cloned.1.call-done = f32[4,8,6,128]{3,2,1,0:T(8,128)} async-done(((f32[4,8,6,128]{3,2,1,0:T(8,128)}), f32[4,8,6,128]{3,2,1,0:T(8,128)}) %all-reduce.2.cloned.1.call-update) | async-done | bytes 98320 | tf_op jit(solution)/shard_map/psum | solution.py:69
  337.8 1.0 add_divide_fusion
  339.1 0.2 convolution_convert_fusion
  339.3 0.4 copy-done.4
  339.8 26.8 %all_to_all.10 = bf16[48,2,384]{2,1,0:T(2,128)(2,1)S(1)} all-to-all(bf16[48,2,384]{2,1,0:T(2,128)(2,1)S(1)} %bitcast.44), channel_id=1, replica_groups=mesh['outer'=48,'dev'=16] {'outer'}, dimensions={0} | all-to-all | bytes 147456 | tf_op jit(solution)/shard_map/all_to_all | solution.py:94
  366.6 0.7 reshape.129
  367.4 72.8 %all-gather.2.cloned.1.call-done = bf16[96,6144]{1,0:T(8,128)(2,1)} async-done(((bf16[96,384]{1,0:T(8,128)(2,1)}), bf16[96,6144]{1,0:T(8,128)(2,1)}) %all-gather.2.cloned.1.call-update) | async-done | bytes 1179664 | tf_op jit(solution)/shard_map/all_gather | solution.py:96
  440.2 2.4 fusion.29
  442.6 4.1 fusion.1
  446.8 111.2 %reduce-scatter.2.cloned.1.call-done = f32[96,384]{1,0:T(8,128)} async-done(((f32[96,6144]{1,0:T(8,128)}), f32[96,384]{1,0:T(8,128)}) %reduce-scatter.2.cloned.1.call-update) | async-done | bytes 147472 | tf_op jit(solution)/shard_map/reduce_scatter | solution.py:101
  558.0 1.6 reshape.130
  559.7 7.4 %all-to-all-start.1 = ((f32[48,2,384]{2,1,0:T(2,128)}), f32[48,2,384]{2,1,0:T(2,128)S(1)}, u32[]{:S(2)}, u32[]{:S(2)}) async-start(f32[48,2,384]{2,1,0:T(2,128)} %reshape.130), calls=%async_computation.2 | async-start | bytes 294912 | tf_op jit(solution)/shard_map/all_to_all | solution.py:102
  567.2 13.7 %all-to-all-done.1 = f32[48,2,384]{2,1,0:T(2,128)S(1)} async-done(((f32[48,2,384]{2,1,0:T(2,128)}), f32[48,2,384]{2,1,0:T(2,128)S(1)}, u32[]{:S(2)}, u32[]{:S(2)}) %all-to-all-start.1) | async-done | bytes 147488 | tf_op jit(solution)/shard_map/all_to_all | solution.py:102
  581.0 1.5 fusion.3
  (47 shorter events, 1.4 us)
Async XLA Ops:
  6.5 436.1 %copy-start = (bf16[96,6144]{1,0:T(8,128)(2,1)S(1)}, bf16[96,6144]{1,0:T(8,128)(2,1)}, u32[]{:S(2)}) copy-start(bf16[96,6144]{1,0:T(8,128)(2,1)} %param.25) | copy-start | bytes 3538948
  6.5 110.5 %copy-start.3 = (bf16[4,64,1024]{2,1,0:T(8,128)(2,1)S(1)}, bf16[4,64,1024]{2,1,0:T(8,128)(2,1)}, u32[]{:S(2)}) copy-start(bf16[4,64,1024]{2,1,0:T(8,128)(2,1)} %param.15) | copy-start | bytes 1572868
  6.5 111.5 %copy-start.7 = (s32[4,2]{0,1:T(2,128)S(1)}, s32[4,2]{0,1:T(2,128)}, u32[]{:S(2)}) copy-start(s32[4,2]{0,1:T(2,128)} %param.19) | copy-start | bytes 100
  6.5 112.5 %copy-start.6 = (bf16[4,1024]{1,0:T(4,128)(2,1)S(1)}, bf16[4,1024]{1,0:T(4,128)(2,1)}, u32[]{:S(2)}) copy-start(bf16[4,1024]{1,0:T(4,128)(2,1)} %param.17) | copy-start | bytes 24580
  6.5 331.3 %all-reduce.2.cloned.1.call-start = ((), (), s32[]{:S(2)}) async-start(), calls=%async_computation.3 | async-start | bytes 262144 | tf_op jit(solution)/shard_map/psum | solution.py:69
  9.2 329.7 %copy-start.5 = (bf16[4,6144]{1,0:T(4,128)(2,1)S(1)}, bf16[4,6144]{1,0:T(4,128)(2,1)}, u32[]{:S(2)}) copy-start(bf16[4,6144]{1,0:T(4,128)(2,1)} %param.21) | copy-start | bytes 147460
  117.0 323.2 %copy-start.2 = (bf16[6144,96]{0,1:T(8,128)(2,1)S(1)}, bf16[6144,96]{0,1:T(8,128)(2,1)}, u32[]{:S(2)}) copy-start(bf16[6144,96]{0,1:T(8,128)(2,1)} %param.23) | copy-start | bytes 3538948
  118.0 322.2 %all-gather.2.cloned.1.call-start = ((), (), s32[]{:S(2)}) async-start(), calls=%async_computation.4 | async-start | bytes 1253376 | tf_op jit(solution)/shard_map/all_gather | solution.py:96
  339.1 0.6 copy-start.4
  367.3 190.7 %reduce-scatter.2.cloned.1.call-start = ((), (), s32[]{:S(2)}) async-start(), calls=%async_computation.5 | async-start | bytes 2506752 | tf_op jit(solution)/shard_map/reduce_scatter | solution.py:101
  440.2 2.4 copy-start.1
  446.8 120.4 %copy-start.8 = (f32[4,2]{0,1:T(2,128)S(1)}, f32[4,2]{0,1:T(2,128)}, u32[]{:S(2)}) copy-start(f32[4,2]{0,1:T(2,128)} %param.20) | copy-start | bytes 100
  559.7 21.3 %all-to-all-start.1 = ((f32[48,2,384]{2,1,0:T(2,128)}), f32[48,2,384]{2,1,0:T(2,128)S(1)}, u32[]{:S(2)}, u32[]{:S(2)}) async-start(f32[48,2,384]{2,1,0:T(2,128)} %reshape.130), calls=%async_computation.2 | async-start | bytes 294912 | tf_op jit(solution)/shard_map/all_to_all | solution.py:102
Sparse Core Ops, SparseCore 0:
  118.1 219.6 all-reduce.1
  367.4 72.6 all-gather.1
  446.9 111.0 reduce-scatter.1
where the time goes:
time: 590 us; the launch traced here: 589 us
  waiting for transfers between devices  314 us (53%)
  blocking collectives  235 us (40%)
  between operations  13.3 us (2%)
  matrix products  10.9 us (2%)
  starting transfers between devices  7.56 us (1%)
    psum x1, waiting for transfers between devices, body(): accumulated, totals = lax.psum((accumulated, totals), 'dev')  116 us
    reduce_scatter x1, waiting for transfers between devices, body(): lax.psum_scatter(partial_sum, 'dev', scatter_dimension=1, tiled=True)  111 us
    pmax x1, blocking collectives, body(): row_top = lax.pmax(local_top, 'dev')  106 us
    psum x1, blocking collectives, body(): accumulated, totals = lax.psum((accumulated, totals), 'dev')  102 us
    all_gather x1, waiting for transfers between devices, body(): expert_rows = lax.all_gather(token_slab, 'dev', axis=1, tiled=True)  72.8 us
    all_to_all x1, blocking collectives, body(): lax.all_to_all(outgoing, 'outer', split_axis=0, concat_axis=0, tiled=True)  26.8 us
    all_to_all x1, waiting for transfers between devices, body(): lax.all_to_all(share_sum.reshape(outer_count, CAP, share_width), 'outer',...  13.7 us
  transfers between devices with their start and end apart: 4, of which 4 were waited for; matrix products, arithmetic and copies ran while one was open for 0% of the time, Pallas kernels for 0%

commit v1 on v0

v1 whole, which is shorter than its diff:
```python
import math

import jax
import jax.numpy as jnp
from jax import lax
from jax.sharding import Mesh
from jax.sharding import PartitionSpec as P

HEADS = 48
KVH = 8
HD = 128
EXPERTS = 8
TOPK = 2
CAP = 2
DEAD = -1e30

OUTER = ("zl", "y")
DEV = ("x", "zh", "c")


def two_parts(v):
    high = lax.reduce_precision(v, 8, 7)
    low = lax.reduce_precision(v - high, 8, 7)
    return high, low


def body(
    queries,
    key_cache,
    value_cache,
    new_key,
    new_value,
    lengths,
    experts,
    combine,
    residual,
    norm_gain,
    w_gate,
    w_up,
    w_down,
):
    bf16, f32 = jnp.bfloat16, jnp.float32
    rows, width = residual.shape
    group = HEADS // KVH
    nx, nz, nc = (lax.axis_size(a) for a in DEV)
    dev_count = nx * nz * nc
    outer_count = lax.axis_size("zl") * lax.axis_size("y")
    copies = outer_count // EXPERTS
    at_x, at_z, at_c = (lax.axis_index(a) for a in DEV)
    dev_index = (at_x * nz + at_z) * nc + at_c
    share = width // dev_count
    own_heads = HEADS // dev_count
    span = key_cache.shape[1]
    scale = 1.0 / math.sqrt(HD)

    q = queries.reshape(rows, KVH, group, HD)
    k = key_cache.reshape(rows, span, KVH, HD)
    v = value_cache.reshape(rows, span, KVH, HD)
    scores = jnp.einsum("rgjd,rpgd->rgjp", q, k, preferred_element_type=f32) * scale
    own_score = (
        jnp.einsum("rgjd,rgd->rgj", q, new_key.reshape(rows, KVH, HD), preferred_element_type=f32)
        * scale
    )
    own_score = jnp.where(dev_index == 0, own_score, DEAD)
    positions = dev_index * span + jnp.arange(span, dtype=jnp.int32)
    live = (positions[None, :] < lengths[:, None])[:, None, None, :]
    top = jnp.maximum(jnp.max(jnp.where(live, scores, DEAD), axis=-1), own_score)
    top_high, top_low = two_parts(top)
    base = top_high + top_low
    weights = jnp.where(live, jnp.exp(scores - base[..., None]), 0.0).astype(bf16)
    own_weight = jnp.where(dev_index == 0, jnp.exp(own_score - base), 0.0)
    own_weight = lax.reduce_precision(own_weight, 8, 7)
    acc = jnp.einsum("rgjp,rpgd->rgjd", weights, v, preferred_element_type=f32)
    acc = acc + own_weight[..., None] * new_value.reshape(rows, KVH, 1, HD).astype(f32)
    total = jnp.sum(weights.astype(f32), axis=-1) + own_weight
    total_high, total_low = two_parts(total)

    def by_target(a):
        a = a.reshape(rows, nx, nz, nc, own_heads, -1)
        return jnp.transpose(a, (1, 3, 0, 2, 4, 5))

    slab_rows = rows * nz * own_heads
    values = by_target(acc.reshape(rows, HEADS, HD)).reshape(nx, nc, slab_rows, HD)
    stats = jnp.stack([top_high, top_low, total_high, total_low]).reshape(4, rows, HEADS)
    stats = jnp.stack([by_target(stats[i]).reshape(nx, nc, slab_rows) for i in range(4)], axis=2)
    stats = jnp.pad(stats, ((0, 0), (0, 0), (0, 4), (0, HD - slab_rows)))
    packet = jnp.concatenate([values, stats], axis=2).astype(bf16)
    packet = jnp.broadcast_to(packet[:, None], (nx, nz, nc) + packet.shape[2:])
    packet = packet.reshape((dev_count,) + packet.shape[3:])
    arrived = lax.all_to_all(packet, DEV, split_axis=0, concat_axis=0, tiled=True)
    part = arrived[:, :slab_rows, :].astype(f32)
    info = arrived[:, slab_rows : slab_rows + 4, :slab_rows].astype(f32)
    base_of = info[:, 0] + info[:, 1]
    factor = jnp.exp(base_of - jnp.max(base_of, axis=0, keepdims=True))
    whole = jnp.sum(factor * (info[:, 2] + info[:, 3]), axis=0)
    attended = jnp.sum((factor / whole)[..., None] * part, axis=0)
    attended = attended.reshape(rows, nz, share)
    res = residual.reshape(rows, nx, nz, nc, share)
    res = lax.dynamic_slice(res, (0, at_x, 0, at_c, 0), (rows, 1, nz, 1, share))
    state = res.reshape(rows, nz, share).astype(f32) + attended
    own_state = lax.dynamic_index_in_dim(state, at_z, 1, keepdims=False)

    chosen = experts.reshape(rows * TOPK)
    hits = (chosen[:, None] == jnp.arange(EXPERTS, dtype=jnp.int32)[None, :]).astype(jnp.int32)
    rank = jnp.sum((jnp.cumsum(hits, axis=0) - hits) * hits, axis=1)
    slot = (rank[:, None] == jnp.arange(CAP, dtype=jnp.int32)[None, :]).astype(jnp.int32)
    placement = (hits[:, :, None] * slot[:, None, :]).reshape(rows, TOPK, EXPERTS, CAP)
    row_slots = jnp.sum(placement, axis=1)
    packed = jnp.einsum(
        "rec,rd->ecd",
        row_slots.astype(bf16),
        state.reshape(rows, nz * share).astype(bf16),
        preferred_element_type=f32,
    ).astype(bf16)
    outgoing = jnp.repeat(packed, copies, axis=0)
    incoming = lax.all_to_all(outgoing, OUTER, split_axis=0, concat_axis=0, tiled=True)
    slab = incoming.reshape(outer_count * CAP, nz * share)
    over_x = lax.all_gather(slab, "x", axis=0, tiled=False)
    half = nx // 2
    low_x = lax.all_gather(over_x[:half], "c", axis=0, tiled=False)
    high_x = lax.all_gather(over_x[half:], "c", axis=0, tiled=False)
    both = jnp.concatenate([low_x, high_x], axis=1)
    both = both.reshape(nc, nx, outer_count * CAP, nz, share)
    expert_state = jnp.transpose(both, (2, 1, 3, 0, 4)).reshape(outer_count * CAP, width)
    expert_state = expert_state.astype(f32)
    mean_square = jnp.mean(expert_state * expert_state, axis=1, keepdims=True)
    normed = (expert_state * lax.rsqrt(mean_square + 1e-05) * norm_gain).astype(bf16)
    gate_sum = jnp.dot(normed, w_gate, preferred_element_type=f32)
    up_sum = jnp.dot(normed, w_up, preferred_element_type=f32)
    activation = (jax.nn.silu(gate_sum) * up_sum).astype(bf16)
    partial_sum = jnp.dot(activation, w_down, preferred_element_type=f32).astype(bf16)

    cut = partial_sum.reshape(outer_count * CAP, nx, nz, nc, share)
    cut = jnp.transpose(cut, (3, 1, 0, 2, 4)).reshape(nc, nx, outer_count * CAP, nz * share)
    over_c = lax.all_to_all(cut, "c", split_axis=0, concat_axis=0, tiled=True)
    over_c = jnp.sum(over_c.astype(f32), axis=0).astype(bf16)
    from_x = lax.all_to_all(over_c, "x", split_axis=0, concat_axis=0, tiled=True)
    from_x = jnp.sum(from_x.astype(f32), axis=0)
    home = from_x.reshape(outer_count, CAP, nz, share)
    home = jnp.transpose(home, (0, 2, 1, 3)).reshape(outer_count * nz, CAP, share).astype(bf16)
    returned = lax.all_to_all(home, OUTER + ("zh",), split_axis=0, concat_axis=0, tiled=True)
    returned = returned.reshape(EXPERTS, copies * nz, CAP, share).astype(f32)
    expert_output = jnp.sum(returned, axis=1)
    mix_weights = jnp.sum(placement.astype(f32) * combine[:, :, None, None], axis=1)
    moe = jnp.einsum("rec,ecd->rd", mix_weights, expert_output, precision=lax.Precision.HIGHEST)
    return (own_state + moe).astype(bf16)


def solution(mesh):
    fine = Mesh(mesh.devices.reshape(6, 8, 4, 2, 2), OUTER + DEV)
    return jax.shard_map(
        body,
        mesh=fine,
        in_specs=(
            P(OUTER, None),
            P(OUTER, DEV, None),
            P(OUTER, DEV, None),
            P(OUTER, None),
            P(OUTER, None),
            P(OUTER),
            P(OUTER, None),
            P(OUTER, None),
            P(OUTER, None),
            P(),
            P(None, OUTER + DEV),
            P(None, OUTER + DEV),
            P(OUTER + DEV, None),
        ),
        out_specs=P(OUTER, DEV),
        check_vma=False,
    )
```

time: 590 us -> 148 us (0.25)
  the two profiles are of different devices: /device:TPU:2 before, /device:TPU:8 now
where the time goes in v1:
time: 148 us; the launch traced here: 147 us
  blocking collectives  63.1 us (43%)
  waiting for transfers between devices  26.1 us (18%)
  starting transfers between devices  23.8 us (16%)
  local copies, waits for them, and re-layouts  19.7 us (13%)
  matrix products  9.2 us (6%)
  other arithmetic  4.71 us (3%)
    all_to_all x1, blocking collectives, body(): lax.all_to_all(outgoing, OUTER, split_axis=0, concat_axis=0, tiled=True)  27.6 us
    all_to_all x1, starting transfers between devices, body(): lax.all_to_all(packet, DEV, split_axis=0, concat_axis=0, tiled=True)  17.1 us
    all_to_all x1, waiting for transfers between devices, body(): lax.all_to_all(home, OUTER + ('zh',), split_axis=0, concat_axis=0, tiled=...  14.3 us
    all_to_all x1, blocking collectives, body(): lax.all_to_all(over_c, 'x', split_axis=0, concat_axis=0, tiled=True)  13.4 us
    all_gather x1, blocking collectives, body(): over_x = lax.all_gather(slab, 'x', axis=0, tiled=False)  12.9 us
    all_to_all x1, waiting for transfers between devices, body(): lax.all_to_all(packet, DEV, split_axis=0, concat_axis=0, tiled=True)  11.8 us
    convert_element_type x3, local copies, waits for them, and re-layouts, body(): expert_state = expert_state.astype(f32)  10.4 us
    all_to_all x1, starting transfers between devices, body(): lax.all_to_all(home, OUTER + ('zh',), split_axis=0, concat_axis=0, tiled=...  6.73 us
  transfers between devices with their start and end apart: 2, of which 2 were waited for; matrix products, arithmetic and copies ran while one was open for 1% of the time, Pallas kernels for 0%

profile of v1, /device:TPU:8, one launch (start us, length us, event | category | flops | bytes accessed | tf_op | source)
XLA Modules:
  0.0 146.9 jit_solution(2966144753366818301)
XLA Ops:
  0.0 0.8 reshape.241
  1.6 0.9 reshape.218
  2.4 0.7 broadcast_compare_fusion
  3.3 1.5 %select_reduce_fusion = (f32[4,8,6]{2,1,0:T(8,128)S(1)}, f32[4,8,6,64]{3,2,1,0:T(8,128)S(1)}) fusion(pred[4,64]{1,0:T(4,128)(4,1)S(1)} %broadcast_compare_fusion, bf16[4,8,6,128]{3,2,1,0:T(8,128)(2,1)S(1)} %reshape.218, bf16[4,64,1024]{2,1,0:T(8,128)(2,1)} %param.14), kind=kOutput, calls=%fused_computation.22 | convolution fusion | flops 3182400 | bytes 623616 | tf_op jit(solution)/shard_map/rgjd,rpgd->rgjp/dot_general | solution.py:59
  8.1 17.1 %all-to-all-start = ((bf16[16,32,128]{2,1,0:T(8,128)(2,1)}), bf16[16,32,128]{2,1,0:T(8,128)(2,1)S(1)}, u32[]{:S(2)}, u32[]{:S(2)}) async-start(bf16[16,32,128]{2,1,0:T(8,128)(2,1)} %bitcast.17), calls=%async_computation | async-start | bytes 262144 | tf_op jit(solution)/shard_map/all_to_all | solution.py:90
  26.7 11.8 %all-to-all-done = bf16[16,32,128]{2,1,0:T(8,128)(2,1)S(1)} async-done(((bf16[16,32,128]{2,1,0:T(8,128)(2,1)}), bf16[16,32,128]{2,1,0:T(8,128)(2,1)S(1)}, u32[]{:S(2)}, u32[]{:S(2)}) %all-to-all-start) | async-done | bytes 131104 | tf_op jit(solution)/shard_map/all_to_all | solution.py:90
  39.1 27.6 %all_to_all.25 = bf16[48,2,768]{2,1,0:T(2,128)(2,1)S(1)} all-to-all(bf16[48,2,768]{2,1,0:T(2,128)(2,1)S(1)} %bitcast.106), channel_id=1, replica_groups=mesh['zl'=6,'y'=8,'x'=4,'zh'=2,'c'=2] {'zl','y'}, dimensions={0} | all-to-all | bytes 294912 | tf_op jit(solution)/shard_map/all_to_all | solution.py:116
  66.8 12.9 %all_gather.15 = bf16[4,96,768]{2,1,0:T(8,128)(2,1)S(1)} all-gather(bf16[1,96,768]{2,1,0:T(8,128)(2,1)S(1)} %all_gather_reshape.3), channel_id=1, replica_groups=mesh['zl'=6,'y'=8,'x'=4,'zh'=2,'c'=2] {'x'}, dimensions={0}, use_global_device_ids=true | all-gather | bytes 737280 | tf_op jit(solution)/shard_map/all_gather | solution.py:118
  79.7 2.2 %all-gather = bf16[4,96,768]{2,1,0:T(8,128)(2,1)S(1)} all-gather(bf16[2,96,768]{2,1,0:T(8,128)(2,1)S(1)} %get-tuple-element.11), channel_id=2, replica_groups=mesh['zl'=6,'y'=8,'x'=4,'zh'=2,'c'=2] {'c'}, dimensions={0}, use_global_device_ids=true | all-gather | bytes 884736 | tf_op jit(solution)/shard_map/all_gather | solution.py:120
  82.0 2.2 %all-gather.1 = bf16[4,96,768]{2,1,0:T(8,128)(2,1)S(1)} all-gather(bf16[2,96,768]{2,1,0:T(8,128)(2,1)S(1)} %get-tuple-element.12), channel_id=3, replica_groups=mesh['zl'=6,'y'=8,'x'=4,'zh'=2,'c'=2] {'c'}, dimensions={0}, use_global_device_ids=true | all-gather | bytes 884736 | tf_op jit(solution)/shard_map/all_gather | solution.py:121
  85.3 2.3 %reshape.233 = f32[2,4,96,2,384]{4,3,2,1,0:T(2,128)} reshape(f32[2,4,96,768]{3,2,1,0:T(8,128)S(1)} %maximum_convert_fusion) | data formatting | bytes 4718592 | tf_op jit(solution)/shard_map/convert_element_type | solution.py:125
  87.6 4.9 %copy.118 = f32[96,4,2,2,384]{4,3,2,1,0:T(2,128)} copy(f32[96,4,2,2,384]{4,2,0,1,3:T(2,128)} %bitcast.99) | data formatting | bytes 4718592 | tf_op jit(solution)/shard_map/convert_element_type | solution.py:125
  92.5 3.2 %reshape.231 = f32[96,6144]{1,0:T(8,128)S(1)} reshape(f32[96,4,2,2,384]{4,3,2,1,0:T(2,128)} %copy.118) | data formatting | bytes 4718592 | tf_op jit(solution)/shard_map/convert_element_type | solution.py:125
  95.7 2.4 %fusion.42 = f32[96,96]{1,0:T(8,128)} fusion(bf16[6144,96]{0,1:T(8,128)(2,1)} %param.23, f32[96,6144]{1,0:T(8,128)S(1)} %reshape.231, f32[6144]{0:T(1024)} %param.22, f32[96]{0:T(128)} %add_rsqrt_fusion), kind=kOutput, calls=%fused_computation.86 | convolution fusion | flops 115015680 | bytes 3600768 | tf_op jit(solution)/shard_map/dot_general | solution.py:128
  98.1 3.8 %convolution_convert_fusion = bf16[96,6144]{1,0:T(8,128)(2,1)} fusion(bf16[96,6144]{1,0:T(8,128)(2,1)S(1)} %copy-done, bf16[6144,96]{0,1:T(8,128)(2,1)} %param.24, f32[96,96]{1,0:T(8,128)} %fusion.42, f32[96,6144]{1,0:T(8,128)S(1)} %reshape.231, f32[6144]{0:T(1024)} %param.22, f32[96]{0:T(128)} %add_rsqrt_fusion), kind=kOutput, calls=%fused_computation | convolution fusion | flops 228907008 | bytes 5960064 | tf_op jit(solution)/shard_map/dot_general | solution.py:131
  101.9 1.9 %reshape.226 = bf16[96,4,2,2,384]{4,3,2,1,0:T(2,128)(2,1)S(1)} reshape(bf16[96,6144]{1,0:T(8,128)(2,1)} %convolution_convert_fusion) | data formatting | bytes 2359296 | tf_op jit(solution)/shard_map/reshape | solution.py:133
  103.8 0.9 copy.148
  104.8 0.8 reshape.227
  105.6 4.7 %all_to_all.26 = bf16[2,4,96,768]{3,2,1,0:T(8,128)(2,1)S(1)} all-to-all(bf16[2,4,96,768]{3,2,1,0:T(8,128)(2,1)S(1)} %reshape.227), channel_id=1, replica_groups=mesh['zl'=6,'y'=8,'x'=4,'zh'=2,'c'=2] {'c'}, dimensions={0} | all-to-all | bytes 2359296 | tf_op jit(solution)/shard_map/all_to_all | solution.py:135
  110.5 13.4 %all_to_all.27 = bf16[4,96,768]{2,1,0:T(8,128)(2,1)S(1)} all-to-all(bf16[4,96,768]{2,1,0:T(8,128)(2,1)S(1)} %reduce_sum.103), channel_id=1, replica_groups=mesh['zl'=6,'y'=8,'x'=4,'zh'=2,'c'=2] {'x'}, dimensions={0} | all-to-all | bytes 1179648 | tf_op jit(solution)/shard_map/all_to_all | solution.py:137
  124.1 0.8 copy.120
  124.8 6.7 %all-to-all-start.4 = ((bf16[96,2,384]{2,1,0:T(2,128)(2,1)}), bf16[96,2,384]{2,1,0:T(2,128)(2,1)S(1)}, u32[]{:S(2)}, u32[]{:S(2)}) async-start(bf16[96,2,384]{2,1,0:T(2,128)(2,1)} %bitcast.27), calls=%async_computation.4 | async-start | bytes 294912 | tf_op jit(solution)/shard_map/all_to_all | solution.py:141
  131.7 14.3 %all-to-all-done.4 = bf16[96,2,384]{2,1,0:T(2,128)(2,1)S(1)} async-done(((bf16[96,2,384]{2,1,0:T(2,128)(2,1)}), bf16[96,2,384]{2,1,0:T(2,128)(2,1)S(1)}, u32[]{:S(2)}, u32[]{:S(2)}) %all-to-all-start.4) | async-done | bytes 147488 | tf_op jit(solution)/shard_map/all_to_all | solution.py:141
  146.1 0.8 fusion.3
  (80 shorter events, 7.9 us)
Async XLA Ops:
  0.0 98.1 %copy-start = (bf16[96,6144]{1,0:T(8,128)(2,1)S(1)}, bf16[96,6144]{1,0:T(8,128)(2,1)}, u32[]{:S(2)}) copy-start(bf16[96,6144]{1,0:T(8,128)(2,1)} %param.25) | copy-start | bytes 3538948
  0.0 5.6 %copy-start.7 = (bf16[4,64,1024]{2,1,0:T(8,128)(2,1)S(1)}, bf16[4,64,1024]{2,1,0:T(8,128)(2,1)}, u32[]{:S(2)}) copy-start(bf16[4,64,1024]{2,1,0:T(8,128)(2,1)} %param.15) | copy-start | bytes 1572868
  5.3 19.9 %copy-start.5 = (s32[4,2]{0,1:T(2,128)S(1)}, s32[4,2]{0,1:T(2,128)}, u32[]{:S(2)}) copy-start(s32[4,2]{0,1:T(2,128)} %param.19) | copy-start | bytes 100
  5.3 20.6 %copy-start.1 = (bf16[4,6144]{1,0:T(4,128)(2,1)S(1)}, bf16[4,6144]{1,0:T(4,128)(2,1)}, u32[]{:S(2)}) copy-start(bf16[4,6144]{1,0:T(4,128)(2,1)} %param.21) | copy-start | bytes 147460
  8.1 30.4 %all-to-all-start = ((bf16[16,32,128]{2,1,0:T(8,128)(2,1)}), bf16[16,32,128]{2,1,0:T(8,128)(2,1)S(1)}, u32[]{:S(2)}, u32[]{:S(2)}) async-start(bf16[16,32,128]{2,1,0:T(8,128)(2,1)} %bitcast.17), calls=%async_computation | async-start | bytes 262144 | tf_op jit(solution)/shard_map/all_to_all | solution.py:90
  25.9 13.2 %copy-start.3 = (s32[4,2,2]{0,2,1:T(2,128)}, s32[4,2,2]{0,2,1:T(2,128)S(1)}, u32[]{:S(2)}) copy-start(s32[4,2,2]{0,2,1:T(2,128)S(1)} %compare_convert_fusion) | copy-start | bytes 196
  110.5 21.1 %copy-start.2 = (f32[4,1,2,1,384]{4,3,2,1,0:T(1,128)S(1)}, f32[4,1,2,1,384]{4,3,2,1,0:T(1,128)}, u32[]{:S(2)}) copy-start(f32[4,1,2,1,384]{4,3,2,1,0:T(1,128)} %get-tuple-element.10) | copy-start | bytes 36868
  110.5 21.1 %copy-start.4 = (s32[4,2,2]{0,2,1:T(2,128)S(1)}, s32[4,2,2]{0,2,1:T(2,128)}, u32[]{:S(2)}) copy-start(s32[4,2,2]{0,2,1:T(2,128)} %copy-done.3) | copy-start | bytes 196
  110.5 21.1 %copy-start.6 = (f32[4,2]{0,1:T(2,128)S(1)}, f32[4,2]{0,1:T(2,128)}, u32[]{:S(2)}) copy-start(f32[4,2]{0,1:T(2,128)} %param.20) | copy-start | bytes 100
  124.8 21.2 %all-to-all-start.4 = ((bf16[96,2,384]{2,1,0:T(2,128)(2,1)}), bf16[96,2,384]{2,1,0:T(2,128)(2,1)S(1)}, u32[]{:S(2)}, u32[]{:S(2)}) async-start(bf16[96,2,384]{2,1,0:T(2,128)(2,1)} %bitcast.27), calls=%async_computation.4 | async-start | bytes 294912 | tf_op jit(solution)/shard_map/all_to_all | solution.py:141

commit v2 on v1

v2 whole, which is shorter than its diff:
```python
import math

import jax
import jax.numpy as jnp
from jax import lax
from jax.experimental import pallas as pl
from jax.experimental.pallas import tpu as pltpu
from jax.sharding import Mesh
from jax.sharding import PartitionSpec as P

HEADS = 48
KVH = 8
HD = 128
EXPERTS = 8
TOPK = 2
CAP = 2
DEAD = -1e30

OUTER = ("zl", "y")
DEV = ("x", "zh", "c")
NX, NZ, NC = 4, 2, 2
VMEM = pl.BlockSpec(memory_space=pltpu.VMEM)
NT = (((1,), (1,)), ((), ()))


def attend_kernel(
    length_ref, q_ref, k_ref, v_ref, nk_ref, nv_ref, out_ref, q_rows, nk_rows, nv_rows, packed
):
    f32, bf16 = jnp.float32, jnp.bfloat16
    tokens = q_ref.shape[0]
    span = k_ref.shape[0] // tokens
    group = HEADS // KVH
    lines = group * tokens
    half = lines // NC
    scale = 1.0 / math.sqrt(HD)
    dev_index = (lax.axis_index("x") * NZ + lax.axis_index("zh")) * NC + lax.axis_index("c")
    queries = q_ref[...].astype(f32)
    new_keys = nk_ref[...].astype(f32)
    new_values = nv_ref[...].astype(f32)
    for head in range(HEADS):
        g = head // group
        at = slice(head * tokens, (head + 1) * tokens)
        q_rows[at, :] = queries[:, head * HD : (head + 1) * HD]
        nk_rows[at, :] = new_keys[:, g * HD : (g + 1) * HD]
        nv_rows[at, :] = new_values[:, g * HD : (g + 1) * HD]
    row = lax.broadcasted_iota(jnp.int32, (lines, tokens * span), 0) % tokens
    column = lax.broadcasted_iota(jnp.int32, (lines, tokens * span), 1)
    limit = jnp.zeros((lines, tokens * span), jnp.int32)
    for t in range(tokens):
        limit = jnp.where(row == t, length_ref[t], limit)
    live = (column // span == row) & (dev_index * span + column % span < limit)
    lane = lax.broadcasted_iota(jnp.int32, (lines, HD), 1)
    first = dev_index == 0
    for g in range(KVH):
        at = slice(g * lines, (g + 1) * lines)
        lanes = slice(g * HD, (g + 1) * HD)
        q = q_rows[at, :]
        scores = lax.dot_general(q.astype(bf16), k_ref[:, lanes], NT, preferred_element_type=f32)
        scores = jnp.where(live, scores * scale, DEAD)
        own = jnp.sum(q * nk_rows[at, :], axis=1, keepdims=True) * scale
        own = jnp.where(first, own, DEAD)
        top = jnp.maximum(jnp.max(scores, axis=1, keepdims=True), own)
        top_high = top.astype(bf16).astype(f32)
        top_low = (top - top_high).astype(bf16).astype(f32)
        base = top_high + top_low
        weights = jnp.where(live, jnp.exp(scores - base), 0.0).astype(bf16)
        own_weight = jnp.where(first, jnp.exp(own - base), 0.0).astype(bf16).astype(f32)
        acc = jnp.dot(weights, v_ref[:, lanes], preferred_element_type=f32)
        acc = acc + own_weight * nv_rows[at, :]
        total = jnp.sum(weights.astype(f32), axis=1, keepdims=True) + own_weight
        total_high = total.astype(bf16).astype(f32)
        total_low = total - total_high
        stats = jnp.where(
            lane == 0,
            top_high,
            jnp.where(lane == 1, top_low, jnp.where(lane == 2, total_high, total_low)),
        )
        x, z = g // NZ, g % NZ
        for c in range(NC):
            to = slice(z * half, (z + 1) * half)
            packed[x * NC + c, to, :HD] = acc[c * half : (c + 1) * half]
            packed[x * NC + c, to, HD:] = stats[c * half : (c + 1) * half]
    for x in range(NX):
        for c in range(NC):
            block = packed[x * NC + c].astype(bf16)
            for z in range(NZ):
                out_ref[(x * NZ + z) * NC + c] = block


def expert_kernel(low_ref, high_ref, gain_ref, gate_ref, up_ref, down_ref, out_ref):
    f32, bf16 = jnp.float32, jnp.bfloat16
    rows = low_ref.shape[2]
    share = low_ref.shape[3] // NZ
    width = gate_ref.shape[1]
    squares = jnp.zeros((rows, HD), f32)
    gate = jnp.zeros((rows, gate_ref.shape[0]), f32)
    up = jnp.zeros((rows, up_ref.shape[0]), f32)
    for x in range(NX):
        source = low_ref if x < NX // 2 else high_ref
        for c in range(NC):
            block = source[c, x % (NX // 2)]
            starts = [((x * NZ + z) * NC + c) * share for z in range(NZ)]

            def columns(ref):
                return jnp.concatenate([ref[:, s : s + share] for s in starts], axis=1)

            gate += lax.dot_general(block, columns(gate_ref), NT, preferred_element_type=f32)
            up += lax.dot_general(block, columns(up_ref), NT, preferred_element_type=f32)
            state = block.astype(f32) / columns(gain_ref)
            state = state * state
            for at in range(0, NZ * share, HD):
                squares += state[:, at : at + HD]
    factor = lax.rsqrt(jnp.sum(squares, axis=1, keepdims=True) / width + 1e-05)
    gate = gate * factor
    active = (gate / (1.0 + jnp.exp(-gate)) * (up * factor)).astype(bf16)
    for x in range(NX):
        for c in range(NC):
            for z in range(NZ):
                start = ((x * NZ + z) * NC + c) * share
                out_ref[c, x, :, z * share : (z + 1) * share] = jnp.dot(
                    active, down_ref[:, start : start + share], preferred_element_type=f32
                ).astype(bf16)


def local_attention(lengths, queries, key_cache, value_cache, new_key, new_value):
    rows, span, features = key_cache.shape
    slab_rows = HEADS // (NX * NC) * rows
    return pl.pallas_call(
        attend_kernel,
        out_shape=jax.ShapeDtypeStruct((NX * NZ * NC, slab_rows, 2 * HD), jnp.bfloat16),
        in_specs=[pl.BlockSpec(memory_space=pltpu.SMEM)] + [pl.BlockSpec()] * 5,
        out_specs=VMEM,
        scratch_shapes=[pltpu.VMEM((HEADS * rows, HD), jnp.float32)] * 3
        + [pltpu.VMEM((NX * NC, slab_rows, 2 * HD), jnp.float32)],
        compiler_params=pltpu.CompilerParams(vmem_limit_bytes=60 * 2**20),
        name="attend",
    )(
        lengths,
        queries,
        key_cache.reshape(rows * span, features),
        value_cache.reshape(rows * span, features),
        new_key,
        new_value,
    )


def merge(arrived):
    f32 = jnp.float32
    part = arrived[:, :, :HD].astype(f32)
    info = arrived[:, :, HD : HD + 4].astype(f32)
    base_of = info[:, :, 0] + info[:, :, 1]
    factor = jnp.exp(base_of - jnp.max(base_of, axis=0, keepdims=True))
    whole = jnp.sum(factor * (info[:, :, 2] + info[:, :, 3]), axis=0)
    return jnp.sum((factor / whole)[..., None] * part, axis=0)


def expert_layer(low, high, gain, gate, up, down):
    slots, features = low.shape[2:]
    return pl.pallas_call(
        expert_kernel,
        out_shape=jax.ShapeDtypeStruct((NC, NX, slots, features), jnp.bfloat16),
        in_specs=[VMEM] * 6,
        out_specs=VMEM,
        compiler_params=pltpu.CompilerParams(vmem_limit_bytes=16 * 2**20),
        name="expert",
    )(low, high, gain, gate, up, down)


def body(
    queries,
    key_cache,
    value_cache,
    new_key,
    new_value,
    lengths,
    experts,
    combine,
    residual,
    norm_gain,
    w_gate,
    w_up,
    w_down,
):
    bf16, f32 = jnp.bfloat16, jnp.float32
    rows, width = residual.shape
    dev_count = NX * NZ * NC
    outer_count = lax.axis_size("zl") * lax.axis_size("y")
    copies = outer_count // EXPERTS
    at_x, at_z, at_c = (lax.axis_index(a) for a in DEV)
    share = width // dev_count
    own_heads = HEADS // dev_count
    slots = outer_count * CAP

    packet = local_attention(lengths, queries, key_cache, value_cache, new_key, new_value)
    arrived = lax.all_to_all(packet, DEV, split_axis=0, concat_axis=0, tiled=True)
    attended = merge(arrived)
    attended = jnp.transpose(attended.reshape(NZ, own_heads, rows, HD), (2, 0, 1, 3))
    attended = attended.reshape(rows, NZ, share)
    res = residual.reshape(rows, NX, NZ, NC, share)
    res = lax.dynamic_slice(res, (0, at_x, 0, at_c, 0), (rows, 1, NZ, 1, share))
    state = res.reshape(rows, NZ, share).astype(f32) + attended
    own_state = lax.dynamic_index_in_dim(state, at_z, 1, keepdims=False)
    gain = norm_gain.reshape(NX, NZ, NC, share)
    gain = lax.dynamic_slice(gain, (at_x, 0, at_c, 0), (1, NZ, 1, share)).reshape(1, NZ, share)
    scaled = (state * gain).reshape(rows, NZ * share).astype(bf16)

    chosen = experts.reshape(rows * TOPK)
    hits = (chosen[:, None] == jnp.arange(EXPERTS, dtype=jnp.int32)[None, :]).astype(jnp.int32)
    rank = jnp.sum((jnp.cumsum(hits, axis=0) - hits) * hits, axis=1)
    slot = (rank[:, None] == jnp.arange(CAP, dtype=jnp.int32)[None, :]).astype(jnp.int32)
    placement = (hits[:, :, None] * slot[:, None, :]).reshape(rows, TOPK, EXPERTS, CAP)
    row_slots = jnp.sum(placement, axis=1)
    packed = jnp.einsum(
        "rec,rd->ecd", row_slots.astype(bf16), scaled, preferred_element_type=f32
    ).astype(bf16)
    outgoing = jnp.repeat(packed, copies, axis=0)
    incoming = lax.all_to_all(outgoing, OUTER, split_axis=0, concat_axis=0, tiled=True)
    slab = incoming.reshape(slots, NZ * share)
    over_x = lax.all_gather(slab, "x", axis=0, tiled=False)
    low = lax.all_gather(over_x[: NX // 2], "c", axis=0, tiled=False)
    high = lax.all_gather(over_x[NX // 2 :], "c", axis=0, tiled=False)
    cut = expert_layer(low, high, norm_gain.reshape(1, width), w_gate.T, w_up.T, w_down)

    over_c = lax.all_to_all(cut, "c", split_axis=0, concat_axis=0, tiled=True)
    over_c = jnp.sum(over_c.astype(f32), axis=0).astype(bf16)
    from_x = lax.all_to_all(over_c, "x", split_axis=0, concat_axis=0, tiled=True)
    from_x = jnp.sum(from_x.astype(f32), axis=0)
    home = from_x.reshape(outer_count, CAP, NZ, share)
    home = jnp.transpose(home, (0, 2, 1, 3)).reshape(outer_count * NZ, CAP, share).astype(bf16)
    returned = lax.all_to_all(home, OUTER + ("zh",), split_axis=0, concat_axis=0, tiled=True)
    returned = returned.reshape(EXPERTS, copies * NZ, CAP, share).astype(f32)
    expert_output = jnp.sum(returned, axis=1)
    mix_weights = jnp.sum(placement.astype(f32) * combine[:, :, None, None], axis=1)
    moe = jnp.einsum("rec,ecd->rd", mix_weights, expert_output, precision=lax.Precision.HIGHEST)
    return (own_state + moe).astype(bf16)


def solution(mesh):
    fine = Mesh(mesh.devices.reshape(6, 8, NX, NZ, NC), OUTER + DEV)
    return jax.shard_map(
        body,
        mesh=fine,
        in_specs=(
            P(OUTER, None),
            P(OUTER, DEV, None),
            P(OUTER, DEV, None),
            P(OUTER, None),
            P(OUTER, None),
            P(OUTER),
            P(OUTER, None),
            P(OUTER, None),
            P(OUTER, None),
            P(),
            P(None, OUTER + DEV),
            P(None, OUTER + DEV),
            P(OUTER + DEV, None),
        ),
        out_specs=P(OUTER, DEV),
        check_vma=False,
    )
```

time: 148 us -> 126 us (0.85)
  local copies, waits for them, and re-layouts: 19.7 us -> 1.53 us
  matrix products: 9.2 us -> 1 us
  Pallas kernels: 0 us -> 5.33 us
  other arithmetic: 4.71 us -> 1.9 us
    convert_element_type x6 -> x3, local copies, waits for them, and re-layouts: 11.2 us -> 0.83 us  [the longest x2 0.81 us: body(): jnp.transpose(home, (0, 2, 1, 3)).reshape(outer_count * NZ, CAP, share)]
    dot_general x6 -> x1, matrix products: 8.4 us -> 0.19 us  [body(): jnp.einsum('rec,rd->ecd', row_slots.astype(bf16), scaled, preferred_eleme...]
    pallas_call x0 -> x2, Pallas kernels: none -> 5.33 us  [the longest x1 4.04 us: local_attention(): pl.pallas_call(attend_kernel, out_shape=jax.ShapeDtypeStruct((NX * NZ * N...]
    reshape x8 -> x3, local copies, waits for them, and re-layouts: 5.4 us -> 0.08 us  [the longest x1 0.04 us: body(): res = residual.reshape(rows, NX, NZ, NC, share)]
where the time goes in v2:
time: 126 us
  blocking collectives  64.5 us (51%)
  waiting for transfers between devices  27.2 us (22%)
  starting transfers between devices  23.8 us (19%)
  Pallas kernels  5.33 us (4%)
  other arithmetic  1.9 us (2%)
  local copies, waits for them, and re-layouts  1.53 us (1%)
    all_to_all x1, blocking collectives, body(): lax.all_to_all(outgoing, OUTER, split_axis=0, concat_axis=0, tiled=True)  29.1 us
    all_to_all x1, starting transfers between devices, body(): lax.all_to_all(packet, DEV, split_axis=0, concat_axis=0, tiled=True)  17.1 us
    all_to_all x1, waiting for transfers between devices, body(): lax.all_to_all(home, OUTER + ('zh',), split_axis=0, concat_axis=0, tiled=...  14.3 us
    all_to_all x1, blocking collectives, body(): lax.all_to_all(over_c, 'x', split_axis=0, concat_axis=0, tiled=True)  13.1 us
    all_gather x1, blocking collectives, body(): over_x = lax.all_gather(slab, 'x', axis=0, tiled=False)  13.1 us
    all_to_all x1, waiting for transfers between devices, body(): lax.all_to_all(packet, DEV, split_axis=0, concat_axis=0, tiled=True)  12.9 us
    all_to_all x1, starting transfers between devices, body(): lax.all_to_all(home, OUTER + ('zh',), split_axis=0, concat_axis=0, tiled=...  6.77 us
    all_to_all x1, blocking collectives, body(): over_c = lax.all_to_all(cut, 'c', split_axis=0, concat_axis=0, tiled=True)  4.68 us
  transfers between devices with their start and end apart: 2, of which 2 were waited for; matrix products, arithmetic and copies ran while one was open for 1% of the time, Pallas kernels for 0%

profile of v2, /device:TPU:8, one launch (start us, length us, event | category | flops | bytes accessed | tf_op | source)
XLA Modules:
  0.0 125.5 jit_solution(848826063574107271)
XLA Ops:
  0.0 4.0 %attend.1 = bf16[16,24,256]{2,1,0:T(8,128)(2,1)} custom-call(s32[4]{0:T(128)} %length_ref.1, bf16[4,6144]{1,0:T(4,128)(2,1)} %q_ref.1, bf16[256,1024]{1,0:T(8,128)(2,1)} %bitcast.42, bf16[256,1024]{1,0:T(8,128)(2,1)} %bitcast.43, bf16[4,1024]{1,0:T(4,128)(2,1)} %nk_ref.1, bf16[4,1024]{1,0:T(4,128)(2,1)} %nv_ref.1), custom_call_target="tpu_custom_call" | custom-call | tf_op jit(solution)/shard_map/attend/pallas_call | solution.py:128
  4.1 17.1 %all-to-all-start = ((bf16[16,24,256]{2,1,0:T(8,128)(2,1)}), bf16[16,24,256]{2,1,0:T(8,128)(2,1)S(1)}, u32[]{:S(2)}, u32[]{:S(2)}) async-start(bf16[16,24,256]{2,1,0:T(8,128)(2,1)} %attend.1), calls=%async_computation | async-start | bytes 393216 | tf_op jit(solution)/shard_map/all_to_all | solution.py:195
  21.1 0.1 copy.41
  21.4 0.2 select_reduce_fusion
  21.7 0.1 copy.42
  22.2 12.9 %all-to-all-done = bf16[16,24,256]{2,1,0:T(8,128)(2,1)S(1)} async-done(((bf16[16,24,256]{2,1,0:T(8,128)(2,1)}), bf16[16,24,256]{2,1,0:T(8,128)(2,1)S(1)}, u32[]{:S(2)}, u32[]{:S(2)}) %all-to-all-start) | async-done | bytes 196640 | tf_op jit(solution)/shard_map/all_to_all | solution.py:195
  35.1 0.4 fusion.14
  35.6 0.3 fusion.3
  35.8 0.1 multiply_reduce_fusion
  36.0 0.2 convolution_convert_fusion
  36.3 29.1 %all_to_all.25 = bf16[48,2,768]{2,1,0:T(2,128)(2,1)S(1)} all-to-all(bf16[48,2,768]{2,1,0:T(2,128)(2,1)S(1)} %bitcast.40), channel_id=1, replica_groups=mesh['zl'=6,'y'=8,'x'=4,'zh'=2,'c'=2] {'zl','y'}, dimensions={0} | all-to-all | bytes 294912 | tf_op jit(solution)/shard_map/all_to_all | solution.py:217
  65.4 13.1 %all_gather.15 = bf16[4,96,768]{2,1,0:T(8,128)(2,1)S(1)} all-gather(bf16[1,96,768]{2,1,0:T(8,128)(2,1)S(1)} %all_gather_reshape.3), channel_id=1, replica_groups=mesh['zl'=6,'y'=8,'x'=4,'zh'=2,'c'=2] {'x'}, dimensions={0}, use_global_device_ids=true | all-gather | bytes 737280 | tf_op jit(solution)/shard_map/all_gather | solution.py:219
  78.5 2.4 %all-gather.1 = bf16[4,96,768]{2,1,0:T(8,128)(2,1)S(1)} all-gather(bf16[2,96,768]{2,1,0:T(8,128)(2,1)S(1)} %get-tuple-element.10), channel_id=3, replica_groups=mesh['zl'=6,'y'=8,'x'=4,'zh'=2,'c'=2] {'c'}, dimensions={0}, use_global_device_ids=true | all-gather | bytes 884736 | tf_op jit(solution)/shard_map/all_gather | solution.py:221
  80.9 2.2 %all-gather = bf16[4,96,768]{2,1,0:T(8,128)(2,1)S(1)} all-gather(bf16[2,96,768]{2,1,0:T(8,128)(2,1)S(1)} %get-tuple-element.11), channel_id=2, replica_groups=mesh['zl'=6,'y'=8,'x'=4,'zh'=2,'c'=2] {'c'}, dimensions={0}, use_global_device_ids=true | all-gather | bytes 884736 | tf_op jit(solution)/shard_map/all_gather | solution.py:220
  83.1 1.3 %expert.1 = bf16[2,4,96,768]{3,2,1,0:T(8,128)(2,1)S(1)} custom-call(bf16[2,2,96,768]{3,2,1,0:T(8,128)(2,1)S(1)} %bitcast.35, bf16[2,2,96,768]{3,2,1,0:T(8,128)(2,1)S(1)} %bitcast.34, f32[1,6144]{1,0:T(1,128)S(1)} %bitcast.38, bf16[96,6144]{1,0:T(8,128)(2,1)S(1)} %bitcast.36, bf16[96,6144]{1,0:T(8,128)(2,1)S(1)} %bitcast.37, bf16[96,6144]{1,0:T(8,128)(2,1)S(1)} %copy-done.2), custom_call_target="tpu_custom_call" | custom-call | tf_op jit(solution)/shard_map/expert/pallas_call | solution.py:159
  84.4 4.7 %all_to_all.26 = bf16[2,4,96,768]{3,2,1,0:T(8,128)(2,1)S(1)} all-to-all(bf16[2,4,96,768]{3,2,1,0:T(8,128)(2,1)S(1)} %expert.1), channel_id=1, replica_groups=mesh['zl'=6,'y'=8,'x'=4,'zh'=2,'c'=2] {'c'}, dimensions={0} | all-to-all | bytes 2359296 | tf_op jit(solution)/shard_map/all_to_all | solution.py:224
  89.1 0.2 reduce_sum.83
  89.4 13.1 %all_to_all.27 = bf16[4,96,768]{2,1,0:T(8,128)(2,1)S(1)} all-to-all(bf16[4,96,768]{2,1,0:T(8,128)(2,1)S(1)} %reduce_sum.83), channel_id=1, replica_groups=mesh['zl'=6,'y'=8,'x'=4,'zh'=2,'c'=2] {'x'}, dimensions={0} | all-to-all | bytes 1179648 | tf_op jit(solution)/shard_map/all_to_all | solution.py:226
  102.5 0.1 reduce_sum.84
  102.6 0.8 copy.44
  103.4 6.8 %all-to-all-start.4 = ((bf16[96,2,384]{2,1,0:T(2,128)(2,1)}), bf16[96,2,384]{2,1,0:T(2,128)(2,1)S(1)}, u32[]{:S(2)}, u32[]{:S(2)}) async-start(bf16[96,2,384]{2,1,0:T(2,128)(2,1)} %bitcast.14), calls=%async_computation.4 | async-start | bytes 294912 | tf_op jit(solution)/shard_map/all_to_all | solution.py:230
  110.4 14.3 %all-to-all-done.4 = bf16[96,2,384]{2,1,0:T(2,128)(2,1)S(1)} async-done(((bf16[96,2,384]{2,1,0:T(2,128)(2,1)}), bf16[96,2,384]{2,1,0:T(2,128)(2,1)S(1)}, u32[]{:S(2)}, u32[]{:S(2)}) %all-to-all-start.4) | async-done | bytes 147488 | tf_op jit(solution)/shard_map/all_to_all | solution.py:230
  124.6 0.1 convert_reduce_fusion
  124.7 0.8 fusion.1
  (39 shorter events, 1.0 us)
Async XLA Ops:
  0.0 21.1 %copy-start.5 = (s32[4,2]{0,1:T(2,128)S(1)}, s32[4,2]{0,1:T(2,128)}, u32[]{:S(2)}) copy-start(s32[4,2]{0,1:T(2,128)} %param.19) | copy-start | bytes 100
  0.0 21.8 %copy-start.3 = (f32[6144]{0:T(1024)S(1)}, f32[6144]{0:T(1024)}, u32[]{:S(2)}) copy-start(f32[6144]{0:T(1024)} %param.22) | copy-start | bytes 73732
  0.0 21.9 %copy-start.4 = (bf16[4,6144]{1,0:T(4,128)(2,1)S(1)}, bf16[4,6144]{1,0:T(4,128)(2,1)}, u32[]{:S(2)}) copy-start(bf16[4,6144]{1,0:T(4,128)(2,1)} %param.21) | copy-start | bytes 147460
  4.1 31.0 %all-to-all-start = ((bf16[16,24,256]{2,1,0:T(8,128)(2,1)}), bf16[16,24,256]{2,1,0:T(8,128)(2,1)S(1)}, u32[]{:S(2)}, u32[]{:S(2)}) async-start(bf16[16,24,256]{2,1,0:T(8,128)(2,1)} %attend.1), calls=%async_computation | async-start | bytes 393216 | tf_op jit(solution)/shard_map/all_to_all | solution.py:195
  65.4 17.7 %copy-start.2 = (bf16[96,6144]{1,0:T(8,128)(2,1)S(1)}, bf16[96,6144]{1,0:T(8,128)(2,1)}, u32[]{:S(2)}) copy-start(bf16[96,6144]{1,0:T(8,128)(2,1)} %down_ref.1) | copy-start | bytes 3538948
  78.5 4.6 %copy-start.1 = (bf16[6144,96]{0,1:T(8,128)(2,1)S(1)}, bf16[6144,96]{0,1:T(8,128)(2,1)}, u32[]{:S(2)}) copy-start(bf16[6144,96]{0,1:T(8,128)(2,1)} %param.24) | copy-start | bytes 3538948
  78.5 4.6 %copy-start = (bf16[6144,96]{0,1:T(8,128)(2,1)S(1)}, bf16[6144,96]{0,1:T(8,128)(2,1)}, u32[]{:S(2)}) copy-start(bf16[6144,96]{0,1:T(8,128)(2,1)} %param.23) | copy-start | bytes 3538948
  89.4 20.9 %copy-start.6 = (f32[4,2]{0,1:T(2,128)S(1)}, f32[4,2]{0,1:T(2,128)}, u32[]{:S(2)}) copy-start(f32[4,2]{0,1:T(2,128)} %param.20) | copy-start | bytes 100
  103.4 21.2 %all-to-all-start.4 = ((bf16[96,2,384]{2,1,0:T(2,128)(2,1)}), bf16[96,2,384]{2,1,0:T(2,128)(2,1)S(1)}, u32[]{:S(2)}, u32[]{:S(2)}) async-start(bf16[96,2,384]{2,1,0:T(2,128)(2,1)} %bitcast.14), calls=%async_computation.4 | async-start | bytes 294912 | tf_op jit(solution)/shard_map/all_to_all | solution.py:230

commit v3 on v2

v3 whole, which is shorter than its diff:
```python
import math

import jax
import jax.numpy as jnp
from jax import lax
from jax.experimental import pallas as pl
from jax.experimental.pallas import tpu as pltpu
from jax.sharding import Mesh
from jax.sharding import PartitionSpec as P

HEADS = 48
KVH = 8
HD = 128
EXPERTS = 8
TOPK = 2
CAP = 2
DEAD = -1e30

OUTER = ("zl", "y")
DEV = ("x", "zh", "c")
NX, NZ, NC = 4, 2, 2
ANY = pl.BlockSpec(memory_space=pl.ANY)
VMEM = pl.BlockSpec(memory_space=pltpu.VMEM)
NT = (((1,), (1,)), ((), ()))


def starts_of(core, share):
    return [pl.multiple_of((i * NC + core) * share, share) for i in range(NX * NZ)]


def pack_copies(refs, out_ref, sems):
    share = refs[0].shape[1] // (NX * NZ * NC)
    return [
        pltpu.make_async_copy(
            ref.at[:, pl.ds(start, share)],
            out_ref.at[kind, :, pl.ds(i * share, share)],
            sems.at[kind, i],
        )
        for kind, ref in enumerate(refs)
        for i, start in enumerate(starts_of(1 - lax.axis_index("c"), share))
    ]


def attend_kernel(
    length_ref,
    q_ref,
    k_ref,
    v_ref,
    nk_ref,
    nv_ref,
    gate_ref,
    up_ref,
    down_ref,
    out_ref,
    other_ref,
    q_rows,
    nk_rows,
    nv_rows,
    packed,
    sems,
):
    copies = pack_copies((gate_ref, up_ref, down_ref), other_ref, sems)
    for copy in copies:
        copy.start()
    f32, bf16 = jnp.float32, jnp.bfloat16
    tokens = q_ref.shape[0]
    span = k_ref.shape[0] // tokens
    group = HEADS // KVH
    lines = group * tokens
    half = lines // NC
    scale = 1.0 / math.sqrt(HD)
    dev_index = (lax.axis_index("x") * NZ + lax.axis_index("zh")) * NC + lax.axis_index("c")
    queries = q_ref[...].astype(f32)
    new_keys = nk_ref[...].astype(f32)
    new_values = nv_ref[...].astype(f32)
    for head in range(HEADS):
        g = head // group
        at = slice(head * tokens, (head + 1) * tokens)
        q_rows[at, :] = queries[:, head * HD : (head + 1) * HD]
        nk_rows[at, :] = new_keys[:, g * HD : (g + 1) * HD]
        nv_rows[at, :] = new_values[:, g * HD : (g + 1) * HD]
    all_lines = HEADS * tokens
    row = lax.broadcasted_iota(jnp.int32, (lines, tokens * span), 0) % tokens
    column = lax.broadcasted_iota(jnp.int32, (lines, tokens * span), 1)
    limit = jnp.zeros((lines, tokens * span), jnp.int32)
    for t in range(tokens):
        limit = jnp.where(row == t, length_ref[t], limit)
    live = (column // span == row) & (dev_index * span + column % span < limit)
    live = jnp.concatenate([live.astype(f32)] * KVH, axis=0) > 0.5
    lane = lax.broadcasted_iota(jnp.int32, (all_lines, HD), 1)
    first = dev_index == 0
    q = q_rows[...]
    scores = jnp.concatenate(
        [
            lax.dot_general(
                q[g * lines : (g + 1) * lines].astype(bf16),
                k_ref[:, g * HD : (g + 1) * HD],
                NT,
                preferred_element_type=f32,
            )
            for g in range(KVH)
        ],
        axis=0,
    )
    scores = jnp.where(live, scores * scale, DEAD)
    own = jnp.sum(q * nk_rows[...], axis=1, keepdims=True) * scale
    own = jnp.where(first, own, DEAD)
    top = jnp.maximum(jnp.max(scores, axis=1, keepdims=True), own)
    top_high = top.astype(bf16).astype(f32)
    top_low = (top - top_high).astype(bf16).astype(f32)
    base = top_high + top_low
    weights = jnp.where(live, jnp.exp(scores - base), 0.0).astype(bf16)
    own_weight = jnp.where(first, jnp.exp(own - base), 0.0).astype(bf16).astype(f32)
    acc = jnp.concatenate(
        [
            jnp.dot(
                weights[g * lines : (g + 1) * lines],
                v_ref[:, g * HD : (g + 1) * HD],
                preferred_element_type=f32,
            )
            for g in range(KVH)
        ],
        axis=0,
    )
    acc = acc + own_weight * nv_rows[...]
    total = jnp.sum(weights.astype(f32), axis=1, keepdims=True) + own_weight
    total_high = total.astype(bf16).astype(f32)
    total_low = total - total_high
    stats = jnp.where(
        lane == 0,
        top_high,
        jnp.where(lane == 1, top_low, jnp.where(lane == 2, total_high, total_low)),
    )
    for x in range(NX):
        for z in range(NZ):
            for c in range(NC):
                to = slice(z * half, (z + 1) * half)
                at = ((x * NZ + z) * NC + c) * half
                packed[x * NC + c, to, :HD] = acc[at : at + half]
                packed[x * NC + c, to, HD:] = stats[at : at + half]
    for x in range(NX):
        for c in range(NC):
            block = packed[x * NC + c].astype(bf16)
            for z in range(NZ):
                out_ref[(x * NZ + z) * NC + c] = block
    for copy in copies:
        copy.wait()


def enter_kernel(state_ref, gain_ref, gate_ref, up_ref, pair_ref, out_ref, other, sem):
    f32 = jnp.float32
    rows, span = state_ref.shape[1:]
    share = span // NZ
    hidden = gate_ref.shape[0]
    at_c = lax.axis_index("c")
    fetch = pltpu.make_async_copy(pair_ref.at[1 - at_c, pl.ds(0, 2)], other, sem)
    fetch.start()
    starts = starts_of(at_c, share)

    def columns(ref, x):
        return jnp.concatenate(
            [ref[:, pl.ds(s, share)] for s in starts[x * NZ : (x + 1) * NZ]], axis=1
        )

    squares = jnp.zeros((rows, HD), f32)
    own = [jnp.zeros((rows, hidden), f32)] * 2
    for x in range(NX):
        block = state_ref[x]
        for kind, ref in enumerate((gate_ref, up_ref)):
            own[kind] += lax.dot_general(block, columns(ref, x), NT, preferred_element_type=f32)
        state = block.astype(f32) / columns(gain_ref, x)
        state = state * state
        for at in range(0, span, HD):
            squares += state[:, at : at + HD]
    total = jnp.sum(squares, axis=1, keepdims=True)
    total = jnp.broadcast_to(total, (rows, HD - hidden))
    fetch.wait()
    for kind in range(2):
        far = jnp.zeros((rows, hidden), f32)
        for x in range(NX):
            far += lax.dot_general(
                state_ref[x],
                other[kind, :, x * span : (x + 1) * span],
                NT,
                preferred_element_type=f32,
            )
        out_ref[kind * NC] = jnp.concatenate([own[kind], total], axis=1)
        out_ref[kind * NC + 1] = jnp.concatenate([far, total], axis=1)


def leave_kernel(sums_ref, down_ref, pair_ref, out_ref, other, sem):
    f32, bf16 = jnp.float32, jnp.bfloat16
    hidden, width = down_ref.shape
    share = out_ref.shape[3]
    at_c = lax.axis_index("c")
    fetch = pltpu.make_async_copy(pair_ref.at[1 - at_c, 2], other, sem)
    fetch.start()
    factor = None
    active = []
    for far in range(NC):
        gate = sums_ref[at_c, far] + sums_ref[1 - at_c, 1 - far]
        up = sums_ref[at_c, NC + far] + sums_ref[1 - at_c, NC + 1 - far]
        if factor is None:
            factor = lax.rsqrt(gate[:, HD - 1 :] / width + 1e-05)
        gate = gate[:, :hidden] * factor
        up = up[:, :hidden] * factor
        active.append((gate / (1.0 + jnp.exp(-gate)) * up).astype(bf16))
    fetch.wait()
    for i, start in enumerate(starts_of(at_c, share)):
        near = jnp.dot(active[0], down_ref[:, pl.ds(start, share)], preferred_element_type=f32)
        far = jnp.dot(active[1], other[:, i * share : (i + 1) * share], preferred_element_type=f32)
        out_ref[i // NZ, i % NZ] = (near + far).astype(bf16)


def local_attention(lengths, queries, key_cache, value_cache, new_key, new_value, gate, up, down):
    rows, span, features = key_cache.shape
    slab_rows = HEADS // (NX * NC) * rows
    hidden, width = down.shape
    return pl.pallas_call(
        attend_kernel,
        out_shape=(
            jax.ShapeDtypeStruct((NX * NZ * NC, slab_rows, 2 * HD), jnp.bfloat16),
            jax.ShapeDtypeStruct((3, hidden, width // NC), jnp.bfloat16),
        ),
        in_specs=[pl.BlockSpec(memory_space=pltpu.SMEM)] + [pl.BlockSpec()] * 5 + [ANY] * 3,
        out_specs=(VMEM, ANY),
        scratch_shapes=[pltpu.VMEM((HEADS * rows, HD), jnp.float32)] * 3
        + [
            pltpu.VMEM((NX * NC, slab_rows, 2 * HD), jnp.float32),
            pltpu.SemaphoreType.DMA((3, NX * NZ)),
        ],
        compiler_params=pltpu.CompilerParams(vmem_limit_bytes=60 * 2**20),
        name="attend",
    )(
        lengths,
        queries,
        key_cache.reshape(rows * span, features),
        value_cache.reshape(rows * span, features),
        new_key,
        new_value,
        gate,
        up,
        down,
    )


def merge(arrived):
    f32 = jnp.float32
    part = arrived[:, :, :HD].astype(f32)
    info = arrived[:, :, HD : HD + 4].astype(f32)
    base_of = info[:, :, 0] + info[:, :, 1]
    factor = jnp.exp(base_of - jnp.max(base_of, axis=0, keepdims=True))
    whole = jnp.sum(factor * (info[:, :, 2] + info[:, :, 3]), axis=0)
    return jnp.sum((factor / whole)[..., None] * part, axis=0)


def expert_enter(state, gain, gate, up, pair):
    hidden, width = gate.shape
    return pl.pallas_call(
        enter_kernel,
        out_shape=jax.ShapeDtypeStruct((2 * NC, state.shape[1], HD), jnp.float32),
        in_specs=[VMEM] * 4 + [ANY],
        out_specs=VMEM,
        scratch_shapes=[
            pltpu.VMEM((2, hidden, width // NC), jnp.bfloat16),
            pltpu.SemaphoreType.DMA,
        ],
        compiler_params=pltpu.CompilerParams(vmem_limit_bytes=50 * 2**20),
        name="enter",
    )(state, gain, gate, up, pair)


def expert_leave(sums, down, pair):
    hidden, width = down.shape
    share = width // (NX * NZ * NC)
    return pl.pallas_call(
        leave_kernel,
        out_shape=jax.ShapeDtypeStruct((NX, NZ, sums.shape[2], share), jnp.bfloat16),
        in_specs=[VMEM] * 2 + [ANY],
        out_specs=VMEM,
        scratch_shapes=[
            pltpu.VMEM((hidden, width // NC), jnp.bfloat16),
            pltpu.SemaphoreType.DMA,
        ],
        compiler_params=pltpu.CompilerParams(vmem_limit_bytes=50 * 2**20),
        name="leave",
    )(sums, down, pair)


def body(
    queries,
    key_cache,
    value_cache,
    new_key,
    new_value,
    lengths,
    experts,
    combine,
    residual,
    norm_gain,
    w_gate,
    w_up,
    w_down,
):
    bf16, f32 = jnp.bfloat16, jnp.float32
    rows, width = residual.shape
    dev_count = NX * NZ * NC
    outer_count = lax.axis_size("zl") * lax.axis_size("y")
    copies = outer_count // EXPERTS
    at_x, at_z, at_c = (lax.axis_index(a) for a in DEV)
    share = width // dev_count
    own_heads = HEADS // dev_count
    slots = outer_count * CAP

    packet, others = local_attention(
        lengths,
        queries,
        key_cache,
        value_cache,
        new_key,
        new_value,
        w_gate.T,
        w_up.T,
        w_down,
    )

    pair = lax.all_gather(others, "c", axis=0, tiled=False)
    arrived = lax.all_to_all(packet, DEV, split_axis=0, concat_axis=0, tiled=True)
    attended = merge(arrived)
    attended = jnp.transpose(attended.reshape(NZ, own_heads, rows, HD), (2, 0, 1, 3))
    attended = attended.reshape(rows, NZ, share)
    res = residual.reshape(rows, NX, NZ, NC, share)
    res = lax.dynamic_slice(res, (0, at_x, 0, at_c, 0), (rows, 1, NZ, 1, share))
    state = res.reshape(rows, NZ, share).astype(f32) + attended
    own_state = lax.dynamic_index_in_dim(state, at_z, 1, keepdims=False)
    gain = norm_gain.reshape(NX, NZ, NC, share)
    gain = lax.dynamic_slice(gain, (at_x, 0, at_c, 0), (1, NZ, 1, share)).reshape(1, NZ, share)
    scaled = (state * gain).reshape(rows, NZ * share).astype(bf16)

    chosen = experts.reshape(rows * TOPK)
    hits = (chosen[:, None] == jnp.arange(EXPERTS, dtype=jnp.int32)[None, :]).astype(jnp.int32)
    rank = jnp.sum((jnp.cumsum(hits, axis=0) - hits) * hits, axis=1)
    slot = (rank[:, None] == jnp.arange(CAP, dtype=jnp.int32)[None, :]).astype(jnp.int32)
    placement = (hits[:, :, None] * slot[:, None, :]).reshape(rows, TOPK, EXPERTS, CAP)
    row_slots = jnp.sum(placement, axis=1)
    packed = jnp.einsum(
        "rec,rd->ecd", row_slots.astype(bf16), scaled, preferred_element_type=f32
    ).astype(bf16)
    outgoing = jnp.repeat(packed, copies, axis=0)
    incoming = lax.all_to_all(outgoing, OUTER, split_axis=0, concat_axis=0, tiled=True)
    slab = incoming.reshape(slots, NZ * share)
    over_x = lax.all_gather(slab, "x", axis=0, tiled=False)
    sums = expert_enter(over_x, norm_gain.reshape(1, width), w_gate.T, w_up.T, pair)
    sums = lax.all_gather(sums, "c", axis=0, tiled=False)
    cut = expert_leave(sums, w_down, pair)

    from_x = lax.all_to_all(cut, "x", split_axis=0, concat_axis=0, tiled=True)
    home = jnp.sum(from_x.astype(f32), axis=0).astype(bf16).reshape(NZ * outer_count, CAP, share)
    returned = lax.all_to_all(home, ("zh",) + OUTER, split_axis=0, concat_axis=0, tiled=True)
    returned = returned.reshape(NZ, EXPERTS, copies, CAP, share).astype(f32)
    expert_output = jnp.sum(returned, axis=(0, 2)).reshape(1, EXPERTS * CAP, share)
    mix_weights = jnp.sum(placement.astype(f32) * combine[:, :, None, None], axis=1)
    moe = jnp.sum(mix_weights.reshape(rows, EXPERTS * CAP, 1) * expert_output, axis=1)
    return (own_state + moe).astype(bf16)


def solution(mesh):
    fine = Mesh(mesh.devices.reshape(6, 8, NX, NZ, NC), OUTER + DEV)
    return jax.shard_map(
        body,
        mesh=fine,
        in_specs=(
            P(OUTER, None),
            P(OUTER, DEV, None),
            P(OUTER, DEV, None),
            P(OUTER, None),
            P(OUTER, None),
            P(OUTER),
            P(OUTER, None),
            P(OUTER, None),
            P(OUTER, None),
            P(),
            P(None, OUTER + DEV),
            P(None, OUTER + DEV),
            P(OUTER + DEV, None),
        ),
        out_specs=P(OUTER, DEV),
        check_vma=False,
    )
```

time: 126 us -> 188 us (1.49)
  the two profiles are of different devices: /device:TPU:8 before, /device:TPU:2 now
where the time goes in v3:
time: 188 us; the launch traced here: 187 us
  Pallas kernels  60.5 us (32%)
  blocking collectives  58.8 us (31%)
  waiting for transfers between devices  26.2 us (14%)
  starting transfers between devices  23.8 us (13%)
  between operations  13.6 us (7%)
  other arithmetic  2.34 us (1%)
    pallas_call x1, Pallas kernels, local_attention(): pl.pallas_call(attend_kernel, out_shape=(jax.ShapeDtypeStruct((NX * NZ *...  56.8 us
    all_to_all x1, blocking collectives, body(): lax.all_to_all(outgoing, OUTER, split_axis=0, concat_axis=0, tiled=True)  30.1 us
    all_to_all x1, starting transfers between devices, body(): lax.all_to_all(packet, DEV, split_axis=0, concat_axis=0, tiled=True)  17.5 us
    all_to_all x1, waiting for transfers between devices, body(): lax.all_to_all(home, ('zh',) + OUTER, split_axis=0, concat_axis=0, tiled=...  15.4 us
    all_to_all x1, blocking collectives, body(): from_x = lax.all_to_all(cut, 'x', split_axis=0, concat_axis=0, tiled=True)  13.4 us
    all_gather x1, blocking collectives, body(): over_x = lax.all_gather(slab, 'x', axis=0, tiled=False)  13.2 us
    all_to_all x1, waiting for transfers between devices, body(): lax.all_to_all(packet, DEV, split_axis=0, concat_axis=0, tiled=True)  10.7 us
    all_to_all x1, starting transfers between devices, body(): lax.all_to_all(home, ('zh',) + OUTER, split_axis=0, concat_axis=0, tiled=...  6.3 us
  transfers between devices with their start and end apart: 3, of which 2 were waited for; matrix products, arithmetic and copies ran while one was open for 1% of the time, Pallas kernels for 0%

profile of v3, /device:TPU:2, one launch (start us, length us, event | category | flops | bytes accessed | tf_op | source)
XLA Modules:
  0.0 187.0 jit_solution(3081196772302484202)
XLA Ops:
  6.5 56.8 %attend.1 = (bf16[16,24,256]{2,1,0:T(8,128)(2,1)}, bf16[3,96,3072]{2,1,0:T(8,128)(2,1)}) custom-call(s32[4]{0:T(128)} %length_ref.1, bf16[4,6144]{1,0:T(4,128)(2,1)} %q_ref.1, bf16[256,1024]{1,0:T(8,128)(2,1)} %bitcast.38, bf16[256,1024]{1,0:T(8,128)(2,1)} %bitcast.39, bf16[4,1024]{1,0:T(4,128)(2,1)} %nk_ref.1, bf16[4,1024]{1,0:T(4,128)(2,1)} %nv_ref.1, ...), custom_call_target="tpu_custom_call" | custom-call | tf_op jit(solution)/shard_map/attend/pallas_call | solution.py:219
  63.5 17.5 %all-to-all-start = ((bf16[16,24,256]{2,1,0:T(8,128)(2,1)}), bf16[16,24,256]{2,1,0:T(8,128)(2,1)S(1)}, u32[]{:S(2)}, u32[]{:S(2)}) async-start(bf16[16,24,256]{2,1,0:T(8,128)(2,1)} %get-tuple-element.7), calls=%async_computation | async-start | bytes 393216 | tf_op jit(solution)/shard_map/all_to_all | solution.py:328
  81.0 0.1 copy.48
  81.3 0.2 select_reduce_fusion
  81.5 0.1 copy.49
  82.0 10.7 %all-to-all-done = bf16[16,24,256]{2,1,0:T(8,128)(2,1)S(1)} async-done(((bf16[16,24,256]{2,1,0:T(8,128)(2,1)}), bf16[16,24,256]{2,1,0:T(8,128)(2,1)S(1)}, u32[]{:S(2)}, u32[]{:S(2)}) %all-to-all-start) | async-done | bytes 196640 | tf_op jit(solution)/shard_map/all_to_all | solution.py:328
  92.8 0.4 fusion.12
  93.2 0.3 fusion.1
  93.5 0.1 multiply_reduce_fusion
  93.6 0.2 convolution_convert_fusion
  93.9 30.1 %all_to_all.20 = bf16[48,2,768]{2,1,0:T(2,128)(2,1)S(1)} all-to-all(bf16[48,2,768]{2,1,0:T(2,128)(2,1)S(1)} %bitcast.37), channel_id=1, replica_groups=mesh['zl'=6,'y'=8,'x'=4,'zh'=2,'c'=2] {'zl','y'}, dimensions={0} | all-to-all | bytes 294912 | tf_op jit(solution)/shard_map/all_to_all | solution.py:350
  124.1 13.2 %all_gather.15.state_ref = bf16[4,96,768]{2,1,0:T(8,128)(2,1)S(1)} all-gather(bf16[1,96,768]{2,1,0:T(8,128)(2,1)S(1)} %all_gather_reshape.3), channel_id=1, replica_groups=mesh['zl'=6,'y'=8,'x'=4,'zh'=2,'c'=2] {'x'}, dimensions={0}, use_global_device_ids=true | all-gather | bytes 737280 | tf_op jit(solution)/shard_map/all_gather | solution.py:352
  137.3 2.1 %enter.1 = f32[4,96,128]{2,1,0:T(8,128)S(1)} custom-call(bf16[4,96,768]{2,1,0:T(8,128)(2,1)S(1)} %all_gather.15.state_ref, f32[1,6144]{1,0:T(1,128)S(1)} %bitcast.33, bf16[96,6144]{1,0:T(8,128)(2,1)S(1)} %bitcast.29, bf16[96,6144]{1,0:T(8,128)(2,1)S(1)} %bitcast.31, bf16[2,3,96,3072]{3,2,1,0:T(8,128)(2,1)} %bitcast.34), custom_call_target="tpu_custom_call" | custom-call | tf_op jit(solution)/shard_map/enter/pallas_call | solution.py:259
  139.4 2.1 %all-gather.1 = f32[8,96,128]{2,1,0:T(8,128)S(1)} all-gather(f32[4,96,128]{2,1,0:T(8,128)S(1)} %enter.1), channel_id=3, replica_groups=mesh['zl'=6,'y'=8,'x'=4,'zh'=2,'c'=2] {'c'}, dimensions={0}, use_global_device_ids=true | all-gather | bytes 589824 | tf_op jit(solution)/shard_map/all_gather | solution.py:354
  141.5 1.6 leave.1
  143.1 13.4 %all_to_all.21 = bf16[4,2,96,384]{3,2,1,0:T(8,128)(2,1)S(1)} all-to-all(bf16[4,2,96,384]{3,2,1,0:T(8,128)(2,1)S(1)} %leave.1), channel_id=1, replica_groups=mesh['zl'=6,'y'=8,'x'=4,'zh'=2,'c'=2] {'x'}, dimensions={0} | all-to-all | bytes 1179648 | tf_op jit(solution)/shard_map/all_to_all | solution.py:357
  156.5 0.1 reduce_sum.80
  156.6 0.7 reshape.118
  157.3 6.3 %all-to-all-start.3 = ((bf16[96,2,384]{2,1,0:T(2,128)(2,1)}), bf16[96,2,384]{2,1,0:T(2,128)(2,1)S(1)}, u32[]{:S(2)}, u32[]{:S(2)}) async-start(bf16[96,2,384]{2,1,0:T(2,128)(2,1)} %reshape.118), calls=%async_computation.3 | async-start | bytes 294912 | tf_op jit(solution)/shard_map/all_to_all | solution.py:359
  163.7 0.1 copy.50
  163.9 15.4 %all-to-all-done.3 = bf16[96,2,384]{2,1,0:T(2,128)(2,1)S(1)} async-done(((bf16[96,2,384]{2,1,0:T(2,128)(2,1)}), bf16[96,2,384]{2,1,0:T(2,128)(2,1)S(1)}, u32[]{:S(2)}, u32[]{:S(2)}) %all-to-all-start.3) | async-done | bytes 147488 | tf_op jit(solution)/shard_map/all_to_all | solution.py:359
  179.3 0.1 convert_reduce_fusion
  179.5 0.1 multiply_reduce_fusion.1
  179.6 0.6 fusion.6
  (42 shorter events, 1.1 us)
Async XLA Ops:
  6.5 130.8 %all-gather.4.cloned.1.call-start = ((), (), s32[]{:S(2)}) async-start(), calls=%async_computation.4 | async-start | bytes 5308416 | tf_op jit(solution)/shard_map/all_gather | solution.py:327
  63.4 17.6 %copy-start.5 = (s32[4,2]{0,1:T(2,128)S(1)}, s32[4,2]{0,1:T(2,128)}, u32[]{:S(2)}) copy-start(s32[4,2]{0,1:T(2,128)} %param.19) | copy-start | bytes 100
  63.4 18.2 %copy-start.3 = (f32[6144]{0:T(1024)S(1)}, f32[6144]{0:T(1024)}, u32[]{:S(2)}) copy-start(f32[6144]{0:T(1024)} %param.22) | copy-start | bytes 73732
  63.4 18.3 %copy-start.4 = (bf16[4,6144]{1,0:T(4,128)(2,1)S(1)}, bf16[4,6144]{1,0:T(4,128)(2,1)}, u32[]{:S(2)}) copy-start(bf16[4,6144]{1,0:T(4,128)(2,1)} %param.21) | copy-start | bytes 147460
  63.5 29.3 %all-to-all-start = ((bf16[16,24,256]{2,1,0:T(8,128)(2,1)}), bf16[16,24,256]{2,1,0:T(8,128)(2,1)S(1)}, u32[]{:S(2)}, u32[]{:S(2)}) async-start(bf16[16,24,256]{2,1,0:T(8,128)(2,1)} %get-tuple-element.7), calls=%async_computation | async-start | bytes 393216 | tf_op jit(solution)/shard_map/all_to_all | solution.py:328
  92.8 44.6 %copy-start.1 = (bf16[6144,96]{0,1:T(8,128)(2,1)S(1)}, bf16[6144,96]{0,1:T(8,128)(2,1)}, u32[]{:S(2)}) copy-start(bf16[6144,96]{0,1:T(8,128)(2,1)} %param.24) | copy-start | bytes 3538948
  93.2 44.1 %copy-start = (bf16[6144,96]{0,1:T(8,128)(2,1)S(1)}, bf16[6144,96]{0,1:T(8,128)(2,1)}, u32[]{:S(2)}) copy-start(bf16[6144,96]{0,1:T(8,128)(2,1)} %param.23) | copy-start | bytes 3538948
  137.3 4.2 %copy-start.2 = (bf16[96,6144]{1,0:T(8,128)(2,1)S(1)}, bf16[96,6144]{1,0:T(8,128)(2,1)}, u32[]{:S(2)}) copy-start(bf16[96,6144]{1,0:T(8,128)(2,1)} %down_ref.3) | copy-start | bytes 3538948
  143.1 20.5 %copy-start.6 = (f32[4,2]{0,1:T(2,128)S(1)}, f32[4,2]{0,1:T(2,128)}, u32[]{:S(2)}) copy-start(f32[4,2]{0,1:T(2,128)} %param.20) | copy-start | bytes 100
  157.3 22.1 %all-to-all-start.3 = ((bf16[96,2,384]{2,1,0:T(2,128)(2,1)}), bf16[96,2,384]{2,1,0:T(2,128)(2,1)S(1)}, u32[]{:S(2)}, u32[]{:S(2)}) async-start(bf16[96,2,384]{2,1,0:T(2,128)(2,1)} %reshape.118), calls=%async_computation.3 | async-start | bytes 294912 | tf_op jit(solution)/shard_map/all_to_all | solution.py:359
Sparse Core Ops, SparseCore 0:
  63.6 30.3 all-gather.3

commit v4 on v3

--- a/solution.py
+++ b/solution.py
@@ -28,12 +28,12 @@
     return [pl.multiple_of((i * NC + core) * share, share) for i in range(NX * NZ)]
 
 
-def pack_copies(refs, out_ref, sems):
+def pack_copies(refs, stage, sems):
     share = refs[0].shape[1] // (NX * NZ * NC)
     return [
         pltpu.make_async_copy(
             ref.at[:, pl.ds(start, share)],
-            out_ref.at[kind, :, pl.ds(i * share, share)],
+            stage.at[kind, :, pl.ds(i * share, share)],
             sems.at[kind, i],
         )
         for kind, ref in enumerate(refs)
@@ -57,9 +57,11 @@
     nk_rows,
     nv_rows,
     packed,
+    stage,
     sems,
+    out_sem,
 ):
-    copies = pack_copies((gate_ref, up_ref, down_ref), other_ref, sems)
+    copies = pack_copies((gate_ref, up_ref, down_ref), stage, sems)
     for copy in copies:
         copy.start()
     f32, bf16 = jnp.float32, jnp.bfloat16
@@ -102,6 +104,10 @@
         ],
         axis=0,
     )
+    for copy in copies:
+        copy.wait()
+    leave = pltpu.make_async_copy(stage, other_ref, out_sem)
+    leave.start()
     scores = jnp.where(live, scores * scale, DEAD)
     own = jnp.sum(q * nk_rows[...], axis=1, keepdims=True) * scale
     own = jnp.where(first, own, DEAD)
@@ -143,18 +149,15 @@
             block = packed[x * NC + c].astype(bf16)
             for z in range(NZ):
                 out_ref[(x * NZ + z) * NC + c] = block
-    for copy in copies:
-        copy.wait()
-
-
-def enter_kernel(state_ref, gain_ref, gate_ref, up_ref, pair_ref, out_ref, other, sem):
+    leave.wait()
+
+
+def enter_kernel(state_ref, gain_ref, gate_ref, up_ref, other, out_ref):
     f32 = jnp.float32
     rows, span = state_ref.shape[1:]
     share = span // NZ
     hidden = gate_ref.shape[0]
     at_c = lax.axis_index("c")
-    fetch = pltpu.make_async_copy(pair_ref.at[1 - at_c, pl.ds(0, 2)], other, sem)
-    fetch.start()
     starts = starts_of(at_c, share)
 
     def columns(ref, x):
@@ -174,7 +177,6 @@
             squares += state[:, at : at + HD]
     total = jnp.sum(squares, axis=1, keepdims=True)
     total = jnp.broadcast_to(total, (rows, HD - hidden))
-    fetch.wait()
     for kind in range(2):
         far = jnp.zeros((rows, hidden), f32)
         for x in range(NX):
@@ -188,13 +190,11 @@
         out_ref[kind * NC + 1] = jnp.concatenate([far, total], axis=1)
 
 
-def leave_kernel(sums_ref, down_ref, pair_ref, out_ref, other, sem):
+def leave_kernel(sums_ref, down_ref, other, out_ref):
     f32, bf16 = jnp.float32, jnp.bfloat16
     hidden, width = down_ref.shape
     share = out_ref.shape[3]
     at_c = lax.axis_index("c")
-    fetch = pltpu.make_async_copy(pair_ref.at[1 - at_c, 2], other, sem)
-    fetch.start()
     factor = None
     active = []
     for far in range(NC):
@@ -205,10 +205,9 @@
         gate = gate[:, :hidden] * factor
         up = up[:, :hidden] * factor
         active.append((gate / (1.0 + jnp.exp(-gate)) * up).astype(bf16))
-    fetch.wait()
     for i, start in enumerate(starts_of(at_c, share)):
         near = jnp.dot(active[0], down_ref[:, pl.ds(start, share)], preferred_element_type=f32)
-        far = jnp.dot(active[1], other[:, i * share : (i + 1) * share], preferred_element_type=f32)
+        far = jnp.dot(active[1], other[2, :, i * share : (i + 1) * share], preferred_element_type=f32)
         out_ref[i // NZ, i % NZ] = (near + far).astype(bf16)
 
 
@@ -227,7 +226,9 @@
         scratch_shapes=[pltpu.VMEM((HEADS * rows, HD), jnp.float32)] * 3
         + [
             pltpu.VMEM((NX * NC, slab_rows, 2 * HD), jnp.float32),
+            pltpu.VMEM((3, hidden, width // NC), jnp.bfloat16),
             pltpu.SemaphoreType.DMA((3, NX * NZ)),
+            pltpu.SemaphoreType.DMA,
         ],
         compiler_params=pltpu.CompilerParams(vmem_limit_bytes=60 * 2**20),
         name="attend",
@@ -254,37 +255,27 @@
     return jnp.sum((factor / whole)[..., None] * part, axis=0)
 
 
-def expert_enter(state, gain, gate, up, pair):
-    hidden, width = gate.shape
+def expert_enter(state, gain, gate, up, other):
     return pl.pallas_call(
         enter_kernel,
         out_shape=jax.ShapeDtypeStruct((2 * NC, state.shape[1], HD), jnp.float32),
-        in_specs=[VMEM] * 4 + [ANY],
+        in_specs=[VMEM] * 5,
         out_specs=VMEM,
-        scratch_shapes=[
-            pltpu.VMEM((2, hidden, width // NC), jnp.bfloat16),
-            pltpu.SemaphoreType.DMA,
-        ],
-        compiler_params=pltpu.CompilerParams(vmem_limit_bytes=50 * 2**20),
+        compiler_params=pltpu.CompilerParams(vmem_limit_bytes=16 * 2**20),
         name="enter",
-    )(state, gain, gate, up, pair)
-
-
-def expert_leave(sums, down, pair):
-    hidden, width = down.shape
-    share = width // (NX * NZ * NC)
+    )(state, gain, gate, up, other)
+
+
+def expert_leave(sums, down, other):
+    share = down.shape[1] // (NX * NZ * NC)
     return pl.pallas_call(
         leave_kernel,
         out_shape=jax.ShapeDtypeStruct((NX, NZ, sums.shape[2], share), jnp.bfloat16),
-        in_specs=[VMEM] * 2 + [ANY],
+        in_specs=[VMEM] * 3,
         out_specs=VMEM,
-        scratch_shapes=[
-            pltpu.VMEM((hidden, width // NC), jnp.bfloat16),
-            pltpu.SemaphoreType.DMA,
-        ],
-        compiler_params=pltpu.CompilerParams(vmem_limit_bytes=50 * 2**20),
+        compiler_params=pltpu.CompilerParams(vmem_limit_bytes=16 * 2**20),
         name="leave",
-    )(sums, down, pair)
+    )(sums, down, other)
 
 
 def body(
@@ -324,7 +315,7 @@
         w_down,
     )
 
-    pair = lax.all_gather(others, "c", axis=0, tiled=False)
+    other = lax.ppermute(others, "c", [(0, 1), (1, 0)])
     arrived = lax.all_to_all(packet, DEV, split_axis=0, concat_axis=0, tiled=True)
     attended = merge(arrived)
     attended = jnp.transpose(attended.reshape(NZ, own_heads, rows, HD), (2, 0, 1, 3))
@@ -350,9 +341,9 @@
     incoming = lax.all_to_all(outgoing, OUTER, split_axis=0, concat_axis=0, tiled=True)
     slab = incoming.reshape(slots, NZ * share)
     over_x = lax.all_gather(slab, "x", axis=0, tiled=False)
-    sums = expert_enter(over_x, norm_gain.reshape(1, width), w_gate.T, w_up.T, pair)
+    sums = expert_enter(over_x, norm_gain.reshape(1, width), w_gate.T, w_up.T, other)
     sums = lax.all_gather(sums, "c", axis=0, tiled=False)
-    cut = expert_leave(sums, w_down, pair)
+    cut = expert_leave(sums, w_down, other)
 
     from_x = lax.all_to_all(cut, "x", split_axis=0, concat_axis=0, tiled=True)
     home = jnp.sum(from_x.astype(f32), axis=0).astype(bf16).reshape(NZ * outer_count, CAP, share)

time: 188 us -> 121 us (0.64)
  Pallas kernels: 60.5 us -> 6.41 us
  between operations: 13.6 us -> 0.21 us
  starting transfers between devices: 23.8 us -> 25.9 us
  waiting for transfers between devices: 26.2 us -> 24.1 us
    pallas_call x1, Pallas kernels: 56.8 us -> 5.05 us  [local_attention(): pl.pallas_call(attend_kernel, out_shape=(jax.ShapeDtypeStruct((NX * NZ *...]
    all_to_all x1, waiting for transfers between devices: 10.7 us -> 8.69 us  [body(): lax.all_to_all(packet, DEV, split_axis=0, concat_axis=0, tiled=True)]
    ppermute x0 -> x1, starting transfers between devices: none -> 2.04 us  [body(): other = lax.ppermute(others, 'c', [(0, 1), (1, 0)])]
  transfers between devices with their start and end apart: 3 -> 3, of which waited for: 2 -> 2; matrix products, arithmetic and copies ran while one was open for 1% -> 2% of each run, Pallas kernels for 0% -> 0%
where the time goes in v4:
time: 121 us
  blocking collectives  58.8 us (49%)
  starting transfers between devices  25.9 us (21%)
  waiting for transfers between devices  24.1 us (20%)
  Pallas kernels  6.41 us (5%)
  local copies, waits for them, and re-layouts  2.85 us (2%)
  other arithmetic  2.33 us (2%)
    all_to_all x1, blocking collectives, body(): lax.all_to_all(outgoing, OUTER, split_axis=0, concat_axis=0, tiled=True)  30.1 us
    all_to_all x1, starting transfers between devices, body(): lax.all_to_all(packet, DEV, split_axis=0, concat_axis=0, tiled=True)  17.5 us
    all_to_all x1, waiting for transfers between devices, body(): lax.all_to_all(home, ('zh',) + OUTER, split_axis=0, concat_axis=0, tiled=...  15.4 us
    all_to_all x1, blocking collectives, body(): from_x = lax.all_to_all(cut, 'x', split_axis=0, concat_axis=0, tiled=True)  13.4 us
    all_gather x1, blocking collectives, body(): over_x = lax.all_gather(slab, 'x', axis=0, tiled=False)  13.2 us
    all_to_all x1, waiting for transfers between devices, body(): lax.all_to_all(packet, DEV, split_axis=0, concat_axis=0, tiled=True)  8.69 us
    all_to_all x1, starting transfers between devices, body(): lax.all_to_all(home, ('zh',) + OUTER, split_axis=0, concat_axis=0, tiled=...  6.31 us
    pallas_call x1, Pallas kernels, local_attention(): pl.pallas_call(attend_kernel, out_shape=(jax.ShapeDtypeStruct((NX * NZ *...  5.05 us
  transfers between devices with their start and end apart: 3, of which 2 were waited for; matrix products, arithmetic and copies ran while one was open for 2% of the time, Pallas kernels for 0%

profile of v4, /device:TPU:2, one launch (start us, length us, event | category | flops | bytes accessed | tf_op | source)
XLA Modules:
  0.0 120.8 jit_solution(5265025766138164741)
XLA Ops:
  0.0 5.0 %attend.1 = (bf16[16,24,256]{2,1,0:T(8,128)(2,1)}, bf16[3,96,3072]{2,1,0:T(8,128)(2,1)}) custom-call(s32[4]{0:T(128)} %length_ref.1, bf16[4,6144]{1,0:T(4,128)(2,1)} %q_ref.1, bf16[256,1024]{1,0:T(8,128)(2,1)} %bitcast.35, bf16[256,1024]{1,0:T(8,128)(2,1)} %bitcast.36, bf16[4,1024]{1,0:T(4,128)(2,1)} %nk_ref.1, bf16[4,1024]{1,0:T(4,128)(2,1)} %nv_ref.1, ...), custom_call_target="tpu_custom_call" | custom-call | tf_op jit(solution)/shard_map/attend/pallas_call | solution.py:218
  5.1 17.5 %all-to-all-start = ((bf16[16,24,256]{2,1,0:T(8,128)(2,1)}), bf16[16,24,256]{2,1,0:T(8,128)(2,1)S(1)}, u32[]{:S(2)}, u32[]{:S(2)}) async-start(bf16[16,24,256]{2,1,0:T(8,128)(2,1)} %get-tuple-element.7), calls=%async_computation | async-start | bytes 393216 | tf_op jit(solution)/shard_map/all_to_all | solution.py:319
  22.6 2.0 %collective-permute-start = (bf16[3,96,3072]{2,1,0:T(8,128)(2,1)}, bf16[3,96,3072]{2,1,0:T(8,128)(2,1)S(1)}, u32[]{:S(2)}, u32[]{:S(2)}) collective-permute-start(bf16[3,96,3072]{2,1,0:T(8,128)(2,1)} %get-tuple-element.8), channel_id=1, source_target_pairs={{0,1},{1,0},{2,3},{3,2},{4,5},{5,4},{6,7},{7,6},{8,9},{9,8},{10,11... | collective-permute-start | bytes 5308424 | tf_op jit(solution)/shard_map/ppermute | solution.py:318
  24.9 0.2 select_reduce_fusion
  25.2 0.1 copy.49
  25.7 8.7 %all-to-all-done = bf16[16,24,256]{2,1,0:T(8,128)(2,1)S(1)} async-done(((bf16[16,24,256]{2,1,0:T(8,128)(2,1)}), bf16[16,24,256]{2,1,0:T(8,128)(2,1)S(1)}, u32[]{:S(2)}, u32[]{:S(2)}) %all-to-all-start) | async-done | bytes 196640 | tf_op jit(solution)/shard_map/all_to_all | solution.py:319
  34.4 0.4 fusion.12
  34.8 0.3 fusion.1
  35.1 0.1 multiply_reduce_fusion
  35.2 0.2 convolution_convert_fusion
  35.5 30.1 %all_to_all.20 = bf16[48,2,768]{2,1,0:T(2,128)(2,1)S(1)} all-to-all(bf16[48,2,768]{2,1,0:T(2,128)(2,1)S(1)} %bitcast.34), channel_id=1, replica_groups=mesh['zl'=6,'y'=8,'x'=4,'zh'=2,'c'=2] {'zl','y'}, dimensions={0} | all-to-all | bytes 294912 | tf_op jit(solution)/shard_map/all_to_all | solution.py:341
  65.7 13.2 %all_gather.9.state_ref = bf16[4,96,768]{2,1,0:T(8,128)(2,1)S(1)} all-gather(bf16[1,96,768]{2,1,0:T(8,128)(2,1)S(1)} %all_gather_reshape.3), channel_id=1, replica_groups=mesh['zl'=6,'y'=8,'x'=4,'zh'=2,'c'=2] {'x'}, dimensions={0}, use_global_device_ids=true | all-gather | bytes 737280 | tf_op jit(solution)/shard_map/all_gather | solution.py:343
  78.9 1.3 %copy-done.1 = bf16[6144,96]{0,1:T(8,128)(2,1)S(1)} copy-done((bf16[6144,96]{0,1:T(8,128)(2,1)S(1)}, bf16[6144,96]{0,1:T(8,128)(2,1)}, u32[]{:S(2)}) %copy-start.1) | copy-done | bytes 1179672
  80.2 0.8 enter.1
  81.0 2.1 %all-gather = f32[8,96,128]{2,1,0:T(8,128)S(1)} all-gather(f32[4,96,128]{2,1,0:T(8,128)S(1)} %enter.1), channel_id=2, replica_groups=mesh['zl'=6,'y'=8,'x'=4,'zh'=2,'c'=2] {'c'}, dimensions={0}, use_global_device_ids=true | all-gather | bytes 589824 | tf_op jit(solution)/shard_map/all_gather | solution.py:345
  83.1 0.6 leave.1
  83.7 13.4 %all_to_all.21 = bf16[4,2,96,384]{3,2,1,0:T(8,128)(2,1)S(1)} all-to-all(bf16[4,2,96,384]{3,2,1,0:T(8,128)(2,1)S(1)} %leave.1), channel_id=1, replica_groups=mesh['zl'=6,'y'=8,'x'=4,'zh'=2,'c'=2] {'x'}, dimensions={0} | all-to-all | bytes 1179648 | tf_op jit(solution)/shard_map/all_to_all | solution.py:348
  97.1 0.7 reshape.118
  97.8 6.3 %all-to-all-start.3 = ((bf16[96,2,384]{2,1,0:T(2,128)(2,1)}), bf16[96,2,384]{2,1,0:T(2,128)(2,1)S(1)}, u32[]{:S(2)}, u32[]{:S(2)}) async-start(bf16[96,2,384]{2,1,0:T(2,128)(2,1)} %reshape.118), calls=%async_computation.3 | async-start | bytes 294912 | tf_op jit(solution)/shard_map/all_to_all | solution.py:350
  104.3 0.1 copy.50
  104.5 15.4 %all-to-all-done.3 = bf16[96,2,384]{2,1,0:T(2,128)(2,1)S(1)} async-done(((bf16[96,2,384]{2,1,0:T(2,128)(2,1)}), bf16[96,2,384]{2,1,0:T(2,128)(2,1)S(1)}, u32[]{:S(2)}, u32[]{:S(2)}) %all-to-all-start.3) | async-done | bytes 147488 | tf_op jit(solution)/shard_map/all_to_all | solution.py:350
  119.9 0.1 convert_reduce_fusion
  120.1 0.1 multiply_reduce_fusion.1
  120.2 0.6 fusion.6
  (41 shorter events, 1.2 us)
Async XLA Ops:
  0.0 24.6 %copy-start.5 = (s32[4,2]{0,1:T(2,128)S(1)}, s32[4,2]{0,1:T(2,128)}, u32[]{:S(2)}) copy-start(s32[4,2]{0,1:T(2,128)} %param.19) | copy-start | bytes 100
  0.0 25.3 %copy-start.4 = (bf16[4,6144]{1,0:T(4,128)(2,1)S(1)}, bf16[4,6144]{1,0:T(4,128)(2,1)}, u32[]{:S(2)}) copy-start(bf16[4,6144]{1,0:T(4,128)(2,1)} %param.21) | copy-start | bytes 147460
  0.0 25.5 %copy-start.3 = (f32[6144]{0:T(1024)S(1)}, f32[6144]{0:T(1024)}, u32[]{:S(2)}) copy-start(f32[6144]{0:T(1024)} %param.22) | copy-start | bytes 73732
  5.1 29.3 %all-to-all-start = ((bf16[16,24,256]{2,1,0:T(8,128)(2,1)}), bf16[16,24,256]{2,1,0:T(8,128)(2,1)S(1)}, u32[]{:S(2)}, u32[]{:S(2)}) async-start(bf16[16,24,256]{2,1,0:T(8,128)(2,1)} %get-tuple-element.7), calls=%async_computation | async-start | bytes 393216 | tf_op jit(solution)/shard_map/all_to_all | solution.py:319
  22.6 56.3 %collective-permute-start = (bf16[3,96,3072]{2,1,0:T(8,128)(2,1)}, bf16[3,96,3072]{2,1,0:T(8,128)(2,1)S(1)}, u32[]{:S(2)}, u32[]{:S(2)}) collective-permute-start(bf16[3,96,3072]{2,1,0:T(8,128)(2,1)} %get-tuple-element.8), channel_id=1, source_target_pairs={{0,1},{1,0},{2,3},{3,2},{4,5},{5,4},{6,7},{7,6},{8,9},{9,8},{10,11... | collective-permute-start | bytes 5308424 | tf_op jit(solution)/shard_map/ppermute | solution.py:318
  34.8 44.1 %copy-start = (bf16[6144,96]{0,1:T(8,128)(2,1)S(1)}, bf16[6144,96]{0,1:T(8,128)(2,1)}, u32[]{:S(2)}) copy-start(bf16[6144,96]{0,1:T(8,128)(2,1)} %param.23) | copy-start | bytes 3538948
  78.9 1.3 %copy-start.1 = (bf16[6144,96]{0,1:T(8,128)(2,1)S(1)}, bf16[6144,96]{0,1:T(8,128)(2,1)}, u32[]{:S(2)}) copy-start(bf16[6144,96]{0,1:T(8,128)(2,1)} %param.24) | copy-start | bytes 3538948
  80.2 2.9 %copy-start.2 = (bf16[96,6144]{1,0:T(8,128)(2,1)S(1)}, bf16[96,6144]{1,0:T(8,128)(2,1)}, u32[]{:S(2)}) copy-start(bf16[96,6144]{1,0:T(8,128)(2,1)} %down_ref.3) | copy-start | bytes 3538948
  83.6 20.5 %copy-start.6 = (f32[4,2]{0,1:T(2,128)S(1)}, f32[4,2]{0,1:T(2,128)}, u32[]{:S(2)}) copy-start(f32[4,2]{0,1:T(2,128)} %param.20) | copy-start | bytes 100
  97.8 22.1 %all-to-all-start.3 = ((bf16[96,2,384]{2,1,0:T(2,128)(2,1)}), bf16[96,2,384]{2,1,0:T(2,128)(2,1)S(1)}, u32[]{:S(2)}, u32[]{:S(2)}) async-start(bf16[96,2,384]{2,1,0:T(2,128)(2,1)} %reshape.118), calls=%async_computation.3 | async-start | bytes 294912 | tf_op jit(solution)/shard_map/all_to_all | solution.py:350

commit v5 on v4

--- a/solution.py
+++ b/solution.py
@@ -28,17 +28,24 @@
     return [pl.multiple_of((i * NC + core) * share, share) for i in range(NX * NZ)]
 
 
-def pack_copies(refs, stage, sems):
-    share = refs[0].shape[1] // (NX * NZ * NC)
-    return [
+def pack_kernel(gate_ref, up_ref, down_ref, own_ref, out_ref, sems):
+    share = gate_ref.shape[1] // (NX * NZ * NC)
+    at_c = lax.axis_index("c")
+    refs = (gate_ref, up_ref, down_ref)
+    copies = [
         pltpu.make_async_copy(
-            ref.at[:, pl.ds(start, share)],
-            stage.at[kind, :, pl.ds(i * share, share)],
-            sems.at[kind, i],
+            refs[kind].at[:, pl.ds(start, share)],
+            to.at[kind, :, pl.ds(i * share, share)],
+            sems.at[side, kind, i],
         )
-        for kind, ref in enumerate(refs)
-        for i, start in enumerate(starts_of(1 - lax.axis_index("c"), share))
+        for side, (to, core) in enumerate(((out_ref, 1 - at_c), (own_ref, at_c)))
+        for kind in range(to.shape[0])
+        for i, start in enumerate(starts_of(core, share))
     ]
+    for copy in copies:
+        copy.start()
+    for copy in copies:
+        copy.wait()
 
 
 def attend_kernel(
@@ -48,22 +55,12 @@
     v_ref,
     nk_ref,
     nv_ref,
-    gate_ref,
-    up_ref,
-    down_ref,
     out_ref,
-    other_ref,
     q_rows,
     nk_rows,
     nv_rows,
     packed,
-    stage,
-    sems,
-    out_sem,
 ):
-    copies = pack_copies((gate_ref, up_ref, down_ref), stage, sems)
-    for copy in copies:
-        copy.start()
     f32, bf16 = jnp.float32, jnp.bfloat16
     tokens = q_ref.shape[0]
     span = k_ref.shape[0] // tokens
@@ -104,10 +101,6 @@
         ],
         axis=0,
     )
-    for copy in copies:
-        copy.wait()
-    leave = pltpu.make_async_copy(stage, other_ref, out_sem)
-    leave.start()
     scores = jnp.where(live, scores * scale, DEAD)
     own = jnp.sum(q * nk_rows[...], axis=1, keepdims=True) * scale
     own = jnp.where(first, own, DEAD)
@@ -149,45 +142,32 @@
             block = packed[x * NC + c].astype(bf16)
             for z in range(NZ):
                 out_ref[(x * NZ + z) * NC + c] = block
-    leave.wait()
-
-
-def enter_kernel(state_ref, gain_ref, gate_ref, up_ref, other, out_ref):
+
+
+def enter_kernel(state_ref, gain_ref, own, other, out_ref):
     f32 = jnp.float32
     rows, span = state_ref.shape[1:]
     share = span // NZ
-    hidden = gate_ref.shape[0]
-    at_c = lax.axis_index("c")
-    starts = starts_of(at_c, share)
-
-    def columns(ref, x):
-        return jnp.concatenate(
-            [ref[:, pl.ds(s, share)] for s in starts[x * NZ : (x + 1) * NZ]], axis=1
-        )
-
+    hidden = own.shape[1]
+    starts = starts_of(lax.axis_index("c"), share)
     squares = jnp.zeros((rows, HD), f32)
-    own = [jnp.zeros((rows, hidden), f32)] * 2
+    sums = [jnp.zeros((rows, hidden), f32)] * (2 * NC)
     for x in range(NX):
         block = state_ref[x]
-        for kind, ref in enumerate((gate_ref, up_ref)):
-            own[kind] += lax.dot_general(block, columns(ref, x), NT, preferred_element_type=f32)
-        state = block.astype(f32) / columns(gain_ref, x)
+        for kind in range(2):
+            for far, ref in enumerate((own, other)):
+                sums[kind * NC + far] += lax.dot_general(
+                    block, ref[kind, :, x * span : (x + 1) * span], NT, preferred_element_type=f32
+                )
+        gain = [gain_ref[:, pl.ds(s, share)] for s in starts[x * NZ : (x + 1) * NZ]]
+        state = block.astype(f32) / jnp.concatenate(gain, axis=1)
         state = state * state
         for at in range(0, span, HD):
             squares += state[:, at : at + HD]
     total = jnp.sum(squares, axis=1, keepdims=True)
     total = jnp.broadcast_to(total, (rows, HD - hidden))
-    for kind in range(2):
-        far = jnp.zeros((rows, hidden), f32)
-        for x in range(NX):
-            far += lax.dot_general(
-                state_ref[x],
-                other[kind, :, x * span : (x + 1) * span],
-                NT,
-                preferred_element_type=f32,
-            )
-        out_ref[kind * NC] = jnp.concatenate([own[kind], total], axis=1)
-        out_ref[kind * NC + 1] = jnp.concatenate([far, total], axis=1)
+    for i in range(2 * NC):
+        out_ref[i] = jnp.concatenate([sums[i], total], axis=1)
 
 
 def leave_kernel(sums_ref, down_ref, other, out_ref):
@@ -211,25 +191,16 @@
         out_ref[i // NZ, i % NZ] = (near + far).astype(bf16)
 
 
-def local_attention(lengths, queries, key_cache, value_cache, new_key, new_value, gate, up, down):
+def local_attention(lengths, queries, key_cache, value_cache, new_key, new_value):
     rows, span, features = key_cache.shape
     slab_rows = HEADS // (NX * NC) * rows
-    hidden, width = down.shape
     return pl.pallas_call(
         attend_kernel,
-        out_shape=(
-            jax.ShapeDtypeStruct((NX * NZ * NC, slab_rows, 2 * HD), jnp.bfloat16),
-            jax.ShapeDtypeStruct((3, hidden, width // NC), jnp.bfloat16),
-        ),
-        in_specs=[pl.BlockSpec(memory_space=pltpu.SMEM)] + [pl.BlockSpec()] * 5 + [ANY] * 3,
-        out_specs=(VMEM, ANY),
+        out_shape=jax.ShapeDtypeStruct((NX * NZ * NC, slab_rows, 2 * HD), jnp.bfloat16),
+        in_specs=[pl.BlockSpec(memory_space=pltpu.SMEM)] + [pl.BlockSpec()] * 5,
+        out_specs=VMEM,
         scratch_shapes=[pltpu.VMEM((HEADS * rows, HD), jnp.float32)] * 3
-        + [
-            pltpu.VMEM((NX * NC, slab_rows, 2 * HD), jnp.float32),
-            pltpu.VMEM((3, hidden, width // NC), jnp.bfloat16),
-            pltpu.SemaphoreType.DMA((3, NX * NZ)),
-            pltpu.SemaphoreType.DMA,
-        ],
+        + [pltpu.VMEM((NX * NC, slab_rows, 2 * HD), jnp.float32)],
         compiler_params=pltpu.CompilerParams(vmem_limit_bytes=60 * 2**20),
         name="attend",
     )(
@@ -239,9 +210,6 @@
         value_cache.reshape(rows * span, features),
         new_key,
         new_value,
-        gate,
-        up,
-        down,
     )
 
 
@@ -255,15 +223,30 @@
     return jnp.sum((factor / whole)[..., None] * part, axis=0)
 
 
-def expert_enter(state, gain, gate, up, other):
+def pack_weights(gate, up, down):
+    hidden, width = down.shape
+    return pl.pallas_call(
+        pack_kernel,
+        out_shape=tuple(
+            jax.ShapeDtypeStruct((kinds, hidden, width // NC), jnp.bfloat16) for kinds in (2, 3)
+        ),
+        in_specs=[ANY] * 3,
+        out_specs=(VMEM, VMEM),
+        scratch_shapes=[pltpu.SemaphoreType.DMA((2, 3, NX * NZ))],
+        compiler_params=pltpu.CompilerParams(vmem_limit_bytes=60 * 2**20),
+        name="pack",
+    )(gate, up, down)
+
+
+def expert_enter(state, gain, own, other):
     return pl.pallas_call(
         enter_kernel,
         out_shape=jax.ShapeDtypeStruct((2 * NC, state.shape[1], HD), jnp.float32),
-        in_specs=[VMEM] * 5,
+        in_specs=[VMEM] * 4,
         out_specs=VMEM,
         compiler_params=pltpu.CompilerParams(vmem_limit_bytes=16 * 2**20),
         name="enter",
-    )(state, gain, gate, up, other)
+    )(state, gain, own, other)
 
 
 def expert_leave(sums, down, other):
@@ -303,19 +286,10 @@
     own_heads = HEADS // dev_count
     slots = outer_count * CAP
 
-    packet, others = local_attention(
-        lengths,
-        queries,
-        key_cache,
-        value_cache,
-        new_key,
-        new_value,
-        w_gate.T,
-        w_up.T,
-        w_down,
-    )
-
-    other = lax.ppermute(others, "c", [(0, 1), (1, 0)])
+    packet = local_attention(lengths, queries, key_cache, value_cache, new_key, new_value)
+
+    own, sent = pack_weights(w_gate.T, w_up.T, w_down)
+    other = lax.ppermute(sent, "c", [(0, 1), (1, 0)])
     arrived = lax.all_to_all(packet, DEV, split_axis=0, concat_axis=0, tiled=True)
     attended = merge(arrived)
     attended = jnp.transpose(attended.reshape(NZ, own_heads, rows, HD), (2, 0, 1, 3))
@@ -341,7 +315,7 @@
     incoming = lax.all_to_all(outgoing, OUTER, split_axis=0, concat_axis=0, tiled=True)
     slab = incoming.reshape(slots, NZ * share)
     over_x = lax.all_gather(slab, "x", axis=0, tiled=False)
-    sums = expert_enter(over_x, norm_gain.reshape(1, width), w_gate.T, w_up.T, other)
+    sums = expert_enter(over_x, norm_gain.reshape(1, width), own, other)
     sums = lax.all_gather(sums, "c", axis=0, tiled=False)
     cut = expert_leave(sums, w_down, other)
 

time: 121 us -> 117 us (0.967)
  waiting for transfers between devices: 24.1 us -> 20.1 us
  Pallas kernels: 6.41 us -> 7.83 us
  local copies, waits for them, and re-layouts: 2.85 us -> 1.59 us
    all_to_all x1, waiting for transfers between devices: 8.69 us -> 4.67 us  [body(): lax.all_to_all(packet, DEV, split_axis=0, concat_axis=0, tiled=True)]
    pallas_call x1 -> x2, Pallas kernels: 5.05 us -> 6.47 us  [the longest x1 3.97 us: pack_weights(): pl.pallas_call(pack_kernel, out_shape=tuple((jax.ShapeDtypeStruct((kinds,...]
    unnamed x17 -> x15, local copies, waits for them, and re-layouts: 1.4 us -> 0.14 us
  transfers between devices with their start and end apart: 3 -> 3, of which waited for: 2 -> 2; matrix products, arithmetic and copies ran while one was open for 2% -> 2% of each run, Pallas kernels for 0% -> 3%
where the time goes in v5:
time: 117 us
  blocking collectives  58.8 us (50%)
  starting transfers between devices  25.9 us (22%)
  waiting for transfers between devices  20.1 us (17%)
  Pallas kernels  7.83 us (7%)
  other arithmetic  2.33 us (2%)
  local copies, waits for them, and re-layouts  1.59 us (1%)
    all_to_all x1, blocking collectives, body(): lax.all_to_all(outgoing, OUTER, split_axis=0, concat_axis=0, tiled=True)  30.1 us
    all_to_all x1, starting transfers between devices, body(): lax.all_to_all(packet, DEV, split_axis=0, concat_axis=0, tiled=True)  17.5 us
    all_to_all x1, waiting for transfers between devices, body(): lax.all_to_all(home, ('zh',) + OUTER, split_axis=0, concat_axis=0, tiled=...  15.4 us
    all_to_all x1, blocking collectives, body(): from_x = lax.all_to_all(cut, 'x', split_axis=0, concat_axis=0, tiled=True)  13.4 us
    all_gather x1, blocking collectives, body(): over_x = lax.all_gather(slab, 'x', axis=0, tiled=False)  13.2 us
    all_to_all x1, starting transfers between devices, body(): lax.all_to_all(home, ('zh',) + OUTER, split_axis=0, concat_axis=0, tiled=...  6.31 us
    all_to_all x1, waiting for transfers between devices, body(): lax.all_to_all(packet, DEV, split_axis=0, concat_axis=0, tiled=True)  4.67 us
    pallas_call x1, Pallas kernels, pack_weights(): pl.pallas_call(pack_kernel, out_shape=tuple((jax.ShapeDtypeStruct((kinds,...  3.97 us
  transfers between devices with their start and end apart: 3, of which 2 were waited for; matrix products, arithmetic and copies ran while one was open for 2% of the time, Pallas kernels for 3%

profile of v5, /device:TPU:2, one launch (start us, length us, event | category | flops | bytes accessed | tf_op | source)
XLA Modules:
  0.0 116.9 jit_solution(17896985240114892344)
XLA Ops:
  0.0 2.5 %attend.1 = bf16[16,24,256]{2,1,0:T(8,128)(2,1)} custom-call(s32[4]{0:T(128)} %length_ref.1, bf16[4,6144]{1,0:T(4,128)(2,1)} %q_ref.1, bf16[256,1024]{1,0:T(8,128)(2,1)} %bitcast.33, bf16[256,1024]{1,0:T(8,128)(2,1)} %bitcast.34, bf16[4,1024]{1,0:T(4,128)(2,1)} %nk_ref.1, bf16[4,1024]{1,0:T(4,128)(2,1)} %nv_ref.1), custom_call_target="tpu_custom_call" | custom-call | tf_op jit(solution)/shard_map/attend/pallas_call | solution.py:197
  2.5 17.5 %all-to-all-start = ((bf16[16,24,256]{2,1,0:T(8,128)(2,1)}), bf16[16,24,256]{2,1,0:T(8,128)(2,1)S(1)}, u32[]{:S(2)}, u32[]{:S(2)}) async-start(bf16[16,24,256]{2,1,0:T(8,128)(2,1)} %attend.1), calls=%async_computation | async-start | bytes 393216 | tf_op jit(solution)/shard_map/all_to_all | solution.py:293
  20.0 4.0 %pack.1 = (bf16[2,96,3072]{2,1,0:T(8,128)(2,1)}, bf16[3,96,3072]{2,1,0:T(8,128)(2,1)}) custom-call(bf16[96,6144]{1,0:T(8,128)(2,1)} %bitcast.29, bf16[96,6144]{1,0:T(8,128)(2,1)} %bitcast.30, bf16[96,6144]{1,0:T(8,128)(2,1)} %down_ref.3), custom_call_target="tpu_custom_call" | custom-call | tf_op jit(solution)/shard_map/pack/pallas_call | solution.py:228
  24.0 2.1 %collective-permute-start = (bf16[3,96,3072]{2,1,0:T(8,128)(2,1)}, bf16[3,96,3072]{2,1,0:T(8,128)(2,1)S(1)}, u32[]{:S(2)}, u32[]{:S(2)}) collective-permute-start(bf16[3,96,3072]{2,1,0:T(8,128)(2,1)} %get-tuple-element.8), channel_id=1, source_target_pairs={{0,1},{1,0},{2,3},{3,2},{4,5},{5,4},{6,7},{7,6},{8,9},{9,8},{10,11... | collective-permute-start | bytes 5308424 | tf_op jit(solution)/shard_map/ppermute | solution.py:292
  26.4 0.2 select_reduce_fusion
  26.7 0.1 copy.49
  27.1 4.7 %all-to-all-done = bf16[16,24,256]{2,1,0:T(8,128)(2,1)S(1)} async-done(((bf16[16,24,256]{2,1,0:T(8,128)(2,1)}), bf16[16,24,256]{2,1,0:T(8,128)(2,1)S(1)}, u32[]{:S(2)}, u32[]{:S(2)}) %all-to-all-start) | async-done | bytes 196640 | tf_op jit(solution)/shard_map/all_to_all | solution.py:293
  31.8 0.4 fusion.12
  32.3 0.3 fusion.1
  32.5 0.1 multiply_reduce_fusion
  32.6 0.2 convolution_convert_fusion
  32.9 30.1 %all_to_all.20 = bf16[48,2,768]{2,1,0:T(2,128)(2,1)S(1)} all-to-all(bf16[48,2,768]{2,1,0:T(2,128)(2,1)S(1)} %bitcast.32), channel_id=1, replica_groups=mesh['zl'=6,'y'=8,'x'=4,'zh'=2,'c'=2] {'zl','y'}, dimensions={0} | all-to-all | bytes 294912 | tf_op jit(solution)/shard_map/all_to_all | solution.py:315
  63.1 13.2 %all_gather.9.state_ref = bf16[4,96,768]{2,1,0:T(8,128)(2,1)S(1)} all-gather(bf16[1,96,768]{2,1,0:T(8,128)(2,1)S(1)} %all_gather_reshape.3), channel_id=1, replica_groups=mesh['zl'=6,'y'=8,'x'=4,'zh'=2,'c'=2] {'x'}, dimensions={0}, use_global_device_ids=true | all-gather | bytes 737280 | tf_op jit(solution)/shard_map/all_gather | solution.py:317
  76.3 0.8 enter.1
  77.1 2.1 %all-gather = f32[8,96,128]{2,1,0:T(8,128)S(1)} all-gather(f32[4,96,128]{2,1,0:T(8,128)S(1)} %enter.1), channel_id=2, replica_groups=mesh['zl'=6,'y'=8,'x'=4,'zh'=2,'c'=2] {'c'}, dimensions={0}, use_global_device_ids=true | all-gather | bytes 589824 | tf_op jit(solution)/shard_map/all_gather | solution.py:319
  79.2 0.6 leave.1
  79.8 13.4 %all_to_all.21 = bf16[4,2,96,384]{3,2,1,0:T(8,128)(2,1)S(1)} all-to-all(bf16[4,2,96,384]{3,2,1,0:T(8,128)(2,1)S(1)} %leave.1), channel_id=1, replica_groups=mesh['zl'=6,'y'=8,'x'=4,'zh'=2,'c'=2] {'x'}, dimensions={0} | all-to-all | bytes 1179648 | tf_op jit(solution)/shard_map/all_to_all | solution.py:322
  93.3 0.7 reshape.118
  94.0 6.3 %all-to-all-start.3 = ((bf16[96,2,384]{2,1,0:T(2,128)(2,1)}), bf16[96,2,384]{2,1,0:T(2,128)(2,1)S(1)}, u32[]{:S(2)}, u32[]{:S(2)}) async-start(bf16[96,2,384]{2,1,0:T(2,128)(2,1)} %reshape.118), calls=%async_computation.3 | async-start | bytes 294912 | tf_op jit(solution)/shard_map/all_to_all | solution.py:324
  100.4 0.1 copy.50
  100.6 15.4 %all-to-all-done.3 = bf16[96,2,384]{2,1,0:T(2,128)(2,1)S(1)} async-done(((bf16[96,2,384]{2,1,0:T(2,128)(2,1)}), bf16[96,2,384]{2,1,0:T(2,128)(2,1)S(1)}, u32[]{:S(2)}, u32[]{:S(2)}) %all-to-all-start.3) | async-done | bytes 147488 | tf_op jit(solution)/shard_map/all_to_all | solution.py:324
  116.0 0.1 convert_reduce_fusion
  116.2 0.1 multiply_reduce_fusion.1
  116.3 0.6 fusion.6
  (40 shorter events, 1.2 us)
Async XLA Ops:
  2.5 29.3 %all-to-all-start = ((bf16[16,24,256]{2,1,0:T(8,128)(2,1)}), bf16[16,24,256]{2,1,0:T(8,128)(2,1)S(1)}, u32[]{:S(2)}, u32[]{:S(2)}) async-start(bf16[16,24,256]{2,1,0:T(8,128)(2,1)} %attend.1), calls=%async_computation | async-start | bytes 393216 | tf_op jit(solution)/shard_map/all_to_all | solution.py:293
  20.0 6.1 %copy-start.4 = (s32[4,2]{0,1:T(2,128)S(1)}, s32[4,2]{0,1:T(2,128)}, u32[]{:S(2)}) copy-start(s32[4,2]{0,1:T(2,128)} %param.19) | copy-start | bytes 100
  20.0 6.7 %copy-start.3 = (bf16[4,6144]{1,0:T(4,128)(2,1)S(1)}, bf16[4,6144]{1,0:T(4,128)(2,1)}, u32[]{:S(2)}) copy-start(bf16[4,6144]{1,0:T(4,128)(2,1)} %param.21) | copy-start | bytes 147460
  20.0 6.9 %copy-start.2 = (f32[6144]{0:T(1024)S(1)}, f32[6144]{0:T(1024)}, u32[]{:S(2)}) copy-start(f32[6144]{0:T(1024)} %param.22) | copy-start | bytes 73732
  24.0 52.3 %collective-permute-start = (bf16[3,96,3072]{2,1,0:T(8,128)(2,1)}, bf16[3,96,3072]{2,1,0:T(8,128)(2,1)S(1)}, u32[]{:S(2)}, u32[]{:S(2)}) collective-permute-start(bf16[3,96,3072]{2,1,0:T(8,128)(2,1)} %get-tuple-element.8), channel_id=1, source_target_pairs={{0,1},{1,0},{2,3},{3,2},{4,5},{5,4},{6,7},{7,6},{8,9},{9,8},{10,11... | collective-permute-start | bytes 5308424 | tf_op jit(solution)/shard_map/ppermute | solution.py:292
  32.2 44.1 %copy-start.1 = (bf16[2,96,3072]{2,1,0:T(8,128)(2,1)S(1)}, bf16[2,96,3072]{2,1,0:T(8,128)(2,1)}, u32[]{:S(2)}) copy-start(bf16[2,96,3072]{2,1,0:T(8,128)(2,1)} %get-tuple-element.7.own) | copy-start | bytes 3538948
  76.3 2.9 %copy-start = (bf16[96,6144]{1,0:T(8,128)(2,1)S(1)}, bf16[96,6144]{1,0:T(8,128)(2,1)}, u32[]{:S(2)}) copy-start(bf16[96,6144]{1,0:T(8,128)(2,1)} %down_ref.3) | copy-start | bytes 3538948
  79.8 20.5 %copy-start.5 = (f32[4,2]{0,1:T(2,128)S(1)}, f32[4,2]{0,1:T(2,128)}, u32[]{:S(2)}) copy-start(f32[4,2]{0,1:T(2,128)} %param.20) | copy-start | bytes 100
  94.0 22.0 %all-to-all-start.3 = ((bf16[96,2,384]{2,1,0:T(2,128)(2,1)}), bf16[96,2,384]{2,1,0:T(2,128)(2,1)S(1)}, u32[]{:S(2)}, u32[]{:S(2)}) async-start(bf16[96,2,384]{2,1,0:T(2,128)(2,1)} %reshape.118), calls=%async_computation.3 | async-start | bytes 294912 | tf_op jit(solution)/shard_map/all_to_all | solution.py:324

commit v6 on v5

--- a/solution.py
+++ b/solution.py
@@ -28,24 +28,34 @@
     return [pl.multiple_of((i * NC + core) * share, share) for i in range(NX * NZ)]
 
 
-def pack_kernel(gate_ref, up_ref, down_ref, own_ref, out_ref, sems):
+def pack_kernel(gate_ref, up_ref, down_ref, own_ref, out_ref, stage, in_sems, out_sems):
     share = gate_ref.shape[1] // (NX * NZ * NC)
     at_c = lax.axis_index("c")
     refs = (gate_ref, up_ref, down_ref)
-    copies = [
-        pltpu.make_async_copy(
-            refs[kind].at[:, pl.ds(start, share)],
-            to.at[kind, :, pl.ds(i * share, share)],
-            sems.at[side, kind, i],
-        )
-        for side, (to, core) in enumerate(((out_ref, 1 - at_c), (own_ref, at_c)))
-        for kind in range(to.shape[0])
-        for i, start in enumerate(starts_of(core, share))
-    ]
-    for copy in copies:
-        copy.start()
-    for copy in copies:
-        copy.wait()
+    groups = []
+    for to, core in ((out_ref, 1 - at_c), (own_ref, at_c)):
+        for kind in range(to.shape[0]):
+            slot = len(groups)
+            copies = [
+                pltpu.make_async_copy(
+                    refs[kind].at[:, pl.ds(start, share)],
+                    stage.at[slot, :, pl.ds(i * share, share)],
+                    in_sems.at[slot, i],
+                )
+                for i, start in enumerate(starts_of(core, share))
+            ]
+            groups.append(
+                (copies, pltpu.make_async_copy(stage.at[slot], to.at[kind], out_sems.at[slot]))
+            )
+    for copies, _ in groups:
+        for copy in copies:
+            copy.start()
+    for copies, leave in groups:
+        for copy in copies:
+            copy.wait()
+        leave.start()
+    for _, leave in groups:
+        leave.wait()
 
 
 def attend_kernel(
@@ -128,7 +138,11 @@
     stats = jnp.where(
         lane == 0,
         top_high,
-        jnp.where(lane == 1, top_low, jnp.where(lane == 2, total_high, total_low)),
+        jnp.where(
+            lane == 1,
+            top_low,
+            jnp.where(lane == 2, total_high, jnp.where(lane == 3, total_low, 0.0)),
+        ),
     )
     for x in range(NX):
         for z in range(NZ):
@@ -137,9 +151,15 @@
                 at = ((x * NZ + z) * NC + c) * half
                 packed[x * NC + c, to, :HD] = acc[at : at + half]
                 packed[x * NC + c, to, HD:] = stats[at : at + half]
+    one_hot = lax.broadcasted_iota(jnp.int32, (lines, HD), 0) == lane[:lines]
+    one_hot = one_hot.astype(f32).astype(bf16)
     for x in range(NX):
         for c in range(NC):
             block = packed[x * NC + c].astype(bf16)
+            turned = lax.dot_general(
+                block[:, HD:], one_hot, (((0,), (0,)), ((), ())), preferred_element_type=f32
+            )
+            block = jnp.concatenate([packed[x * NC + c, :, :HD], turned[:8]], axis=0).astype(bf16)
             for z in range(NZ):
                 out_ref[(x * NZ + z) * NC + c] = block
 
@@ -196,7 +216,7 @@
     slab_rows = HEADS // (NX * NC) * rows
     return pl.pallas_call(
         attend_kernel,
-        out_shape=jax.ShapeDtypeStruct((NX * NZ * NC, slab_rows, 2 * HD), jnp.bfloat16),
+        out_shape=jax.ShapeDtypeStruct((NX * NZ * NC, slab_rows + 8, HD), jnp.bfloat16),
         in_specs=[pl.BlockSpec(memory_space=pltpu.SMEM)] + [pl.BlockSpec()] * 5,
         out_specs=VMEM,
         scratch_shapes=[pltpu.VMEM((HEADS * rows, HD), jnp.float32)] * 3
@@ -215,11 +235,12 @@
 
 def merge(arrived):
     f32 = jnp.float32
-    part = arrived[:, :, :HD].astype(f32)
-    info = arrived[:, :, HD : HD + 4].astype(f32)
-    base_of = info[:, :, 0] + info[:, :, 1]
+    lines = arrived.shape[1] - 8
+    part = arrived[:, :lines].astype(f32)
+    info = arrived[:, lines : lines + 4, :lines].astype(f32)
+    base_of = info[:, 0] + info[:, 1]
     factor = jnp.exp(base_of - jnp.max(base_of, axis=0, keepdims=True))
-    whole = jnp.sum(factor * (info[:, :, 2] + info[:, :, 3]), axis=0)
+    whole = jnp.sum(factor * (info[:, 2] + info[:, 3]), axis=0)
     return jnp.sum((factor / whole)[..., None] * part, axis=0)
 
 
@@ -231,8 +252,12 @@
             jax.ShapeDtypeStruct((kinds, hidden, width // NC), jnp.bfloat16) for kinds in (2, 3)
         ),
         in_specs=[ANY] * 3,
-        out_specs=(VMEM, VMEM),
-        scratch_shapes=[pltpu.SemaphoreType.DMA((2, 3, NX * NZ))],
+        out_specs=(ANY, ANY),
+        scratch_shapes=[
+            pltpu.VMEM((5, hidden, width // NC), jnp.bfloat16),
+            pltpu.SemaphoreType.DMA((5, NX * NZ)),
+            pltpu.SemaphoreType.DMA((5,)),
+        ],
         compiler_params=pltpu.CompilerParams(vmem_limit_bytes=60 * 2**20),
         name="pack",
     )(gate, up, down)

time: 117 us -> 115 us (0.983)
  blocking collectives: 58.8 us -> 57.2 us
    all_to_all x1, blocking collectives: 30.1 us -> 28.7 us  [body(): lax.all_to_all(outgoing, OUTER, split_axis=0, concat_axis=0, tiled=True)]
where the time goes in v6:
time: 115 us; the launch traced here: 114 us
  blocking collectives  57.2 us (50%)
  starting transfers between devices  26 us (23%)
  waiting for transfers between devices  20.2 us (18%)
  Pallas kernels  7.12 us (6%)
  other arithmetic  1.71 us (1%)
  local copies, waits for them, and re-layouts  1.59 us (1%)
    all_to_all x1, blocking collectives, body(): lax.all_to_all(outgoing, OUTER, split_axis=0, concat_axis=0, tiled=True)  28.7 us
    all_to_all x1, starting transfers between devices, body(): lax.all_to_all(packet, DEV, split_axis=0, concat_axis=0, tiled=True)  17.5 us
    all_to_all x1, waiting for transfers between devices, body(): lax.all_to_all(home, ('zh',) + OUTER, split_axis=0, concat_axis=0, tiled=...  15.4 us
    all_to_all x1, blocking collectives, body(): from_x = lax.all_to_all(cut, 'x', split_axis=0, concat_axis=0, tiled=True)  13.5 us
    all_gather x1, blocking collectives, body(): over_x = lax.all_gather(slab, 'x', axis=0, tiled=False)  12.9 us
    all_to_all x1, starting transfers between devices, body(): lax.all_to_all(home, ('zh',) + OUTER, split_axis=0, concat_axis=0, tiled=...  6.31 us
    all_to_all x1, waiting for transfers between devices, body(): lax.all_to_all(packet, DEV, split_axis=0, concat_axis=0, tiled=True)  4.86 us
    pallas_call x1, Pallas kernels, pack_weights(): pl.pallas_call(pack_kernel, out_shape=tuple((jax.ShapeDtypeStruct((kinds,...  3.18 us
  transfers between devices with their start and end apart: 3, of which 2 were waited for; matrix products, arithmetic and copies ran while one was open for 2% of the time, Pallas kernels for 3%

profile of v6, /device:TPU:2, one launch (start us, length us, event | category | flops | bytes accessed | tf_op | source)
XLA Modules:
  0.0 114.3 jit_solution(1158115820423003038)
XLA Ops:
  0.0 2.6 %attend.1 = bf16[16,32,128]{2,1,0:T(8,128)(2,1)} custom-call(s32[4]{0:T(128)} %length_ref.1, bf16[4,6144]{1,0:T(4,128)(2,1)} %q_ref.1, bf16[256,1024]{1,0:T(8,128)(2,1)} %bitcast.44, bf16[256,1024]{1,0:T(8,128)(2,1)} %bitcast.45, bf16[4,1024]{1,0:T(4,128)(2,1)} %nk_ref.1, bf16[4,1024]{1,0:T(4,128)(2,1)} %nv_ref.1), custom_call_target="tpu_custom_call" | custom-call | tf_op jit(solution)/shard_map/attend/pallas_call | solution.py:217
  2.6 17.5 %all-to-all-start = ((bf16[16,32,128]{2,1,0:T(8,128)(2,1)}), bf16[16,32,128]{2,1,0:T(8,128)(2,1)S(1)}, u32[]{:S(2)}, u32[]{:S(2)}) async-start(bf16[16,32,128]{2,1,0:T(8,128)(2,1)} %attend.1), calls=%async_computation | async-start | bytes 262144 | tf_op jit(solution)/shard_map/all_to_all | solution.py:318
  20.1 3.2 %pack.1 = (bf16[2,96,3072]{2,1,0:T(8,128)(2,1)}, bf16[3,96,3072]{2,1,0:T(8,128)(2,1)}) custom-call(bf16[96,6144]{1,0:T(8,128)(2,1)} %bitcast.40, bf16[96,6144]{1,0:T(8,128)(2,1)} %bitcast.41, bf16[96,6144]{1,0:T(8,128)(2,1)} %down_ref.3), custom_call_target="tpu_custom_call" | custom-call | tf_op jit(solution)/shard_map/pack/pallas_call | solution.py:249
  23.3 2.2 %collective-permute-start = (bf16[3,96,3072]{2,1,0:T(8,128)(2,1)}, bf16[3,96,3072]{2,1,0:T(8,128)(2,1)S(1)}, u32[]{:S(2)}, u32[]{:S(2)}) collective-permute-start(bf16[3,96,3072]{2,1,0:T(8,128)(2,1)} %get-tuple-element.8), channel_id=1, source_target_pairs={{0,1},{1,0},{2,3},{3,2},{4,5},{5,4},{6,7},{7,6},{8,9},{9,8},{10,11... | collective-permute-start | bytes 5308424 | tf_op jit(solution)/shard_map/ppermute | solution.py:317
  25.6 0.1 copy.58
  25.8 0.2 select_reduce_fusion
  26.1 0.1 copy.59
  26.6 4.9 %all-to-all-done = bf16[16,32,128]{2,1,0:T(8,128)(2,1)S(1)} async-done(((bf16[16,32,128]{2,1,0:T(8,128)(2,1)}), bf16[16,32,128]{2,1,0:T(8,128)(2,1)S(1)}, u32[]{:S(2)}, u32[]{:S(2)}) %all-to-all-start) | async-done | bytes 131104 | tf_op jit(solution)/shard_map/all_to_all | solution.py:318
  31.5 0.1 multiply_reduce_fusion
  31.7 0.2 convolution_convert_fusion
  32.0 28.7 %all_to_all.20 = bf16[48,2,768]{2,1,0:T(2,128)(2,1)S(1)} all-to-all(bf16[48,2,768]{2,1,0:T(2,128)(2,1)S(1)} %bitcast.43), channel_id=1, replica_groups=mesh['zl'=6,'y'=8,'x'=4,'zh'=2,'c'=2] {'zl','y'}, dimensions={0} | all-to-all | bytes 294912 | tf_op jit(solution)/shard_map/all_to_all | solution.py:340
  60.7 12.9 %all_gather.9.state_ref = bf16[4,96,768]{2,1,0:T(8,128)(2,1)S(1)} all-gather(bf16[1,96,768]{2,1,0:T(8,128)(2,1)S(1)} %all_gather_reshape.3), channel_id=1, replica_groups=mesh['zl'=6,'y'=8,'x'=4,'zh'=2,'c'=2] {'x'}, dimensions={0}, use_global_device_ids=true | all-gather | bytes 737280 | tf_op jit(solution)/shard_map/all_gather | solution.py:342
  73.7 0.8 enter.1
  74.5 2.1 %all-gather = f32[8,96,128]{2,1,0:T(8,128)S(1)} all-gather(f32[4,96,128]{2,1,0:T(8,128)S(1)} %enter.1), channel_id=2, replica_groups=mesh['zl'=6,'y'=8,'x'=4,'zh'=2,'c'=2] {'c'}, dimensions={0}, use_global_device_ids=true | all-gather | bytes 589824 | tf_op jit(solution)/shard_map/all_gather | solution.py:344
  76.5 0.6 leave.1
  77.1 13.5 %all_to_all.21 = bf16[4,2,96,384]{3,2,1,0:T(8,128)(2,1)S(1)} all-to-all(bf16[4,2,96,384]{3,2,1,0:T(8,128)(2,1)S(1)} %leave.1), channel_id=1, replica_groups=mesh['zl'=6,'y'=8,'x'=4,'zh'=2,'c'=2] {'x'}, dimensions={0} | all-to-all | bytes 1179648 | tf_op jit(solution)/shard_map/all_to_all | solution.py:347
  90.6 0.1 reduce_sum.80
  90.7 0.7 reshape.140
  91.4 6.3 %all-to-all-start.3 = ((bf16[96,2,384]{2,1,0:T(2,128)(2,1)}), bf16[96,2,384]{2,1,0:T(2,128)(2,1)S(1)}, u32[]{:S(2)}, u32[]{:S(2)}) async-start(bf16[96,2,384]{2,1,0:T(2,128)(2,1)} %reshape.140), calls=%async_computation.3 | async-start | bytes 294912 | tf_op jit(solution)/shard_map/all_to_all | solution.py:349
  97.8 0.1 copy.60
  98.0 15.4 %all-to-all-done.3 = bf16[96,2,384]{2,1,0:T(2,128)(2,1)S(1)} async-done(((bf16[96,2,384]{2,1,0:T(2,128)(2,1)}), bf16[96,2,384]{2,1,0:T(2,128)(2,1)S(1)}, u32[]{:S(2)}, u32[]{:S(2)}) %all-to-all-start.3) | async-done | bytes 147488 | tf_op jit(solution)/shard_map/all_to_all | solution.py:349
  113.4 0.1 convert_reduce_fusion
  113.6 0.1 multiply_reduce_fusion.1
  113.7 0.6 fusion.6
  (41 shorter events, 1.1 us)
Async XLA Ops:
  2.6 28.8 %all-to-all-start = ((bf16[16,32,128]{2,1,0:T(8,128)(2,1)}), bf16[16,32,128]{2,1,0:T(8,128)(2,1)S(1)}, u32[]{:S(2)}, u32[]{:S(2)}) async-start(bf16[16,32,128]{2,1,0:T(8,128)(2,1)} %attend.1), calls=%async_computation | async-start | bytes 262144 | tf_op jit(solution)/shard_map/all_to_all | solution.py:318
  20.1 5.4 %copy-start.4 = (s32[4,2]{0,1:T(2,128)S(1)}, s32[4,2]{0,1:T(2,128)}, u32[]{:S(2)}) copy-start(s32[4,2]{0,1:T(2,128)} %param.19) | copy-start | bytes 100
  20.1 6.1 %copy-start.3 = (bf16[4,6144]{1,0:T(4,128)(2,1)S(1)}, bf16[4,6144]{1,0:T(4,128)(2,1)}, u32[]{:S(2)}) copy-start(bf16[4,6144]{1,0:T(4,128)(2,1)} %param.21) | copy-start | bytes 147460
  20.1 6.2 %copy-start.2 = (f32[6144]{0:T(1024)S(1)}, f32[6144]{0:T(1024)}, u32[]{:S(2)}) copy-start(f32[6144]{0:T(1024)} %param.22) | copy-start | bytes 73732
  23.3 50.3 %copy-start.1 = (bf16[2,96,3072]{2,1,0:T(8,128)(2,1)S(1)}, bf16[2,96,3072]{2,1,0:T(8,128)(2,1)}, u32[]{:S(2)}) copy-start(bf16[2,96,3072]{2,1,0:T(8,128)(2,1)} %get-tuple-element.7.own) | copy-start | bytes 3538948
  23.3 50.3 %collective-permute-start = (bf16[3,96,3072]{2,1,0:T(8,128)(2,1)}, bf16[3,96,3072]{2,1,0:T(8,128)(2,1)S(1)}, u32[]{:S(2)}, u32[]{:S(2)}) collective-permute-start(bf16[3,96,3072]{2,1,0:T(8,128)(2,1)} %get-tuple-element.8), channel_id=1, source_target_pairs={{0,1},{1,0},{2,3},{3,2},{4,5},{5,4},{6,7},{7,6},{8,9},{9,8},{10,11... | collective-permute-start | bytes 5308424 | tf_op jit(solution)/shard_map/ppermute | solution.py:317
  73.7 2.9 %copy-start = (bf16[96,6144]{1,0:T(8,128)(2,1)S(1)}, bf16[96,6144]{1,0:T(8,128)(2,1)}, u32[]{:S(2)}) copy-start(bf16[96,6144]{1,0:T(8,128)(2,1)} %down_ref.3) | copy-start | bytes 3538948
  77.1 20.6 %copy-start.5 = (f32[4,2]{0,1:T(2,128)S(1)}, f32[4,2]{0,1:T(2,128)}, u32[]{:S(2)}) copy-start(f32[4,2]{0,1:T(2,128)} %param.20) | copy-start | bytes 100
  91.4 22.1 %all-to-all-start.3 = ((bf16[96,2,384]{2,1,0:T(2,128)(2,1)}), bf16[96,2,384]{2,1,0:T(2,128)(2,1)S(1)}, u32[]{:S(2)}, u32[]{:S(2)}) async-start(bf16[96,2,384]{2,1,0:T(2,128)(2,1)} %reshape.140), calls=%async_computation.3 | async-start | bytes 294912 | tf_op jit(solution)/shard_map/all_to_all | solution.py:349

commit v7 on v6

--- a/solution.py
+++ b/solution.py
@@ -28,33 +28,43 @@
     return [pl.multiple_of((i * NC + core) * share, share) for i in range(NX * NZ)]
 
 
-def pack_kernel(gate_ref, up_ref, down_ref, own_ref, out_ref, stage, in_sems, out_sems):
-    share = gate_ref.shape[1] // (NX * NZ * NC)
-    at_c = lax.axis_index("c")
-    refs = (gate_ref, up_ref, down_ref)
-    groups = []
-    for to, core in ((out_ref, 1 - at_c), (own_ref, at_c)):
-        for kind in range(to.shape[0]):
-            slot = len(groups)
-            copies = [
-                pltpu.make_async_copy(
-                    refs[kind].at[:, pl.ds(start, share)],
-                    stage.at[slot, :, pl.ds(i * share, share)],
-                    in_sems.at[slot, i],
-                )
-                for i, start in enumerate(starts_of(core, share))
-            ]
-            groups.append(
-                (copies, pltpu.make_async_copy(stage.at[slot], to.at[kind], out_sems.at[slot]))
+def pack_copies(refs, core, to, sems):
+    share = refs[0].shape[1] // (NX * NZ * NC)
+    return [
+        [
+            pltpu.make_async_copy(
+                ref.at[:, pl.ds(start, share)],
+                to.at[kind, :, pl.ds(i * share, share)],
+                sems.at[kind, i],
             )
-    for copies, _ in groups:
-        for copy in copies:
-            copy.start()
-    for copies, leave in groups:
+            for i, start in enumerate(starts_of(core, share))
+        ]
+        for kind, ref in enumerate(refs)
+    ]
+
+
+def pack_own_kernel(gate_ref, up_ref, out_ref, sems):
+    groups = pack_copies((gate_ref, up_ref), lax.axis_index("c"), out_ref, sems)
+    for copy in sum(groups, []):
+        copy.start()
+    for copy in sum(groups, []):
+        copy.wait()
+
+
+def pack_sent_kernel(gate_ref, up_ref, down_ref, out_ref, stage, in_sems, out_sems):
+    other = 1 - lax.axis_index("c")
+    groups = pack_copies((gate_ref, up_ref, down_ref), other, stage, in_sems)
+    for copy in sum(groups, []):
+        copy.start()
+    leaves = []
+    for kind, copies in enumerate(groups):
         for copy in copies:
             copy.wait()
-        leave.start()
-    for _, leave in groups:
+        leaves.append(
+            pltpu.make_async_copy(stage.at[kind], out_ref.at[kind], out_sems.at[kind])
+        )
+        leaves[-1].start()
+    for leave in leaves:
         leave.wait()
 
 
@@ -244,23 +254,36 @@
     return jnp.sum((factor / whole)[..., None] * part, axis=0)
 
 
-def pack_weights(gate, up, down):
-    hidden, width = down.shape
+def pack_own(*weights):
+    hidden, width = weights[0].shape
+    packed = jax.ShapeDtypeStruct((len(weights), hidden, width // NC), jnp.bfloat16)
     return pl.pallas_call(
-        pack_kernel,
-        out_shape=tuple(
-            jax.ShapeDtypeStruct((kinds, hidden, width // NC), jnp.bfloat16) for kinds in (2, 3)
-        ),
-        in_specs=[ANY] * 3,
-        out_specs=(ANY, ANY),
+        pack_own_kernel,
+        out_shape=packed,
+        in_specs=[ANY] * len(weights),
+        out_specs=VMEM,
+        scratch_shapes=[pltpu.SemaphoreType.DMA((len(weights), NX * NZ))],
+        compiler_params=pltpu.CompilerParams(vmem_limit_bytes=16 * 2**20),
+        name="pack_own",
+    )(*weights)
+
+
+def pack_sent(*weights):
+    hidden, width = weights[0].shape
+    packed = jax.ShapeDtypeStruct((len(weights), hidden, width // NC), jnp.bfloat16)
+    return pl.pallas_call(
+        pack_sent_kernel,
+        out_shape=packed,
+        in_specs=[ANY] * len(weights),
+        out_specs=ANY,
         scratch_shapes=[
-            pltpu.VMEM((5, hidden, width // NC), jnp.bfloat16),
-            pltpu.SemaphoreType.DMA((5, NX * NZ)),
-            pltpu.SemaphoreType.DMA((5,)),
+            pltpu.VMEM(packed.shape, packed.dtype),
+            pltpu.SemaphoreType.DMA((len(weights), NX * NZ)),
+            pltpu.SemaphoreType.DMA((len(weights),)),
         ],
         compiler_params=pltpu.CompilerParams(vmem_limit_bytes=60 * 2**20),
-        name="pack",
-    )(gate, up, down)
+        name="pack_sent",
+    )(*weights)
 
 
 def expert_enter(state, gain, own, other):
@@ -313,7 +336,7 @@
 
     packet = local_attention(lengths, queries, key_cache, value_cache, new_key, new_value)
 
-    own, sent = pack_weights(w_gate.T, w_up.T, w_down)
+    sent = pack_sent(w_gate.T, w_up.T, w_down)
     other = lax.ppermute(sent, "c", [(0, 1), (1, 0)])
     arrived = lax.all_to_all(packet, DEV, split_axis=0, concat_axis=0, tiled=True)
     attended = merge(arrived)
@@ -337,6 +360,7 @@
         "rec,rd->ecd", row_slots.astype(bf16), scaled, preferred_element_type=f32
     ).astype(bf16)
     outgoing = jnp.repeat(packed, copies, axis=0)
+    own = pack_own(w_gate.T, w_up.T)
     incoming = lax.all_to_all(outgoing, OUTER, split_axis=0, concat_axis=0, tiled=True)
     slab = incoming.reshape(slots, NZ * share)
     over_x = lax.all_gather(slab, "x", axis=0, tiled=False)

time: 115 us -> 116 us (level)
  blocking collectives: 57.2 us -> 28.5 us
  starting transfers between devices: 26 us -> 40.7 us
  waiting for transfers between devices: 20.2 us -> 32.1 us
  local copies, waits for them, and re-layouts: 1.59 us -> 4.78 us
    all_to_all x1 -> x0, blocking collectives: 28.7 us -> none  [body(): lax.all_to_all(outgoing, OUTER, split_axis=0, concat_axis=0, tiled=True)]
    all_to_all x0 -> x1, starting transfers between devices: none -> 14.8 us  [body(): lax.all_to_all(outgoing, OUTER, split_axis=0, concat_axis=0, tiled=True)]
    all_to_all x0 -> x1, waiting for transfers between devices: none -> 11.1 us  [body(): lax.all_to_all(outgoing, OUTER, split_axis=0, concat_axis=0, tiled=True)]
    unnamed x15 -> x17, local copies, waits for them, and re-layouts: 0.14 us -> 2.67 us
    pallas_call x1 -> x2, Pallas kernels: 3.18 us -> 3 us  [the longest x1 2.64 us: pack_sent(): pl.pallas_call(pack_sent_kernel, out_shape=packed, in_specs=[ANY] * len(w...]
  transfers between devices with their start and end apart: 3 -> 4, of which waited for: 2 -> 3; matrix products, arithmetic and copies ran while one was open for 2% -> 2% of each run, Pallas kernels for 3% -> 3%
where the time goes in v7:
time: 116 us; the launch traced here: 115 us
  starting transfers between devices  40.7 us (35%)
  waiting for transfers between devices  32.1 us (28%)
  blocking collectives  28.5 us (25%)
  Pallas kernels  6.94 us (6%)
  local copies, waits for them, and re-layouts  4.78 us (4%)
  other arithmetic  1.71 us (1%)
    all_to_all x1, starting transfers between devices, body(): lax.all_to_all(packet, DEV, split_axis=0, concat_axis=0, tiled=True)  17.5 us
    all_to_all x1, waiting for transfers between devices, body(): lax.all_to_all(home, ('zh',) + OUTER, split_axis=0, concat_axis=0, tiled=...  15.4 us
    all_to_all x1, starting transfers between devices, body(): lax.all_to_all(outgoing, OUTER, split_axis=0, concat_axis=0, tiled=True)  14.8 us
    all_to_all x1, blocking collectives, body(): from_x = lax.all_to_all(cut, 'x', split_axis=0, concat_axis=0, tiled=True)  13.5 us
    all_gather x1, blocking collectives, body(): over_x = lax.all_gather(slab, 'x', axis=0, tiled=False)  12.9 us
    all_to_all x1, waiting for transfers between devices, body(): lax.all_to_all(outgoing, OUTER, split_axis=0, concat_axis=0, tiled=True)  11.1 us
    all_to_all x1, starting transfers between devices, body(): lax.all_to_all(home, ('zh',) + OUTER, split_axis=0, concat_axis=0, tiled=...  6.31 us
    all_to_all x1, waiting for transfers between devices, body(): lax.all_to_all(packet, DEV, split_axis=0, concat_axis=0, tiled=True)  5.54 us
  transfers between devices with their start and end apart: 4, of which 3 were waited for; matrix products, arithmetic and copies ran while one was open for 2% of the time, Pallas kernels for 3%

profile of v7, /device:TPU:2, one launch (start us, length us, event | category | flops | bytes accessed | tf_op | source)
XLA Modules:
  0.0 115.1 jit_solution(9449706227788153132)
XLA Ops:
  0.0 2.6 %attend.1 = bf16[16,32,128]{2,1,0:T(8,128)(2,1)} custom-call(s32[4]{0:T(128)} %length_ref.1, bf16[4,6144]{1,0:T(4,128)(2,1)} %q_ref.1, bf16[256,1024]{1,0:T(8,128)(2,1)} %bitcast.45, bf16[256,1024]{1,0:T(8,128)(2,1)} %bitcast.46, bf16[4,1024]{1,0:T(4,128)(2,1)} %nk_ref.1, bf16[4,1024]{1,0:T(4,128)(2,1)} %nv_ref.1), custom_call_target="tpu_custom_call" | custom-call | tf_op jit(solution)/shard_map/attend/pallas_call | solution.py:227
  2.6 17.5 %all-to-all-start = ((bf16[16,32,128]{2,1,0:T(8,128)(2,1)}), bf16[16,32,128]{2,1,0:T(8,128)(2,1)S(1)}, u32[]{:S(2)}, u32[]{:S(2)}) async-start(bf16[16,32,128]{2,1,0:T(8,128)(2,1)} %attend.1), calls=%async_computation | async-start | bytes 262144 | tf_op jit(solution)/shard_map/all_to_all | solution.py:341
  20.1 2.6 %pack_sent.1 = bf16[3,96,3072]{2,1,0:T(8,128)(2,1)} custom-call(bf16[96,6144]{1,0:T(8,128)(2,1)} %bitcast.38, bf16[96,6144]{1,0:T(8,128)(2,1)} %bitcast.40, bf16[96,6144]{1,0:T(8,128)(2,1)} %down_ref.3), custom_call_target="tpu_custom_call" | custom-call | tf_op jit(solution)/shard_map/pack_sent/pallas_call | solution.py:274
  22.8 2.1 %collective-permute-start = (bf16[3,96,3072]{2,1,0:T(8,128)(2,1)}, bf16[3,96,3072]{2,1,0:T(8,128)(2,1)S(1)}, u32[]{:S(2)}, u32[]{:S(2)}) collective-permute-start(bf16[3,96,3072]{2,1,0:T(8,128)(2,1)} %pack_sent.1), channel_id=1, source_target_pairs={{0,1},{1,0},{2,3},{3,2},{4,5},{5,4},{6,7},{7,6},{8,9},{9,8},{10,11... | collective-permute-start | bytes 5308424 | tf_op jit(solution)/shard_map/ppermute | solution.py:340
  25.2 0.2 select_reduce_fusion
  25.9 5.5 %all-to-all-done = bf16[16,32,128]{2,1,0:T(8,128)(2,1)S(1)} async-done(((bf16[16,32,128]{2,1,0:T(8,128)(2,1)}), bf16[16,32,128]{2,1,0:T(8,128)(2,1)S(1)}, u32[]{:S(2)}, u32[]{:S(2)}) %all-to-all-start) | async-done | bytes 131104 | tf_op jit(solution)/shard_map/all_to_all | solution.py:341
  31.5 0.1 multiply_reduce_fusion
  31.7 0.2 convolution_convert_fusion
  31.9 0.7 broadcast_in_dim.2
  32.6 14.8 %all-to-all-start.1 = ((bf16[48,2,768]{2,1,0:T(2,128)(2,1)}), bf16[48,2,768]{2,1,0:T(2,128)(2,1)S(1)}, u32[]{:S(2)}, u32[]{:S(2)}) async-start(bf16[48,2,768]{2,1,0:T(2,128)(2,1)} %bitcast.10), calls=%async_computation.1 | async-start | bytes 294912 | tf_op jit(solution)/shard_map/all_to_all | solution.py:364
  47.5 1.3 %copy-done = bf16[6144,96]{0,1:T(8,128)(2,1)S(1)} copy-done((bf16[6144,96]{0,1:T(8,128)(2,1)S(1)}, bf16[6144,96]{0,1:T(8,128)(2,1)}, u32[]{:S(2)}) %copy-start) | copy-done | bytes 1179672
  48.7 1.3 %copy-done.1 = bf16[6144,96]{0,1:T(8,128)(2,1)S(1)} copy-done((bf16[6144,96]{0,1:T(8,128)(2,1)S(1)}, bf16[6144,96]{0,1:T(8,128)(2,1)}, u32[]{:S(2)}) %copy-start.1) | copy-done | bytes 1179672
  50.0 0.4 pack_own.1.own
  50.4 11.1 %all-to-all-done.1 = bf16[48,2,768]{2,1,0:T(2,128)(2,1)S(1)} async-done(((bf16[48,2,768]{2,1,0:T(2,128)(2,1)}), bf16[48,2,768]{2,1,0:T(2,128)(2,1)S(1)}, u32[]{:S(2)}, u32[]{:S(2)}) %all-to-all-start.1) | async-done | bytes 147488 | tf_op jit(solution)/shard_map/all_to_all | solution.py:364
  61.6 12.9 %all_gather.9.state_ref = bf16[4,96,768]{2,1,0:T(8,128)(2,1)S(1)} all-gather(bf16[1,96,768]{2,1,0:T(8,128)(2,1)S(1)} %all_gather_reshape.3), channel_id=1, replica_groups=mesh['zl'=6,'y'=8,'x'=4,'zh'=2,'c'=2] {'x'}, dimensions={0}, use_global_device_ids=true | all-gather | bytes 737280 | tf_op jit(solution)/shard_map/all_gather | solution.py:366
  74.5 0.8 enter.1
  75.3 2.1 %all-gather = f32[8,96,128]{2,1,0:T(8,128)S(1)} all-gather(f32[4,96,128]{2,1,0:T(8,128)S(1)} %enter.1), channel_id=2, replica_groups=mesh['zl'=6,'y'=8,'x'=4,'zh'=2,'c'=2] {'c'}, dimensions={0}, use_global_device_ids=true | all-gather | bytes 589824 | tf_op jit(solution)/shard_map/all_gather | solution.py:368
  77.4 0.6 leave.1
  78.0 13.5 %all_to_all.20 = bf16[4,2,96,384]{3,2,1,0:T(8,128)(2,1)S(1)} all-to-all(bf16[4,2,96,384]{3,2,1,0:T(8,128)(2,1)S(1)} %leave.1), channel_id=1, replica_groups=mesh['zl'=6,'y'=8,'x'=4,'zh'=2,'c'=2] {'x'}, dimensions={0} | all-to-all | bytes 1179648 | tf_op jit(solution)/shard_map/all_to_all | solution.py:371
  91.5 0.7 reshape.140
  92.2 6.3 %all-to-all-start.3 = ((bf16[96,2,384]{2,1,0:T(2,128)(2,1)}), bf16[96,2,384]{2,1,0:T(2,128)(2,1)S(1)}, u32[]{:S(2)}, u32[]{:S(2)}) async-start(bf16[96,2,384]{2,1,0:T(2,128)(2,1)} %reshape.140), calls=%async_computation.3 | async-start | bytes 294912 | tf_op jit(solution)/shard_map/all_to_all | solution.py:373
  98.9 15.4 %all-to-all-done.3 = bf16[96,2,384]{2,1,0:T(2,128)(2,1)S(1)} async-done(((bf16[96,2,384]{2,1,0:T(2,128)(2,1)}), bf16[96,2,384]{2,1,0:T(2,128)(2,1)S(1)}, u32[]{:S(2)}, u32[]{:S(2)}) %all-to-all-start.3) | async-done | bytes 147488 | tf_op jit(solution)/shard_map/all_to_all | solution.py:373
  114.3 0.1 convert_reduce_fusion
  114.5 0.6 fusion.6
  (45 shorter events, 1.5 us)
Async XLA Ops:
  2.6 28.8 %all-to-all-start = ((bf16[16,32,128]{2,1,0:T(8,128)(2,1)}), bf16[16,32,128]{2,1,0:T(8,128)(2,1)S(1)}, u32[]{:S(2)}, u32[]{:S(2)}) async-start(bf16[16,32,128]{2,1,0:T(8,128)(2,1)} %attend.1), calls=%async_computation | async-start | bytes 262144 | tf_op jit(solution)/shard_map/all_to_all | solution.py:341
  20.1 4.8 %copy-start.4 = (bf16[4,6144]{1,0:T(4,128)(2,1)S(1)}, bf16[4,6144]{1,0:T(4,128)(2,1)}, u32[]{:S(2)}) copy-start(bf16[4,6144]{1,0:T(4,128)(2,1)} %param.21) | copy-start | bytes 147460
  20.1 4.8 %copy-start.5 = (s32[4,2]{0,1:T(2,128)S(1)}, s32[4,2]{0,1:T(2,128)}, u32[]{:S(2)}) copy-start(s32[4,2]{0,1:T(2,128)} %param.19) | copy-start | bytes 100
  20.1 5.5 %copy-start.3 = (f32[6144]{0:T(1024)S(1)}, f32[6144]{0:T(1024)}, u32[]{:S(2)}) copy-start(f32[6144]{0:T(1024)} %param.22) | copy-start | bytes 73732
  22.8 51.7 %collective-permute-start = (bf16[3,96,3072]{2,1,0:T(8,128)(2,1)}, bf16[3,96,3072]{2,1,0:T(8,128)(2,1)S(1)}, u32[]{:S(2)}, u32[]{:S(2)}) collective-permute-start(bf16[3,96,3072]{2,1,0:T(8,128)(2,1)} %pack_sent.1), channel_id=1, source_target_pairs={{0,1},{1,0},{2,3},{3,2},{4,5},{5,4},{6,7},{7,6},{8,9},{9,8},{10,11... | collective-permute-start | bytes 5308424 | tf_op jit(solution)/shard_map/ppermute | solution.py:340
  32.6 28.9 %all-to-all-start.1 = ((bf16[48,2,768]{2,1,0:T(2,128)(2,1)}), bf16[48,2,768]{2,1,0:T(2,128)(2,1)S(1)}, u32[]{:S(2)}, u32[]{:S(2)}) async-start(bf16[48,2,768]{2,1,0:T(2,128)(2,1)} %bitcast.10), calls=%async_computation.1 | async-start | bytes 294912 | tf_op jit(solution)/shard_map/all_to_all | solution.py:364
  47.5 1.3 %copy-start = (bf16[6144,96]{0,1:T(8,128)(2,1)S(1)}, bf16[6144,96]{0,1:T(8,128)(2,1)}, u32[]{:S(2)}) copy-start(bf16[6144,96]{0,1:T(8,128)(2,1)} %param.23) | copy-start | bytes 3538948
  48.7 1.3 %copy-start.1 = (bf16[6144,96]{0,1:T(8,128)(2,1)S(1)}, bf16[6144,96]{0,1:T(8,128)(2,1)}, u32[]{:S(2)}) copy-start(bf16[6144,96]{0,1:T(8,128)(2,1)} %param.24) | copy-start | bytes 3538948
  74.5 2.9 %copy-start.2 = (bf16[96,6144]{1,0:T(8,128)(2,1)S(1)}, bf16[96,6144]{1,0:T(8,128)(2,1)}, u32[]{:S(2)}) copy-start(bf16[96,6144]{1,0:T(8,128)(2,1)} %down_ref.3) | copy-start | bytes 3538948
  78.0 20.6 %copy-start.6 = (f32[4,2]{0,1:T(2,128)S(1)}, f32[4,2]{0,1:T(2,128)}, u32[]{:S(2)}) copy-start(f32[4,2]{0,1:T(2,128)} %param.20) | copy-start | bytes 100
  92.2 22.0 %all-to-all-start.3 = ((bf16[96,2,384]{2,1,0:T(2,128)(2,1)}), bf16[96,2,384]{2,1,0:T(2,128)(2,1)S(1)}, u32[]{:S(2)}, u32[]{:S(2)}) async-start(bf16[96,2,384]{2,1,0:T(2,128)(2,1)} %reshape.140), calls=%async_computation.3 | async-start | bytes 294912 | tf_op jit(solution)/shard_map/all_to_all | solution.py:373

commit v8 on v6

--- a/solution.py
+++ b/solution.py
@@ -28,7 +28,23 @@
     return [pl.multiple_of((i * NC + core) * share, share) for i in range(NX * NZ)]
 
 
-def pack_kernel(gate_ref, up_ref, down_ref, own_ref, out_ref, stage, in_sems, out_sems):
+def pack_kernel(
+    gate_ref,
+    up_ref,
+    down_ref,
+    experts_ref,
+    combine_ref,
+    own_ref,
+    out_ref,
+    place_ref,
+    mix_ref,
+    stage,
+    experts,
+    combine,
+    in_sems,
+    out_sems,
+    small_sems,
+):
     share = gate_ref.shape[1] // (NX * NZ * NC)
     at_c = lax.axis_index("c")
     refs = (gate_ref, up_ref, down_ref)
@@ -47,9 +63,34 @@
             groups.append(
                 (copies, pltpu.make_async_copy(stage.at[slot], to.at[kind], out_sems.at[slot]))
             )
+    small = [
+        pltpu.make_async_copy(experts_ref, experts, small_sems.at[0]),
+        pltpu.make_async_copy(combine_ref, combine, small_sems.at[1]),
+    ]
+    for copy in small:
+        copy.start()
     for copies, _ in groups:
         for copy in copies:
             copy.start()
+
+    for copy in small:
+        copy.wait()
+    choices = [(r, k) for r in range(place_ref.shape[0]) for k in range(TOPK)]
+    chosen = [experts[k, r] for r, k in choices]
+    row = lax.broadcasted_iota(jnp.int32, place_ref.shape, 0)
+    column = lax.broadcasted_iota(jnp.int32, place_ref.shape, 1)
+    place = jnp.zeros(place_ref.shape, jnp.float32)
+    mix = jnp.zeros(place_ref.shape, jnp.float32)
+    for i, (r, k) in enumerate(choices):
+        rank = jnp.int32(0)
+        for earlier in chosen[:i]:
+            rank += jnp.where(earlier == chosen[i], 1, 0)
+        hit = (row == r) & (column == chosen[i] * CAP + rank)
+        place = jnp.where(hit, 1.0, place)
+        mix = jnp.where(hit, combine[k, r], mix)
+    place_ref[...] = place
+    mix_ref[...] = mix
+
     for copies, leave in groups:
         for copy in copies:
             copy.wait()
@@ -244,23 +285,29 @@
     return jnp.sum((factor / whole)[..., None] * part, axis=0)
 
 
-def pack_weights(gate, up, down):
+def pack_weights(gate, up, down, experts, combine):
+    rows = experts.shape[1]
+    slots = jax.ShapeDtypeStruct((rows, EXPERTS * CAP), jnp.float32)
     hidden, width = down.shape
     return pl.pallas_call(
         pack_kernel,
         out_shape=tuple(
             jax.ShapeDtypeStruct((kinds, hidden, width // NC), jnp.bfloat16) for kinds in (2, 3)
-        ),
-        in_specs=[ANY] * 3,
-        out_specs=(ANY, ANY),
+        )
+        + (slots, slots),
+        in_specs=[ANY] * 5,
+        out_specs=(ANY, ANY, VMEM, VMEM),
         scratch_shapes=[
             pltpu.VMEM((5, hidden, width // NC), jnp.bfloat16),
+            pltpu.SMEM(experts.shape, jnp.int32),
+            pltpu.SMEM(combine.shape, jnp.float32),
             pltpu.SemaphoreType.DMA((5, NX * NZ)),
             pltpu.SemaphoreType.DMA((5,)),
+            pltpu.SemaphoreType.DMA((2,)),
         ],
         compiler_params=pltpu.CompilerParams(vmem_limit_bytes=60 * 2**20),
         name="pack",
-    )(gate, up, down)
+    )(gate, up, down, experts, combine)
 
 
 def expert_enter(state, gain, own, other):
@@ -313,7 +360,7 @@
 
     packet = local_attention(lengths, queries, key_cache, value_cache, new_key, new_value)
 
-    own, sent = pack_weights(w_gate.T, w_up.T, w_down)
+    own, sent, place, mix = pack_weights(w_gate.T, w_up.T, w_down, experts.T, combine.T)
     other = lax.ppermute(sent, "c", [(0, 1), (1, 0)])
     arrived = lax.all_to_all(packet, DEV, split_axis=0, concat_axis=0, tiled=True)
     attended = merge(arrived)
@@ -327,16 +374,12 @@
     gain = lax.dynamic_slice(gain, (at_x, 0, at_c, 0), (1, NZ, 1, share)).reshape(1, NZ, share)
     scaled = (state * gain).reshape(rows, NZ * share).astype(bf16)
 
-    chosen = experts.reshape(rows * TOPK)
-    hits = (chosen[:, None] == jnp.arange(EXPERTS, dtype=jnp.int32)[None, :]).astype(jnp.int32)
-    rank = jnp.sum((jnp.cumsum(hits, axis=0) - hits) * hits, axis=1)
-    slot = (rank[:, None] == jnp.arange(CAP, dtype=jnp.int32)[None, :]).astype(jnp.int32)
-    placement = (hits[:, :, None] * slot[:, None, :]).reshape(rows, TOPK, EXPERTS, CAP)
-    row_slots = jnp.sum(placement, axis=1)
     packed = jnp.einsum(
-        "rec,rd->ecd", row_slots.astype(bf16), scaled, preferred_element_type=f32
+        "rs,rd->sd", place.astype(bf16), scaled, preferred_element_type=f32
     ).astype(bf16)
+    packed = packed.reshape(EXPERTS, CAP, NZ * share)
     outgoing = jnp.repeat(packed, copies, axis=0)
+    outgoing, own_state = lax.optimization_barrier((outgoing, own_state))
     incoming = lax.all_to_all(outgoing, OUTER, split_axis=0, concat_axis=0, tiled=True)
     slab = incoming.reshape(slots, NZ * share)
     over_x = lax.all_gather(slab, "x", axis=0, tiled=False)
@@ -349,8 +392,7 @@
     returned = lax.all_to_all(home, ("zh",) + OUTER, split_axis=0, concat_axis=0, tiled=True)
     returned = returned.reshape(NZ, EXPERTS, copies, CAP, share).astype(f32)
     expert_output = jnp.sum(returned, axis=(0, 2)).reshape(1, EXPERTS * CAP, share)
-    mix_weights = jnp.sum(placement.astype(f32) * combine[:, :, None, None], axis=1)
-    moe = jnp.sum(mix_weights.reshape(rows, EXPERTS * CAP, 1) * expert_output, axis=1)
+    moe = jnp.sum(mix.reshape(rows, EXPERTS * CAP, 1) * expert_output, axis=1)
     return (own_state + moe).astype(bf16)
 
 

time: 115 us -> 115 us (level)
  blocking collectives: 57.2 us -> 79 us
  waiting for transfers between devices: 20.2 us -> 5.08 us
  starting transfers between devices: 26 us -> 19.7 us
  local copies, waits for them, and re-layouts: 1.59 us -> 0.39 us
    all_to_all x0 -> x1, blocking collectives: none -> 21.8 us  [body(): lax.all_to_all(home, ('zh',) + OUTER, split_axis=0, concat_axis=0, tiled=...]
    all_to_all x1 -> x0, waiting for transfers between devices: 15.4 us -> none  [body(): lax.all_to_all(home, ('zh',) + OUTER, split_axis=0, concat_axis=0, tiled=...]
    all_to_all x1 -> x0, starting transfers between devices: 6.31 us -> none  [body(): lax.all_to_all(home, ('zh',) + OUTER, split_axis=0, concat_axis=0, tiled=...]
  transfers between devices with their start and end apart: 3 -> 2, of which waited for: 2 -> 1; matrix products, arithmetic and copies ran while one was open for 2% -> 1% of each run, Pallas kernels for 3% -> 3%
where the time goes in v8:
time: 115 us; the launch traced here: 114 us
  blocking collectives  79 us (69%)
  starting transfers between devices  19.7 us (17%)
  Pallas kernels  7.72 us (7%)
  waiting for transfers between devices  5.08 us (4%)
  other arithmetic  1.19 us (1%)
    all_to_all x1, blocking collectives, body(): lax.all_to_all(outgoing, OUTER, split_axis=0, concat_axis=0, tiled=True)  28.7 us
    all_to_all x1, blocking collectives, body(): lax.all_to_all(home, ('zh',) + OUTER, split_axis=0, concat_axis=0, tiled=...  21.8 us
    all_to_all x1, starting transfers between devices, body(): lax.all_to_all(packet, DEV, split_axis=0, concat_axis=0, tiled=True)  17.5 us
    all_to_all x1, blocking collectives, body(): from_x = lax.all_to_all(cut, 'x', split_axis=0, concat_axis=0, tiled=True)  13.5 us
    all_gather x1, blocking collectives, body(): over_x = lax.all_gather(slab, 'x', axis=0, tiled=False)  12.9 us
    all_to_all x1, waiting for transfers between devices, body(): lax.all_to_all(packet, DEV, split_axis=0, concat_axis=0, tiled=True)  5.07 us
    pallas_call x1, Pallas kernels, pack_weights(): pl.pallas_call(pack_kernel, out_shape=tuple((jax.ShapeDtypeStruct((kinds,...  3.78 us
    pallas_call x1, Pallas kernels, local_attention(): pl.pallas_call(attend_kernel, out_shape=jax.ShapeDtypeStruct((NX * NZ * N...  2.59 us
  transfers between devices with their start and end apart: 2, of which 1 were waited for; matrix products, arithmetic and copies ran while one was open for 1% of the time, Pallas kernels for 3%

profile of v8, /device:TPU:2, one launch (start us, length us, event | category | flops | bytes accessed | tf_op | source)
XLA Modules:
  0.0 114.2 jit_solution(16330154044544421882)
XLA Ops:
  0.0 2.6 %attend.1 = bf16[16,32,128]{2,1,0:T(8,128)(2,1)} custom-call(s32[4]{0:T(128)} %length_ref.1, bf16[4,6144]{1,0:T(4,128)(2,1)} %q_ref.1, bf16[256,1024]{1,0:T(8,128)(2,1)} %bitcast.41, bf16[256,1024]{1,0:T(8,128)(2,1)} %bitcast.42, bf16[4,1024]{1,0:T(4,128)(2,1)} %nk_ref.1, bf16[4,1024]{1,0:T(4,128)(2,1)} %nv_ref.1), custom_call_target="tpu_custom_call" | custom-call | tf_op jit(solution)/shard_map/attend/pallas_call | solution.py:258
  2.6 17.5 %all-to-all-start = ((bf16[16,32,128]{2,1,0:T(8,128)(2,1)}), bf16[16,32,128]{2,1,0:T(8,128)(2,1)S(1)}, u32[]{:S(2)}, u32[]{:S(2)}) async-start(bf16[16,32,128]{2,1,0:T(8,128)(2,1)} %attend.1), calls=%async_computation | async-start | bytes 262144 | tf_op jit(solution)/shard_map/all_to_all | solution.py:365
  20.1 0.0 copy-start.3
  20.1 3.8 %pack.1 = (bf16[2,96,3072]{2,1,0:T(8,128)(2,1)}, bf16[3,96,3072]{2,1,0:T(8,128)(2,1)}, f32[4,16]{1,0:T(4,128)}, f32[4,16]{1,0:T(4,128)}) custom-call(bf16[96,6144]{1,0:T(8,128)(2,1)} %bitcast.37, bf16[96,6144]{1,0:T(8,128)(2,1)} %bitcast.38, bf16[96,6144]{1,0:T(8,128)(2,1)} %down_ref.3, s32[2,4]{1,0:T(2,128)} %bitcast.56, f32[2,4]{1,0:T(2,128)} %bitcast.57), custom_call_target="tpu_custom_call" | custom-call | tf_op jit(solution)/shard_map/pack/pallas_call | solution.py:292
  23.9 2.2 %collective-permute-start = (bf16[3,96,3072]{2,1,0:T(8,128)(2,1)}, bf16[3,96,3072]{2,1,0:T(8,128)(2,1)S(1)}, u32[]{:S(2)}, u32[]{:S(2)}) collective-permute-start(bf16[3,96,3072]{2,1,0:T(8,128)(2,1)} %get-tuple-element.16), channel_id=1, source_target_pairs={{0,1},{1,0},{2,3},{3,2},{4,5},{5,4},{6,7},{7,6},{8,9},{9,8},{10,11... | collective-permute-start | bytes 5308424 | tf_op jit(solution)/shard_map/ppermute | solution.py:364
  26.3 0.1 fusion.4
  26.4 5.1 %all-to-all-done = bf16[16,32,128]{2,1,0:T(8,128)(2,1)S(1)} async-done(((bf16[16,32,128]{2,1,0:T(8,128)(2,1)}), bf16[16,32,128]{2,1,0:T(8,128)(2,1)S(1)}, u32[]{:S(2)}, u32[]{:S(2)}) %all-to-all-start) | async-done | bytes 131104 | tf_op jit(solution)/shard_map/all_to_all | solution.py:365
  31.5 0.1 multiply_reduce_fusion
  31.7 0.9 convolution_convert_fusion
  32.6 0.1 broadcast_in_dim.2
  32.7 28.7 %all_to_all.20 = bf16[48,2,768]{2,1,0:T(2,128)(2,1)S(1)} all-to-all(bf16[48,2,768]{2,1,0:T(2,128)(2,1)S(1)} %bitcast.39), channel_id=1, replica_groups=mesh['zl'=6,'y'=8,'x'=4,'zh'=2,'c'=2] {'zl','y'}, dimensions={0} | all-to-all | bytes 294912 | tf_op jit(solution)/shard_map/all_to_all | solution.py:383
  61.4 0.1 all_gather_reshape.3
  61.5 12.9 %all_gather.9.state_ref = bf16[4,96,768]{2,1,0:T(8,128)(2,1)S(1)} all-gather(bf16[1,96,768]{2,1,0:T(8,128)(2,1)S(1)} %all_gather_reshape.3), channel_id=1, replica_groups=mesh['zl'=6,'y'=8,'x'=4,'zh'=2,'c'=2] {'x'}, dimensions={0}, use_global_device_ids=true | all-gather | bytes 737280 | tf_op jit(solution)/shard_map/all_gather | solution.py:385
  74.4 0.0 collective-permute-done.other
  74.4 0.8 enter.1
  75.2 2.1 %all-gather = f32[8,96,128]{2,1,0:T(8,128)S(1)} all-gather(f32[4,96,128]{2,1,0:T(8,128)S(1)} %enter.1), channel_id=2, replica_groups=mesh['zl'=6,'y'=8,'x'=4,'zh'=2,'c'=2] {'c'}, dimensions={0}, use_global_device_ids=true | all-gather | bytes 589824 | tf_op jit(solution)/shard_map/all_gather | solution.py:387
  77.3 0.6 leave.1
  77.9 13.5 %all_to_all.21 = bf16[4,2,96,384]{3,2,1,0:T(8,128)(2,1)S(1)} all-to-all(bf16[4,2,96,384]{3,2,1,0:T(8,128)(2,1)S(1)} %leave.1), channel_id=1, replica_groups=mesh['zl'=6,'y'=8,'x'=4,'zh'=2,'c'=2] {'x'}, dimensions={0} | all-to-all | bytes 1179648 | tf_op jit(solution)/shard_map/all_to_all | solution.py:390
  91.4 0.1 reduce_sum.50
  91.4 0.1 reshape.97
  91.5 21.8 %all_to_all.22 = bf16[96,2,384]{2,1,0:T(2,128)(2,1)S(1)} all-to-all(bf16[96,2,384]{2,1,0:T(2,128)(2,1)S(1)} %reshape.97), channel_id=1, replica_groups=mesh['zl'=6,'y'=8,'x'=4,'zh'=2,'c'=2] {'zh','zl','y'}, dimensions={0} | all-to-all | bytes 294912 | tf_op jit(solution)/shard_map/all_to_all | solution.py:392
  113.3 0.1 convert_reduce_fusion
  113.5 0.1 multiply_reduce_fusion.1
  113.6 0.6 add_convert_fusion
  (26 shorter events, 0.3 us)
Async XLA Ops:
  2.6 28.8 %all-to-all-start = ((bf16[16,32,128]{2,1,0:T(8,128)(2,1)}), bf16[16,32,128]{2,1,0:T(8,128)(2,1)S(1)}, u32[]{:S(2)}, u32[]{:S(2)}) async-start(bf16[16,32,128]{2,1,0:T(8,128)(2,1)} %attend.1), calls=%async_computation | async-start | bytes 262144 | tf_op jit(solution)/shard_map/all_to_all | solution.py:365
  20.1 6.0 %copy-start.2 = (f32[6144]{0:T(1024)S(1)}, f32[6144]{0:T(1024)}, u32[]{:S(2)}) copy-start(f32[6144]{0:T(1024)} %param.22) | copy-start | bytes 73732
  20.1 6.1 %copy-start.3 = (bf16[4,6144]{1,0:T(4,128)(2,1)S(1)}, bf16[4,6144]{1,0:T(4,128)(2,1)}, u32[]{:S(2)}) copy-start(bf16[4,6144]{1,0:T(4,128)(2,1)} %param.21) | copy-start | bytes 147460
  23.9 50.5 %copy-start.1 = (bf16[2,96,3072]{2,1,0:T(8,128)(2,1)S(1)}, bf16[2,96,3072]{2,1,0:T(8,128)(2,1)}, u32[]{:S(2)}) copy-start(bf16[2,96,3072]{2,1,0:T(8,128)(2,1)} %get-tuple-element.15.own) | copy-start | bytes 3538948
  23.9 50.5 %collective-permute-start = (bf16[3,96,3072]{2,1,0:T(8,128)(2,1)}, bf16[3,96,3072]{2,1,0:T(8,128)(2,1)S(1)}, u32[]{:S(2)}, u32[]{:S(2)}) collective-permute-start(bf16[3,96,3072]{2,1,0:T(8,128)(2,1)} %get-tuple-element.16), channel_id=1, source_target_pairs={{0,1},{1,0},{2,3},{3,2},{4,5},{5,4},{6,7},{7,6},{8,9},{9,8},{10,11... | collective-permute-start | bytes 5308424 | tf_op jit(solution)/shard_map/ppermute | solution.py:364
  74.4 2.9 %copy-start = (bf16[96,6144]{1,0:T(8,128)(2,1)S(1)}, bf16[96,6144]{1,0:T(8,128)(2,1)}, u32[]{:S(2)}) copy-start(bf16[96,6144]{1,0:T(8,128)(2,1)} %down_ref.3) | copy-start | bytes 3538948
  77.9 35.6 %copy-start.4 = (f32[4,16]{1,0:T(4,128)S(1)}, f32[4,16]{1,0:T(4,128)}, u32[]{:S(2)}) copy-start(f32[4,16]{1,0:T(4,128)} %get-tuple-element.13) | copy-start | bytes 772

commit v9 on v8

--- a/solution.py
+++ b/solution.py
@@ -63,15 +63,20 @@
             groups.append(
                 (copies, pltpu.make_async_copy(stage.at[slot], to.at[kind], out_sems.at[slot]))
             )
+    for copies, _ in groups:
+        for copy in copies:
+            copy.start()
     small = [
         pltpu.make_async_copy(experts_ref, experts, small_sems.at[0]),
         pltpu.make_async_copy(combine_ref, combine, small_sems.at[1]),
     ]
     for copy in small:
         copy.start()
-    for copies, _ in groups:
+
+    for copies, leave in groups:
         for copy in copies:
-            copy.start()
+            copy.wait()
+        leave.start()
 
     for copy in small:
         copy.wait()
@@ -91,10 +96,6 @@
     place_ref[...] = place
     mix_ref[...] = mix
 
-    for copies, leave in groups:
-        for copy in copies:
-            copy.wait()
-        leave.start()
     for _, leave in groups:
         leave.wait()
 
@@ -305,7 +306,7 @@
             pltpu.SemaphoreType.DMA((5,)),
             pltpu.SemaphoreType.DMA((2,)),
         ],
-        compiler_params=pltpu.CompilerParams(vmem_limit_bytes=60 * 2**20),
+        compiler_params=pltpu.CompilerParams(vmem_limit_bytes=52 * 2**20),
         name="pack",
     )(gate, up, down, experts, combine)
 

time: 115 us -> 114 us (level)
  transfers between devices with their start and end apart: 2 -> 2, of which waited for: 1 -> 1; matrix products, arithmetic and copies ran while one was open for 1% -> 1% of each run, Pallas kernels for 3% -> 2%
where the time goes in v9:
time: 114 us
  blocking collectives  79 us (69%)
  starting transfers between devices  19.6 us (17%)
  Pallas kernels  6.81 us (6%)
  waiting for transfers between devices  6.15 us (5%)
  other arithmetic  1.19 us (1%)
    all_to_all x1, blocking collectives, body(): lax.all_to_all(outgoing, OUTER, split_axis=0, concat_axis=0, tiled=True)  28.7 us
    all_to_all x1, blocking collectives, body(): lax.all_to_all(home, ('zh',) + OUTER, split_axis=0, concat_axis=0, tiled=...  21.8 us
    all_to_all x1, starting transfers between devices, body(): lax.all_to_all(packet, DEV, split_axis=0, concat_axis=0, tiled=True)  17.5 us
    all_to_all x1, blocking collectives, body(): from_x = lax.all_to_all(cut, 'x', split_axis=0, concat_axis=0, tiled=True)  13.5 us
    all_gather x1, blocking collectives, body(): over_x = lax.all_gather(slab, 'x', axis=0, tiled=False)  12.9 us
    all_to_all x1, waiting for transfers between devices, body(): lax.all_to_all(packet, DEV, split_axis=0, concat_axis=0, tiled=True)  6.15 us
    pallas_call x1, Pallas kernels, pack_weights(): pl.pallas_call(pack_kernel, out_shape=tuple((jax.ShapeDtypeStruct((kinds,...  2.82 us
    pallas_call x1, Pallas kernels, local_attention(): pl.pallas_call(attend_kernel, out_shape=jax.ShapeDtypeStruct((NX * NZ * N...  2.62 us
  transfers between devices with their start and end apart: 2, of which 1 were waited for; matrix products, arithmetic and copies ran while one was open for 1% of the time, Pallas kernels for 2%

profile of v9, /device:TPU:2, one launch (start us, length us, event | category | flops | bytes accessed | tf_op | source)
XLA Modules:
  0.0 113.5 jit_solution(10187632726177603475)
XLA Ops:
  0.0 2.6 %attend.1 = bf16[16,32,128]{2,1,0:T(8,128)(2,1)} custom-call(s32[4]{0:T(128)} %length_ref.1, bf16[4,6144]{1,0:T(4,128)(2,1)} %q_ref.1, bf16[256,1024]{1,0:T(8,128)(2,1)} %bitcast.43, bf16[256,1024]{1,0:T(8,128)(2,1)} %bitcast.44, bf16[4,1024]{1,0:T(4,128)(2,1)} %nk_ref.1, bf16[4,1024]{1,0:T(4,128)(2,1)} %nv_ref.1), custom_call_target="tpu_custom_call" | custom-call | tf_op jit(solution)/shard_map/attend/pallas_call | solution.py:259
  2.6 17.5 %all-to-all-start = ((bf16[16,32,128]{2,1,0:T(8,128)(2,1)}), bf16[16,32,128]{2,1,0:T(8,128)(2,1)S(1)}, u32[]{:S(2)}, u32[]{:S(2)}) async-start(bf16[16,32,128]{2,1,0:T(8,128)(2,1)} %attend.1), calls=%async_computation | async-start | bytes 262144 | tf_op jit(solution)/shard_map/all_to_all | solution.py:366
  20.2 0.0 copy-start.1
  20.2 0.0 copy-start.4
  20.2 2.8 %pack.1 = (bf16[2,96,3072]{2,1,0:T(8,128)(2,1)S(1)}, bf16[3,96,3072]{2,1,0:T(8,128)(2,1)}, f32[4,16]{1,0:T(4,128)S(1)}, f32[4,16]{1,0:T(4,128)S(1)}) custom-call(bf16[96,6144]{1,0:T(8,128)(2,1)} %bitcast.39, bf16[96,6144]{1,0:T(8,128)(2,1)} %bitcast.40, bf16[96,6144]{1,0:T(8,128)(2,1)} %down_ref.3, s32[2,4]{1,0:T(2,128)S(1)} %bitcast.37, f32[2,4]{1,0:T(2,128)S(1)} %bitcast.38), custom_call_target="tpu_custom_call" | custom-call | tf_op jit(solution)/shard_map/pack/pallas_call | solution.py:293
  23.0 2.1 %collective-permute-start = (bf16[3,96,3072]{2,1,0:T(8,128)(2,1)}, bf16[3,96,3072]{2,1,0:T(8,128)(2,1)S(1)}, u32[]{:S(2)}, u32[]{:S(2)}) collective-permute-start(bf16[3,96,3072]{2,1,0:T(8,128)(2,1)} %get-tuple-element.16), channel_id=1, source_target_pairs={{0,1},{1,0},{2,3},{3,2},{4,5},{5,4},{6,7},{7,6},{8,9},{9,8},{10,11... | collective-permute-start | bytes 5308424 | tf_op jit(solution)/shard_map/ppermute | solution.py:365
  25.2 0.1 fusion.4
  25.3 6.2 %all-to-all-done = bf16[16,32,128]{2,1,0:T(8,128)(2,1)S(1)} async-done(((bf16[16,32,128]{2,1,0:T(8,128)(2,1)}), bf16[16,32,128]{2,1,0:T(8,128)(2,1)S(1)}, u32[]{:S(2)}, u32[]{:S(2)}) %all-to-all-start) | async-done | bytes 131104 | tf_op jit(solution)/shard_map/all_to_all | solution.py:366
  31.6 0.1 multiply_reduce_fusion
  31.8 0.2 convolution_convert_fusion
  32.0 0.1 broadcast_in_dim.2
  32.1 28.7 %all_to_all.20 = bf16[48,2,768]{2,1,0:T(2,128)(2,1)S(1)} all-to-all(bf16[48,2,768]{2,1,0:T(2,128)(2,1)S(1)} %bitcast.41), channel_id=1, replica_groups=mesh['zl'=6,'y'=8,'x'=4,'zh'=2,'c'=2] {'zl','y'}, dimensions={0} | all-to-all | bytes 294912 | tf_op jit(solution)/shard_map/all_to_all | solution.py:384
  60.8 0.1 all_gather_reshape.3
  60.8 12.9 %all_gather.9.state_ref = bf16[4,96,768]{2,1,0:T(8,128)(2,1)S(1)} all-gather(bf16[1,96,768]{2,1,0:T(8,128)(2,1)S(1)} %all_gather_reshape.3), channel_id=1, replica_groups=mesh['zl'=6,'y'=8,'x'=4,'zh'=2,'c'=2] {'x'}, dimensions={0}, use_global_device_ids=true | all-gather | bytes 737280 | tf_op jit(solution)/shard_map/all_gather | solution.py:386
  73.8 0.8 enter.1
  74.6 2.1 %all-gather = f32[8,96,128]{2,1,0:T(8,128)S(1)} all-gather(f32[4,96,128]{2,1,0:T(8,128)S(1)} %enter.1), channel_id=2, replica_groups=mesh['zl'=6,'y'=8,'x'=4,'zh'=2,'c'=2] {'c'}, dimensions={0}, use_global_device_ids=true | all-gather | bytes 589824 | tf_op jit(solution)/shard_map/all_gather | solution.py:388
  76.7 0.6 leave.1
  77.2 13.5 %all_to_all.21 = bf16[4,2,96,384]{3,2,1,0:T(8,128)(2,1)S(1)} all-to-all(bf16[4,2,96,384]{3,2,1,0:T(8,128)(2,1)S(1)} %leave.1), channel_id=1, replica_groups=mesh['zl'=6,'y'=8,'x'=4,'zh'=2,'c'=2] {'x'}, dimensions={0} | all-to-all | bytes 1179648 | tf_op jit(solution)/shard_map/all_to_all | solution.py:391
  90.7 0.1 reduce_sum.50
  90.8 0.1 reshape.97
  90.8 21.8 %all_to_all.22 = bf16[96,2,384]{2,1,0:T(2,128)(2,1)S(1)} all-to-all(bf16[96,2,384]{2,1,0:T(2,128)(2,1)S(1)} %reshape.97), channel_id=1, replica_groups=mesh['zl'=6,'y'=8,'x'=4,'zh'=2,'c'=2] {'zh','zl','y'}, dimensions={0} | all-to-all | bytes 294912 | tf_op jit(solution)/shard_map/all_to_all | solution.py:393
  112.7 0.1 convert_reduce_fusion
  112.8 0.1 multiply_reduce_fusion.1
  112.9 0.6 add_convert_fusion
  (26 shorter events, 0.3 us)
Async XLA Ops:
  0.0 20.1 %copy-start.3 = (f32[4,2]{0,1:T(2,128)S(1)}, f32[4,2]{0,1:T(2,128)}, u32[]{:S(2)}) copy-start(f32[4,2]{0,1:T(2,128)} %param.20) | copy-start | bytes 100
  0.0 20.1 %copy-start.2 = (s32[4,2]{0,1:T(2,128)S(1)}, s32[4,2]{0,1:T(2,128)}, u32[]{:S(2)}) copy-start(s32[4,2]{0,1:T(2,128)} %param.19) | copy-start | bytes 100
  2.6 28.8 %all-to-all-start = ((bf16[16,32,128]{2,1,0:T(8,128)(2,1)}), bf16[16,32,128]{2,1,0:T(8,128)(2,1)S(1)}, u32[]{:S(2)}, u32[]{:S(2)}) async-start(bf16[16,32,128]{2,1,0:T(8,128)(2,1)} %attend.1), calls=%async_computation | async-start | bytes 262144 | tf_op jit(solution)/shard_map/all_to_all | solution.py:366
  20.2 4.9 %copy-start.1 = (f32[6144]{0:T(1024)S(1)}, f32[6144]{0:T(1024)}, u32[]{:S(2)}) copy-start(f32[6144]{0:T(1024)} %param.22) | copy-start | bytes 73732
  20.2 5.0 %copy-start.4 = (bf16[4,6144]{1,0:T(4,128)(2,1)S(1)}, bf16[4,6144]{1,0:T(4,128)(2,1)}, u32[]{:S(2)}) copy-start(bf16[4,6144]{1,0:T(4,128)(2,1)} %param.21) | copy-start | bytes 147460
  23.0 50.7 %collective-permute-start = (bf16[3,96,3072]{2,1,0:T(8,128)(2,1)}, bf16[3,96,3072]{2,1,0:T(8,128)(2,1)S(1)}, u32[]{:S(2)}, u32[]{:S(2)}) collective-permute-start(bf16[3,96,3072]{2,1,0:T(8,128)(2,1)} %get-tuple-element.16), channel_id=1, source_target_pairs={{0,1},{1,0},{2,3},{3,2},{4,5},{5,4},{6,7},{7,6},{8,9},{9,8},{10,11... | collective-permute-start | bytes 5308424 | tf_op jit(solution)/shard_map/ppermute | solution.py:365
  73.8 2.9 %copy-start = (bf16[96,6144]{1,0:T(8,128)(2,1)S(1)}, bf16[96,6144]{1,0:T(8,128)(2,1)}, u32[]{:S(2)}) copy-start(bf16[96,6144]{1,0:T(8,128)(2,1)} %down_ref.3) | copy-start | bytes 3538948

commit v10 on v9

--- a/solution.py
+++ b/solution.py
@@ -55,14 +55,15 @@
             copies = [
                 pltpu.make_async_copy(
                     refs[kind].at[:, pl.ds(start, share)],
-                    stage.at[slot, :, pl.ds(i * share, share)],
+                    (stage if to is out_ref else own_ref).at[kind, :, pl.ds(i * share, share)],
                     in_sems.at[slot, i],
                 )
                 for i, start in enumerate(starts_of(core, share))
             ]
-            groups.append(
-                (copies, pltpu.make_async_copy(stage.at[slot], to.at[kind], out_sems.at[slot]))
-            )
+            leave = None
+            if to is out_ref:
+                leave = pltpu.make_async_copy(stage.at[kind], to.at[kind], out_sems.at[kind])
+            groups.append((copies, leave))
     for copies, _ in groups:
         for copy in copies:
             copy.start()
@@ -76,7 +77,8 @@
     for copies, leave in groups:
         for copy in copies:
             copy.wait()
-        leave.start()
+        if leave is not None:
+            leave.start()
 
     for copy in small:
         copy.wait()
@@ -97,7 +99,8 @@
     mix_ref[...] = mix
 
     for _, leave in groups:
-        leave.wait()
+        if leave is not None:
+            leave.wait()
 
 
 def attend_kernel(
@@ -299,11 +302,11 @@
         in_specs=[ANY] * 5,
         out_specs=(ANY, ANY, VMEM, VMEM),
         scratch_shapes=[
-            pltpu.VMEM((5, hidden, width // NC), jnp.bfloat16),
+            pltpu.VMEM((3, hidden, width // NC), jnp.bfloat16),
             pltpu.SMEM(experts.shape, jnp.int32),
             pltpu.SMEM(combine.shape, jnp.float32),
             pltpu.SemaphoreType.DMA((5, NX * NZ)),
-            pltpu.SemaphoreType.DMA((5,)),
+            pltpu.SemaphoreType.DMA((3,)),
             pltpu.SemaphoreType.DMA((2,)),
         ],
         compiler_params=pltpu.CompilerParams(vmem_limit_bytes=52 * 2**20),

time: 114 us -> 114 us (level)
  no operation moved by 1% of the time
where the time goes in v10:
time: 114 us
  blocking collectives  79 us (69%)
  starting transfers between devices  19.6 us (17%)
  Pallas kernels  6.79 us (6%)
  waiting for transfers between devices  6.18 us (5%)
  other arithmetic  1.19 us (1%)
    all_to_all x1, blocking collectives, body(): lax.all_to_all(outgoing, OUTER, split_axis=0, concat_axis=0, tiled=True)  28.7 us
    all_to_all x1, blocking collectives, body(): lax.all_to_all(home, ('zh',) + OUTER, split_axis=0, concat_axis=0, tiled=...  21.8 us
    all_to_all x1, starting transfers between devices, body(): lax.all_to_all(packet, DEV, split_axis=0, concat_axis=0, tiled=True)  17.5 us
    all_to_all x1, blocking collectives, body(): from_x = lax.all_to_all(cut, 'x', split_axis=0, concat_axis=0, tiled=True)  13.5 us
    all_gather x1, blocking collectives, body(): over_x = lax.all_gather(slab, 'x', axis=0, tiled=False)  12.9 us
    all_to_all x1, waiting for transfers between devices, body(): lax.all_to_all(packet, DEV, split_axis=0, concat_axis=0, tiled=True)  6.17 us
    pallas_call x1, Pallas kernels, pack_weights(): pl.pallas_call(pack_kernel, out_shape=tuple((jax.ShapeDtypeStruct((kinds,...  2.8 us
    pallas_call x1, Pallas kernels, local_attention(): pl.pallas_call(attend_kernel, out_shape=jax.ShapeDtypeStruct((NX * NZ * N...  2.62 us
  transfers between devices with their start and end apart: 2, of which 1 were waited for; matrix products, arithmetic and copies ran while one was open for 1% of the time, Pallas kernels for 2%

profile of v10, /device:TPU:2, one launch (start us, length us, event | category | flops | bytes accessed | tf_op | source)
XLA Modules:
  0.0 113.5 jit_solution(16814910619152148623)
XLA Ops:
  0.0 2.6 %attend.1 = bf16[16,32,128]{2,1,0:T(8,128)(2,1)} custom-call(s32[4]{0:T(128)} %length_ref.1, bf16[4,6144]{1,0:T(4,128)(2,1)} %q_ref.1, bf16[256,1024]{1,0:T(8,128)(2,1)} %bitcast.43, bf16[256,1024]{1,0:T(8,128)(2,1)} %bitcast.44, bf16[4,1024]{1,0:T(4,128)(2,1)} %nk_ref.1, bf16[4,1024]{1,0:T(4,128)(2,1)} %nv_ref.1), custom_call_target="tpu_custom_call" | custom-call | tf_op jit(solution)/shard_map/attend/pallas_call | solution.py:262
  2.6 17.5 %all-to-all-start = ((bf16[16,32,128]{2,1,0:T(8,128)(2,1)}), bf16[16,32,128]{2,1,0:T(8,128)(2,1)S(1)}, u32[]{:S(2)}, u32[]{:S(2)}) async-start(bf16[16,32,128]{2,1,0:T(8,128)(2,1)} %attend.1), calls=%async_computation | async-start | bytes 262144 | tf_op jit(solution)/shard_map/all_to_all | solution.py:369
  20.2 0.0 copy-start.1
  20.2 0.0 copy-start.4
  20.2 2.8 %pack.1 = (bf16[2,96,3072]{2,1,0:T(8,128)(2,1)S(1)}, bf16[3,96,3072]{2,1,0:T(8,128)(2,1)}, f32[4,16]{1,0:T(4,128)S(1)}, f32[4,16]{1,0:T(4,128)S(1)}) custom-call(bf16[96,6144]{1,0:T(8,128)(2,1)} %bitcast.39, bf16[96,6144]{1,0:T(8,128)(2,1)} %bitcast.40, bf16[96,6144]{1,0:T(8,128)(2,1)} %down_ref.3, s32[2,4]{1,0:T(2,128)S(1)} %bitcast.37, f32[2,4]{1,0:T(2,128)S(1)} %bitcast.38), custom_call_target="tpu_custom_call" | custom-call | tf_op jit(solution)/shard_map/pack/pallas_call | solution.py:296
  23.0 2.1 %collective-permute-start = (bf16[3,96,3072]{2,1,0:T(8,128)(2,1)}, bf16[3,96,3072]{2,1,0:T(8,128)(2,1)S(1)}, u32[]{:S(2)}, u32[]{:S(2)}) collective-permute-start(bf16[3,96,3072]{2,1,0:T(8,128)(2,1)} %get-tuple-element.16), channel_id=1, source_target_pairs={{0,1},{1,0},{2,3},{3,2},{4,5},{5,4},{6,7},{7,6},{8,9},{9,8},{10,11... | collective-permute-start | bytes 5308424 | tf_op jit(solution)/shard_map/ppermute | solution.py:368
  25.2 0.1 fusion.4
  25.3 6.2 %all-to-all-done = bf16[16,32,128]{2,1,0:T(8,128)(2,1)S(1)} async-done(((bf16[16,32,128]{2,1,0:T(8,128)(2,1)}), bf16[16,32,128]{2,1,0:T(8,128)(2,1)S(1)}, u32[]{:S(2)}, u32[]{:S(2)}) %all-to-all-start) | async-done | bytes 131104 | tf_op jit(solution)/shard_map/all_to_all | solution.py:369
  31.6 0.1 multiply_reduce_fusion
  31.8 0.2 convolution_convert_fusion
  32.0 0.1 broadcast_in_dim.2
  32.1 28.7 %all_to_all.20 = bf16[48,2,768]{2,1,0:T(2,128)(2,1)S(1)} all-to-all(bf16[48,2,768]{2,1,0:T(2,128)(2,1)S(1)} %bitcast.41), channel_id=1, replica_groups=mesh['zl'=6,'y'=8,'x'=4,'zh'=2,'c'=2] {'zl','y'}, dimensions={0} | all-to-all | bytes 294912 | tf_op jit(solution)/shard_map/all_to_all | solution.py:387
  60.8 0.1 all_gather_reshape.3
  60.8 12.9 %all_gather.9.state_ref = bf16[4,96,768]{2,1,0:T(8,128)(2,1)S(1)} all-gather(bf16[1,96,768]{2,1,0:T(8,128)(2,1)S(1)} %all_gather_reshape.3), channel_id=1, replica_groups=mesh['zl'=6,'y'=8,'x'=4,'zh'=2,'c'=2] {'x'}, dimensions={0}, use_global_device_ids=true | all-gather | bytes 737280 | tf_op jit(solution)/shard_map/all_gather | solution.py:389
  73.8 0.8 enter.1
  74.6 2.1 %all-gather = f32[8,96,128]{2,1,0:T(8,128)S(1)} all-gather(f32[4,96,128]{2,1,0:T(8,128)S(1)} %enter.1), channel_id=2, replica_groups=mesh['zl'=6,'y'=8,'x'=4,'zh'=2,'c'=2] {'c'}, dimensions={0}, use_global_device_ids=true | all-gather | bytes 589824 | tf_op jit(solution)/shard_map/all_gather | solution.py:391
  76.7 0.6 leave.1
  77.2 13.5 %all_to_all.21 = bf16[4,2,96,384]{3,2,1,0:T(8,128)(2,1)S(1)} all-to-all(bf16[4,2,96,384]{3,2,1,0:T(8,128)(2,1)S(1)} %leave.1), channel_id=1, replica_groups=mesh['zl'=6,'y'=8,'x'=4,'zh'=2,'c'=2] {'x'}, dimensions={0} | all-to-all | bytes 1179648 | tf_op jit(solution)/shard_map/all_to_all | solution.py:394
  90.7 0.1 reduce_sum.50
  90.8 0.1 reshape.97
  90.8 21.8 %all_to_all.22 = bf16[96,2,384]{2,1,0:T(2,128)(2,1)S(1)} all-to-all(bf16[96,2,384]{2,1,0:T(2,128)(2,1)S(1)} %reshape.97), channel_id=1, replica_groups=mesh['zl'=6,'y'=8,'x'=4,'zh'=2,'c'=2] {'zh','zl','y'}, dimensions={0} | all-to-all | bytes 294912 | tf_op jit(solution)/shard_map/all_to_all | solution.py:396
  112.7 0.1 convert_reduce_fusion
  112.8 0.1 multiply_reduce_fusion.1
  112.9 0.6 add_convert_fusion
  (26 shorter events, 0.3 us)
Async XLA Ops:
  0.0 20.1 %copy-start.3 = (f32[4,2]{0,1:T(2,128)S(1)}, f32[4,2]{0,1:T(2,128)}, u32[]{:S(2)}) copy-start(f32[4,2]{0,1:T(2,128)} %param.20) | copy-start | bytes 100
  0.0 20.1 %copy-start.2 = (s32[4,2]{0,1:T(2,128)S(1)}, s32[4,2]{0,1:T(2,128)}, u32[]{:S(2)}) copy-start(s32[4,2]{0,1:T(2,128)} %param.19) | copy-start | bytes 100
  2.6 28.8 %all-to-all-start = ((bf16[16,32,128]{2,1,0:T(8,128)(2,1)}), bf16[16,32,128]{2,1,0:T(8,128)(2,1)S(1)}, u32[]{:S(2)}, u32[]{:S(2)}) async-start(bf16[16,32,128]{2,1,0:T(8,128)(2,1)} %attend.1), calls=%async_computation | async-start | bytes 262144 | tf_op jit(solution)/shard_map/all_to_all | solution.py:369
  20.2 4.9 %copy-start.1 = (f32[6144]{0:T(1024)S(1)}, f32[6144]{0:T(1024)}, u32[]{:S(2)}) copy-start(f32[6144]{0:T(1024)} %param.22) | copy-start | bytes 73732
  20.2 5.0 %copy-start.4 = (bf16[4,6144]{1,0:T(4,128)(2,1)S(1)}, bf16[4,6144]{1,0:T(4,128)(2,1)}, u32[]{:S(2)}) copy-start(bf16[4,6144]{1,0:T(4,128)(2,1)} %param.21) | copy-start | bytes 147460
  23.0 50.8 %collective-permute-start = (bf16[3,96,3072]{2,1,0:T(8,128)(2,1)}, bf16[3,96,3072]{2,1,0:T(8,128)(2,1)S(1)}, u32[]{:S(2)}, u32[]{:S(2)}) collective-permute-start(bf16[3,96,3072]{2,1,0:T(8,128)(2,1)} %get-tuple-element.16), channel_id=1, source_target_pairs={{0,1},{1,0},{2,3},{3,2},{4,5},{5,4},{6,7},{7,6},{8,9},{9,8},{10,11... | collective-permute-start | bytes 5308424 | tf_op jit(solution)/shard_map/ppermute | solution.py:368
  73.8 2.9 %copy-start = (bf16[96,6144]{1,0:T(8,128)(2,1)S(1)}, bf16[96,6144]{1,0:T(8,128)(2,1)}, u32[]{:S(2)}) copy-start(bf16[96,6144]{1,0:T(8,128)(2,1)} %down_ref.3) | copy-start | bytes 3538948
